TPU v7x, 768 devices: a whole 4x8x12 slice. The times are simulated.
768 devices in a mesh: rows: 32 (over y, z_hi, core), cols: 24 (over x, z_lo).
Axes of the slice: x: 4, y: 8, z: 12 (z_hi: 2, z_lo: 6; z = z_hi * 6 + z_lo), core: 2. Of those that a mesh axis runs over, the one named last changes fastest.
Arguments:
- tokens: bfloat16 [256, 384, 512], P('rows', 'cols'), may hold values from -6 to 6
- cotangent: bfloat16 [256, 384, 512], P('rows', 'cols'), may hold values from -6 to 6
- region: int32 [256, 384], P('rows', 'cols'), may hold values from 0 to 1
- norm_gain: float32 [512], replicated, may hold values from 0.5 to 1.5
- qkv_weight: bfloat16 [512, 1536], replicated, may hold values from -0.25 to 0.25
- out_weight: bfloat16 [512, 512], replicated, may hold values from -0.25 to 0.25
- bias_table: float32 [225, 16], replicated, may hold values from -2 to 203
- bias_bucket: int32 [64, 64], replicated, may hold values from 0 to 224
Outputs:
- grad_tokens: bfloat16 [256, 384, 512], P('rows', 'cols')
- grad_qkv: float32 [512, 1536], P('rows', 'cols')
- grad_out_weight: float32 [512, 512], P('rows')
- grad_gain: float32 [512], replicated
- grad_bias_table: float32 [225, 16], replicated
All inputs are finite; a program needn't handle non-finite values.
Results may differ from a plain program's by a relative error of at most 0.033.
Values may be sent and summed in bfloat16 or wider, within the bound.
No kernel may reach another device: no remote copies, remote signals or barrier semaphores. Data moves between devices by JAX's collectives and lax.ppermute only.
A program may use at most 64 MiB of HBM per device.

v0:
```python
import jax
import jax.numpy as jnp
from jax import lax
from jax.sharding import PartitionSpec as P

HEADS = 16
WIN = 8
SHIFT = 4
NBIAS = 225


EPSILON = 1e-05


def shifted(value, axis, by):
    size = lax.axis_size(axis)
    return lax.ppermute(value, axis, [(i, (i + by) % size) for i in range(size)])


def for_sending(value):

    def short(part):
        return part.astype(jnp.bfloat16) if part.dtype == jnp.float32 else part

    return jax.tree.map(short, value)


def layer_stats(values):
    floats = values.astype(jnp.float32)
    average = jnp.mean(floats, axis=-1, keepdims=True)
    centred = floats - average
    variance = jnp.mean(centred * centred, axis=-1, keepdims=True)
    inv_std = lax.rsqrt(variance + EPSILON)
    return (centred * inv_std, inv_std)


def to_windows(array):
    frame_rows = array.shape[0]
    frame_cols = array.shape[1]
    trailing = array.shape[2:]
    blocked = array.reshape((frame_rows // WIN, WIN, frame_cols // WIN, WIN) + trailing)
    order = (0, 2, 1, 3) + tuple(range(4, 4 + len(trailing)))
    return blocked.transpose(order).reshape(
        (frame_rows // WIN * (frame_cols // WIN), WIN * WIN) + trailing
    )


def from_windows(array, frame_rows, frame_cols):
    trailing = array.shape[2:]
    blocked = array.reshape((frame_rows // WIN, frame_cols // WIN, WIN, WIN) + trailing)
    order = (0, 2, 1, 3) + tuple(range(4, 4 + len(trailing)))
    return blocked.transpose(order).reshape((frame_rows, frame_cols) + trailing)


def window_core(normed, grad_out, labels, flags, qkv_weight, out_weight, bias):
    count = normed.shape[0]
    width = normed.shape[2]
    head_dim = width // HEADS
    scale = head_dim ** (-0.5)
    area = WIN * WIN
    packed = jnp.dot(
        normed.reshape(-1, width), qkv_weight, preferred_element_type=jnp.float32
    ).astype(jnp.bfloat16)
    packed = packed.reshape(count, area, 3, HEADS, head_dim).transpose(2, 0, 3, 1, 4)
    query_heads = packed[0]
    key_heads = packed[1]
    value_heads = packed[2]
    allowed = (labels[:, :, None] == labels[:, None, :]) & (flags[:, :, None] == flags[:, None, :])
    scores = (
        jnp.einsum("whqd,whkd->whqk", query_heads, key_heads, preferred_element_type=jnp.float32)
        * scale
        + bias[None]
    )
    scores = jnp.where(allowed[:, None], scores, -1e30)
    raised = jnp.exp(scores - jnp.max(scores, axis=-1, keepdims=True))
    probs = raised / jnp.sum(raised, axis=-1, keepdims=True)
    probs_low = probs.astype(jnp.bfloat16)
    attended = jnp.einsum(
        "whqk,whkd->whqd", probs_low, value_heads, preferred_element_type=jnp.float32
    ).astype(jnp.bfloat16)
    attended_flat = attended.transpose(0, 2, 1, 3).reshape(count, area, width)
    grad_attended = jnp.dot(
        grad_out.reshape(-1, width), out_weight.T, preferred_element_type=jnp.float32
    ).astype(jnp.bfloat16)
    grad_attended = grad_attended.reshape(count, area, HEADS, head_dim).transpose(0, 2, 1, 3)
    grad_probs = jnp.einsum(
        "whqd,whkd->whqk", grad_attended, value_heads, preferred_element_type=jnp.float32
    )
    grad_values = jnp.einsum(
        "whqk,whqd->whkd", probs_low, grad_attended, preferred_element_type=jnp.float32
    ).astype(jnp.bfloat16)
    grad_scores = probs * (grad_probs - jnp.sum(probs * grad_probs, axis=-1, keepdims=True))
    grad_scaled = (grad_scores * scale).astype(jnp.bfloat16)
    grad_queries = jnp.einsum(
        "whqk,whkd->whqd", grad_scaled, key_heads, preferred_element_type=jnp.float32
    ).astype(jnp.bfloat16)
    grad_keys = jnp.einsum(
        "whqk,whqd->whkd", grad_scaled, query_heads, preferred_element_type=jnp.float32
    ).astype(jnp.bfloat16)
    grad_packed = (
        jnp.stack([grad_queries, grad_keys, grad_values], axis=0)
        .transpose(1, 3, 0, 2, 4)
        .reshape(count, area, 3 * width)
    )
    grad_normed = jnp.dot(
        grad_packed.reshape(-1, 3 * width), qkv_weight.T, preferred_element_type=jnp.float32
    ).reshape(count, area, width)
    return (grad_normed, attended_flat, grad_packed, grad_scores)


def frame_grads(
    frame_tokens,
    frame_cot,
    frame_labels,
    first_row,
    total_rows,
    norm_gain,
    qkv_weight,
    out_weight,
    bias,
):
    frame_rows = frame_tokens.shape[0]
    frame_cols = frame_tokens.shape[1]
    frame_hat = layer_stats(frame_tokens)[0]
    normed = (frame_hat * norm_gain).astype(jnp.bfloat16)
    row_ids = first_row + jnp.arange(frame_rows, dtype=jnp.int32)
    flag_rows = (jnp.mod(row_ids, total_rows) < SHIFT).astype(jnp.int32)
    flags = jnp.broadcast_to(flag_rows[:, None], (frame_rows, frame_cols))
    grad_win, attended_win, packed_win, score_grads = window_core(
        to_windows(normed),
        to_windows(frame_cot),
        to_windows(frame_labels),
        to_windows(flags),
        qkv_weight,
        out_weight,
        bias,
    )
    grad_normed = from_windows(grad_win, frame_rows, frame_cols)
    attended = from_windows(attended_win, frame_rows, frame_cols)
    grad_packed = from_windows(packed_win, frame_rows, frame_cols)
    pair_grads = score_grads.reshape(
        frame_rows // WIN, frame_cols // WIN, HEADS, WIN * WIN, WIN * WIN
    ).sum(axis=(0, 1))

    def keep_owned(array):
        return array.reshape(-1, array.shape[-1])

    return (
        grad_normed,
        keep_owned(normed),
        keep_owned(attended),
        keep_owned(grad_packed),
        keep_owned(frame_cot),
        pair_grads,
    )


def local(tokens, cotangent, region, norm_gain, qkv_weight, out_weight, bias_table, bias_bucket):
    tile_rows = tokens.shape[0]
    tile_cols = tokens.shape[1]
    width = tokens.shape[2]
    total_rows = tile_rows * lax.axis_size("rows")
    row_anchor = lax.axis_index("rows") * tile_rows
    labels = region.astype(jnp.bfloat16)
    one_hot = (
        bias_bucket.reshape(-1)[:, None] == jnp.arange(NBIAS, dtype=jnp.int32)[None, :]
    ).astype(jnp.float32)
    bias = jnp.dot(one_hot, bias_table, precision=lax.Precision.HIGHEST).T.reshape(
        HEADS, WIN * WIN, WIN * WIN
    )
    below_tokens, below_cot, below_labels = shifted(
        (tokens[:SHIFT], cotangent[:SHIFT], labels[:SHIFT]), "rows", -1
    )
    ext_tokens = jnp.concatenate([tokens[SHIFT:], below_tokens], axis=0)
    ext_cot = jnp.concatenate([cotangent[SHIFT:], below_cot], axis=0)
    ext_labels = jnp.concatenate([labels[SHIFT:], below_labels], axis=0)
    right_tokens, right_cot, right_labels = shifted(
        (ext_tokens[:, :SHIFT], ext_cot[:, :SHIFT], ext_labels[:, :SHIFT]), "cols", -1
    )
    frame_tokens = jnp.concatenate([ext_tokens[:, SHIFT:], right_tokens], axis=1)
    frame_cot = jnp.concatenate([ext_cot[:, SHIFT:], right_cot], axis=1)
    frame_labels = jnp.concatenate([ext_labels[:, SHIFT:], right_labels], axis=1)
    frame_grad, owned_normed, owned_attended, owned_packed, owned_cot, pair_grads = frame_grads(
        frame_tokens,
        frame_cot,
        frame_labels,
        row_anchor + SHIFT,
        total_rows,
        norm_gain,
        qkv_weight,
        out_weight,
        bias,
    )
    from_left = shifted(frame_grad[:, tile_cols - SHIFT :].astype(jnp.bfloat16), "cols", 1).astype(
        jnp.float32
    )
    ext_grad = jnp.concatenate([from_left, frame_grad[:, : tile_cols - SHIFT]], axis=1)
    from_above = shifted(for_sending(ext_grad[tile_rows - SHIFT :]), "rows", 1)
    grad_normed = jnp.concatenate([from_above, ext_grad[: tile_rows - SHIFT]], axis=0)
    token_hat, inv_std = layer_stats(tokens)
    grad_hat = grad_normed * norm_gain
    grad_tokens = cotangent.astype(jnp.float32) + inv_std * (
        grad_hat
        - jnp.mean(grad_hat, axis=-1, keepdims=True)
        - token_hat * jnp.mean(grad_hat * token_hat, axis=-1, keepdims=True)
    )
    gain_local = jnp.sum(grad_normed * token_hat, axis=(0, 1))
    table_local = jnp.dot(
        one_hot.T, pair_grads.reshape(HEADS, -1).T, precision=lax.Precision.HIGHEST
    )
    grad_gain, grad_bias_table = lax.psum((gain_local, table_local), ("rows", "cols"))
    contract = (((0,), (0,)), ((), ()))
    qkv_part = lax.dot_general(
        owned_normed, owned_packed, contract, preferred_element_type=jnp.float32
    )
    out_part = lax.dot_general(
        owned_attended, owned_cot, contract, preferred_element_type=jnp.float32
    )
    row_slices = lax.psum_scatter(
        jnp.concatenate([qkv_part, out_part], axis=1).astype(jnp.bfloat16),
        "rows",
        scatter_dimension=0,
        tiled=True,
    ).astype(jnp.float32)
    grad_qkv = lax.psum_scatter(
        row_slices[:, : 3 * width].astype(jnp.bfloat16), "cols", scatter_dimension=1, tiled=True
    ).astype(jnp.float32)
    grad_out_weight = lax.psum(row_slices[:, 3 * width :].astype(jnp.bfloat16), "cols").astype(
        jnp.float32
    )
    return (grad_tokens.astype(jnp.bfloat16), grad_qkv, grad_out_weight, grad_gain, grad_bias_table)


def solution(mesh):
    return jax.shard_map(
        local,
        mesh=mesh,
        in_specs=(
            P("rows", "cols", None),
            P("rows", "cols", None),
            P("rows", "cols"),
            P(),
            P(),
            P(),
            P(),
            P(),
        ),
        out_specs=(P("rows", "cols", None), P("rows", "cols"), P("rows", None), P(), P()),
        check_vma=False,
    )
```

profile of v0, /device:TPU:32, one launch (start us, length us, event | category | flops | bytes accessed | tf_op | source)
XLA Modules:
  0.0 537.4 jit_solution(5155433209050356611)
XLA Ops:
  7.2 0.8 convert_element_type.113
  8.0 14.5 %collective-permute-start = (bf16[4,16]{1,0:T(4,128)(2,1)S(1)}, bf16[4,16]{1,0:T(4,128)(2,1)S(1)}, u32[]{:S(2)}, u32[]{:S(2)}) collective-permute-start(bf16[4,16]{1,0:T(4,128)(2,1)S(1)} %get-tuple-element.17), channel_id=1, source_target_pairs={{0,744},{24,0},{48,24},{72,48},{96,72},{120,96},{144,120},{168,144... | collective-permute-start | bytes 392 | tf_op jit(solution)/shard_map/ppermute | solution.py:17
  22.5 0.9 fusion.56
  23.4 2.6 collective-permute-start.4
  26.0 0.9 fusion.55
  26.9 1.9 collective-permute-start.2
  28.8 1.0 convert_reduce_fusion.1
  30.0 1.1 fusion.37
  31.1 0.8 eq.60
  31.9 2.8 convolution_bitcast_fusion
  34.9 1.0 copy.86
  36.0 9.5 %collective-permute-start.1 = (bf16[8,4]{1,0:T(8,128)(2,1)S(1)}, bf16[8,4]{1,0:T(8,128)(2,1)S(1)}, u32[]{:S(2)}, u32[]{:S(2)}) collective-permute-start(bf16[8,4]{1,0:T(8,128)(2,1)S(1)} %bitcast.120), channel_id=1, source_target_pairs={{0,23},{1,0},{2,1},{3,2},{4,3},{5,4},{6,5},{7,6},{8,7},{9,8},{10,9... | collective-permute-start | bytes 200 | tf_op jit(solution)/shard_map/ppermute | solution.py:17
  45.5 1.2 collective-permute-done.1
  47.7 11.1 %collective-permute-start.5 = (bf16[8,4,512]{2,1,0:T(4,128)(2,1)S(1)}, bf16[8,4,512]{2,1,0:T(4,128)(2,1)S(1)}, u32[]{:S(2)}, u32[]{:S(2)}) collective-permute-start(bf16[8,4,512]{2,1,0:T(4,128)(2,1)S(1)} %pad_maximum_fusion.4), channel_id=1, source_target_pairs={{0,23},{1,0},{2,1},{3,2},{4,3},{5,4},{6,5},{7,6},{8,7},{9,8},{10,9... | collective-permute-start | bytes 98312 | tf_op jit(solution)/shard_map/ppermute | solution.py:17
  58.8 1.9 collective-permute-start.3
  62.7 1.9 collective-permute-done.3
  66.4 1.3 fusion.45
  68.1 1.9 fusion.58
  70.0 2.1 fusion.14
  72.1 1.8 fusion.16
  73.9 3.4 fusion.59
  78.2 1.1 maximum_bitcast_fusion
  79.3 2.3 copy.94
  81.6 2.3 reshape.220
  83.8 1.6 fusion.17
  86.2 2.1 collective-permute-start.6
  89.0 2.1 copy.99
  91.2 1.5 reshape_reshape.24
  92.7 6.3 %collective-permute-done.6 = bf16[8,4,512]{2,1,0:T(4,128)(2,1)S(1)} collective-permute-done((bf16[8,4,512]{2,1,0:T(4,128)(2,1)S(1)}, bf16[8,4,512]{2,1,0:T(4,128)(2,1)S(1)}, u32[]{:S(2)}, u32[]{:S(2)}) %collective-permute-start.6) | collective-permute-done | bytes 32800 | tf_op jit(solution)/shard_map/ppermute | solution.py:17
  99.0 1.5 fusion.49
  100.5 2.1 collective-permute-start.7
  102.6 2.0 convolution_convert_fusion.2
  104.6 2.3 reshape_reshape.22
  106.9 1.1 copy.97
  108.0 6.8 %collective-permute-done.7 = bf16[4,16,512]{2,1,0:T(8,128)(2,1)} collective-permute-done((bf16[4,16,512]{2,1,0:T(8,128)(2,1)}, bf16[4,16,512]{2,1,0:T(8,128)(2,1)}, u32[]{:S(2)}, u32[]{:S(2)}) %collective-permute-start.7) | collective-permute-done | bytes 65568 | tf_op jit(solution)/shard_map/ppermute | solution.py:17
  114.8 0.8 convert_element_type.127
  115.7 1.2 fusion.36
  117.5 1.6 pad_maximum_fusion
  119.2 0.9 copy-done.9
  120.5 1.4 fusion.2
  122.0 145.8 %reduce-scatter.5.cloned.1.call-done = bf16[16,2048]{1,0:T(8,128)(2,1)} async-done(((bf16[512,2048]{1,0:T(8,128)(2,1)}), bf16[16,2048]{1,0:T(8,128)(2,1)}) %reduce-scatter.5.cloned.1.call-update) | async-done | bytes 65552 | tf_op jit(solution)/shard_map/reduce_scatter | solution.py:219
  267.7 0.8 slice.99
  268.5 0.9 copy.109
  269.5 0.8 fusion.35
  270.3 107.1 %all-reduce = (f32[512]{0:T(512)}, f32[225,16]{0,1:T(8,128)}) all-reduce(f32[512]{0:T(512)S(1)} %get-tuple-element.5, f32[225,16]{0,1:T(8,128)S(1)} %fusion.2), channel_id=1, replica_groups=mesh['rows'=32,'cols'=24] {'rows','cols'}, use_global_device_ids=true, to_apply=%region_13.14 | all-reduce | flops 4112 | bytes 32896 | tf_op jit(solution)/shard_map/psum | solution.py:211
  377.4 0.7 slice.100
  378.1 150.5 %psum.21 = bf16[16,512]{1,0:T(8,128)(2,1)S(1)} all-reduce(bf16[16,512]{1,0:T(8,128)(2,1)S(1)} %slice.100), channel_id=1, replica_groups=mesh['rows'=32,'cols'=24] {'cols'}, use_global_device_ids=true, to_apply=%region_11.12 | all-reduce | flops 8192 | bytes 32768 | tf_op jit(solution)/shard_map/psum | solution.py:228
  529.2 0.8 copy.110
  (99 shorter events, 10.1 us)
Async XLA Ops:
  7.2 58.1 %copy-start = (bf16[512,1536]{1,0:T(8,128)(2,1)S(1)}, bf16[512,1536]{1,0:T(8,128)(2,1)}, u32[]{:S(2)}) copy-start(bf16[512,1536]{1,0:T(8,128)(2,1)} %param.12) | copy-start | bytes 4718596
  7.2 260.6 %reduce-scatter.5.cloned.1.call-start = ((), (), s32[]{:S(2)}) async-start(), calls=%async_computation.2 | async-start | bytes 2162688 | tf_op jit(solution)/shard_map/reduce_scatter | solution.py:219
  8.0 27.9 %collective-permute-start = (bf16[4,16]{1,0:T(4,128)(2,1)S(1)}, bf16[4,16]{1,0:T(4,128)(2,1)S(1)}, u32[]{:S(2)}, u32[]{:S(2)}) collective-permute-start(bf16[4,16]{1,0:T(4,128)(2,1)S(1)} %get-tuple-element.17), channel_id=1, source_target_pairs={{0,744},{24,0},{48,24},{72,48},{96,72},{120,96},{144,120},{168,144... | collective-permute-start | bytes 392 | tf_op jit(solution)/shard_map/ppermute | solution.py:17
  23.4 24.3 %collective-permute-start.4 = (bf16[4,16,512]{2,1,0:T(8,128)(2,1)S(1)}, bf16[4,16,512]{2,1,0:T(8,128)(2,1)S(1)}, u32[]{:S(2)}, u32[]{:S(2)}) collective-permute-start(bf16[4,16,512]{2,1,0:T(8,128)(2,1)S(1)} %get-tuple-element.14), channel_id=1, source_target_pairs={{0,744},{24,0},{48,24},{72,48},{96,72},{120,96},{144,120},{168,144... | collective-permute-start | bytes 196616 | tf_op jit(solution)/shard_map/ppermute | solution.py:17
  26.9 31.9 %collective-permute-start.2 = (bf16[4,16,512]{2,1,0:T(8,128)(2,1)S(1)}, bf16[4,16,512]{2,1,0:T(8,128)(2,1)S(1)}, u32[]{:S(2)}, u32[]{:S(2)}) collective-permute-start(bf16[4,16,512]{2,1,0:T(8,128)(2,1)S(1)} %get-tuple-element.12), channel_id=1, source_target_pairs={{0,744},{24,0},{48,24},{72,48},{96,72},{120,96},{144,120},{168,144... | collective-permute-start | bytes 196616 | tf_op jit(solution)/shard_map/ppermute | solution.py:17
  31.9 30.2 %copy-start.19 = (s32[4096]{0:T(1024)}, s32[4096]{0:T(1024)S(1)}, u32[]{:S(2)}) copy-start(s32[4096]{0:T(1024)S(1)} %eq.60) | copy-start | bytes 49156
  31.9 30.2 %copy-start.8 = (bf16[512,512]{1,0:T(8,128)(2,1)S(1)}, bf16[512,512]{1,0:T(8,128)(2,1)}, u32[]{:S(2)}) copy-start(bf16[512,512]{1,0:T(8,128)(2,1)} %param.13) | copy-start | bytes 1572868
  34.9 30.2 %copy-start.17 = (f32[512]{0:T(512)S(1)}, f32[512]{0:T(512)}, u32[]{:S(2)}) copy-start(f32[512]{0:T(512)} %param.11) | copy-start | bytes 6148
  36.0 10.7 %collective-permute-start.1 = (bf16[8,4]{1,0:T(8,128)(2,1)S(1)}, bf16[8,4]{1,0:T(8,128)(2,1)S(1)}, u32[]{:S(2)}, u32[]{:S(2)}) collective-permute-start(bf16[8,4]{1,0:T(8,128)(2,1)S(1)} %bitcast.120), channel_id=1, source_target_pairs={{0,23},{1,0},{2,1},{3,2},{4,3},{5,4},{6,5},{7,6},{8,7},{9,8},{10,9... | collective-permute-start | bytes 200 | tf_op jit(solution)/shard_map/ppermute | solution.py:17
  47.7 13.2 %collective-permute-start.5 = (bf16[8,4,512]{2,1,0:T(4,128)(2,1)S(1)}, bf16[8,4,512]{2,1,0:T(4,128)(2,1)S(1)}, u32[]{:S(2)}, u32[]{:S(2)}) collective-permute-start(bf16[8,4,512]{2,1,0:T(4,128)(2,1)S(1)} %pad_maximum_fusion.4), channel_id=1, source_target_pairs={{0,23},{1,0},{2,1},{3,2},{4,3},{5,4},{6,5},{7,6},{8,7},{9,8},{10,9... | collective-permute-start | bytes 98312 | tf_op jit(solution)/shard_map/ppermute | solution.py:17
  58.8 5.8 %collective-permute-start.3 = (bf16[8,4,512]{2,1,0:T(4,128)(2,1)S(1)}, bf16[8,4,512]{2,1,0:T(4,128)(2,1)S(1)}, u32[]{:S(2)}, u32[]{:S(2)}) collective-permute-start(bf16[8,4,512]{2,1,0:T(4,128)(2,1)S(1)} %pad_maximum_fusion.5), channel_id=1, source_target_pairs={{0,23},{1,0},{2,1},{3,2},{4,3},{5,4},{6,5},{7,6},{8,7},{9,8},{10,9... | collective-permute-start | bytes 98312 | tf_op jit(solution)/shard_map/ppermute | solution.py:17
  60.8 0.7 copy-start.5
  61.5 0.6 copy-start.14
  62.7 3.7 copy-start.7
  64.6 0.6 copy-start.10
  66.2 1.5 copy-start.3
  66.2 1.5 copy-start.16
  77.3 0.9 copy-start.13
  81.6 6.7 %copy-start.6 = (bf16[8,12,512]{2,1,0:T(8,128)(2,1)S(1)}, bf16[8,12,512]{2,1,0:T(8,128)(2,1)}, u32[]{:S(2)}) copy-start(bf16[8,12,512]{2,1,0:T(8,128)(2,1)} %copy-done.5) | copy-start | bytes 294916
  81.6 6.7 %copy-start.15 = (bf16[8,4,512]{2,1,0:T(4,128)(2,1)S(1)}, bf16[8,4,512]{2,1,0:T(4,128)(2,1)}, u32[]{:S(2)}) copy-start(bf16[8,4,512]{2,1,0:T(4,128)(2,1)} %copy-done.14) | copy-start | bytes 98308
  85.5 0.7 copy-start.2
  86.2 12.7 %collective-permute-start.6 = (bf16[8,4,512]{2,1,0:T(4,128)(2,1)S(1)}, bf16[8,4,512]{2,1,0:T(4,128)(2,1)S(1)}, u32[]{:S(2)}, u32[]{:S(2)}) collective-permute-start(bf16[8,4,512]{2,1,0:T(4,128)(2,1)S(1)} %slice.123), channel_id=1, source_target_pairs={{0,1},{1,2},{2,3},{3,4},{4,5},{5,6},{6,7},{7,8},{8,9},{9,10},{10,1... | collective-permute-start | bytes 98312 | tf_op jit(solution)/shard_map/ppermute | solution.py:17
  92.7 23.0 %copy-start.1 = (bf16[8,16,512]{2,1,0:T(8,128)(2,1)S(1)}, bf16[8,16,512]{2,1,0:T(8,128)(2,1)}, u32[]{:S(2)}) copy-start(bf16[8,16,512]{2,1,0:T(8,128)(2,1)} %param.8) | copy-start | bytes 393220
  92.7 23.0 %copy-start.11 = (bf16[8,4,512]{2,1,0:T(4,128)(2,1)S(1)}, bf16[8,4,512]{2,1,0:T(4,128)(2,1)}, u32[]{:S(2)}) copy-start(bf16[8,4,512]{2,1,0:T(4,128)(2,1)} %copy-done.10) | copy-start | bytes 98308
  100.5 14.3 %collective-permute-start.7 = (bf16[4,16,512]{2,1,0:T(8,128)(2,1)}, bf16[4,16,512]{2,1,0:T(8,128)(2,1)}, u32[]{:S(2)}, u32[]{:S(2)}) collective-permute-start(bf16[4,16,512]{2,1,0:T(8,128)(2,1)} %fusion.49), channel_id=1, source_target_pairs={{0,24},{24,48},{48,72},{72,96},{96,120},{120,144},{144,168},{168,1... | collective-permute-start | bytes 196616 | tf_op jit(solution)/shard_map/ppermute | solution.py:17
  106.9 10.6 %copy-start.4 = (bf16[512,512]{1,0:T(8,128)(2,1)S(1)}, bf16[512,512]{1,0:T(8,128)(2,1)}, u32[]{:S(2)}) copy-start(bf16[512,512]{1,0:T(8,128)(2,1)} %convolution_convert_fusion.2) | copy-start | bytes 1572868
  119.1 1.0 copy-start.9
  119.1 1.4 copy-start.20
  119.1 150.4 %copy-start.12 = (bf16[8,16,512]{2,1,0:T(8,128)(2,1)S(1)}, bf16[8,16,512]{2,1,0:T(8,128)(2,1)}, u32[]{:S(2)}) copy-start(bf16[8,16,512]{2,1,0:T(8,128)(2,1)} %param.9) | copy-start | bytes 393220
  119.1 150.4 %copy-start.18 = (f32[512]{0:T(512)S(1)}, f32[512]{0:T(512)}, u32[]{:S(2)}) copy-start(f32[512]{0:T(512)} %param.11) | copy-start | bytes 6148
  119.1 410.0 %reduce-scatter.7.cloned.1.call-start = ((), (), s32[]{:S(2)}) async-start(), calls=%async_computation.3 | async-start | bytes 409600
Sparse Core Ops, SparseCore 0:
  119.2 148.4 reduce-scatter.4
  271.1 157.0 reduce-scatter.6
where the time goes:
time: 539 us; the launch traced here: 537 us
  blocking collectives  258 us (48%)
  waiting for transfers between devices  162 us (30%)
  starting transfers between devices  45.7 us (8%)
  local copies, waits for them, and re-layouts  23.7 us (4%)
  other arithmetic  18.6 us (3%)
  matrix products  15.3 us (3%)
  between operations  14.6 us (3%)
    psum x1, blocking collectives, local(): lax.psum(row_slices[:, 3 * width:].astype(jnp.bfloat16), 'cols')  150 us
    reduce_scatter x1, waiting for transfers between devices, local(): lax.psum_scatter(jnp.concatenate([qkv_part, out_part], axis=1).astype(jnp...  146 us
    psum x1, blocking collectives, local(): lax.psum((gain_local, table_local), ('rows', 'cols'))  107 us
    ppermute x8, starting transfers between devices, shifted(): lax.ppermute(value, axis, [(i, (i + by) % size) for i in range(size)])  45.6 us
    ppermute x8, waiting for transfers between devices, shifted(): lax.ppermute(value, axis, [(i, (i + by) % size) for i in range(size)])  16.2 us
  transfers between devices with their start and end apart: 10, of which 5 were waited for; matrix products, arithmetic and copies ran while one was open for 5% of the time, Pallas kernels for 0%

commit v1 on v0

v1 whole, which is shorter than its diff:
```python
import jax
import jax.numpy as jnp
from jax import lax
from jax.experimental import pallas as pl
from jax.experimental.pallas import tpu as pltpu
from jax.sharding import Mesh
from jax.sharding import PartitionSpec as P

D = 512
HEADS = 16
HEAD_DIM = 32
WIN = 8
SHIFT = 4
NBIAS = 225
AREA = WIN * WIN
TOKENS = 128
GROUP = 4
SCALE = HEAD_DIM ** (-0.5)
EPSILON = 1e-05

F32 = jnp.float32
BF16 = jnp.bfloat16

PARTS = (("y", 8), ("zh", 2), ("core", 2), ("x", 4), ("zl", 6))
ROWS = ("y", "zh", "core")
COLS = ("x", "zl")
NROWS = 32
NCOLS = 24

ANY_PARAMS = pltpu.CompilerParams(vmem_limit_bytes=48 * 1024 * 1024)


def dot(a, b):
    return lax.dot_general(a, b, (((1,), (0,)), ((), ())), preferred_element_type=F32)


def dot_nt(a, b):
    return lax.dot_general(a, b, (((1,), (1,)), ((), ())), preferred_element_type=F32)


def dot_tn(a, b):
    return lax.dot_general(a, b, (((0,), (0,)), ((), ())), preferred_element_type=F32)


def iota(shape, dim):
    return lax.broadcasted_iota(jnp.int32, shape, dim)


def split_high_low(value):
    high = value.astype(BF16)
    low = (value - high.astype(F32)).astype(BF16)
    return high, low


def layer_stats(floats):
    average = jnp.mean(floats, axis=-1, keepdims=True)
    centred = floats - average
    variance = jnp.mean(centred * centred, axis=-1, keepdims=True)
    inv_std = lax.rsqrt(variance + EPSILON)
    return centred * inv_std, inv_std


def pack_kernel(tok, cot, reg, to_up, to_left, to_diag):
    to_up[8] = jnp.zeros((12, D), BF16)
    to_left[8] = jnp.zeros((4, D), BF16)
    to_diag[8] = jnp.zeros((4, D), BF16)
    for k, src in ((0, tok), (4, cot)):
        for r in range(SHIFT):
            top = src[r].astype(F32)
            low = src[SHIFT + r].astype(F32)
            to_up[k + r] = top[4:16].astype(BF16)
            to_diag[k + r] = top[0:4].astype(BF16)
            to_left[k + r] = low[0:4].astype(BF16)
    labels = reg[...].astype(F32)
    to_up[8, 0:4, 0:16] = labels[0:4].astype(BF16)
    to_diag[8, 0:4, 0:16] = labels[0:4].astype(BF16)
    to_left[8, 0:4, 0:16] = labels[4:8].astype(BF16)


def bias_kernel(table, bucket, bias, bucket2, padded):
    padded[...] = jnp.zeros_like(padded)
    padded[0:NBIAS, 0:HEADS] = table[...]
    turned = padded[...].T
    both = jnp.concatenate([bucket[...], bucket[...]], axis=1)
    bucket2[...] = both
    for block in range(AREA // 8):
        index = both[block * 8 : block * 8 + 8]
        upper = index >= 128
        within = jnp.bitwise_and(index, 127)
        for h in range(HEADS):
            first = jnp.broadcast_to(turned[h : h + 1, 0:128], (8, 128))
            second = jnp.broadcast_to(turned[h : h + 1, 128:256], (8, 128))
            got_first = jnp.take_along_axis(first, within, axis=1, mode="promise_in_bounds")
            got_second = jnp.take_along_axis(second, within, axis=1, mode="promise_in_bounds")
            bias[h, block * 8 : block * 8 + 8, :] = jnp.where(upper, got_second, got_first)


def window_kernel(
    tok, cot, reg, up, left, diag, gain, wqkv, wout, bias, bucket2,
    send, keep, own_grad, down_grad, right_grad, diag_grad,
    frame_t, frame_c, labels, packed, attended, grad_att, pairs, grad_in,
):
    for src, k, frame in ((tok, 0, frame_t), (cot, 4, frame_c)):
        for r in range(SHIFT):
            own = src[SHIFT + r].astype(F32)
            frame[r * 8 : r * 8 + 8, :] = own[4:12]
            frame[64 + r * 8 : 64 + r * 8 + 4, :] = own[12:16]
            frame[64 + r * 8 + 4 : 64 + r * 8 + 8, :] = left[k + r].astype(F32)
            s = SHIFT + r
            below = up[k + r].astype(F32)
            frame[s * 8 : s * 8 + 8, :] = below[0:8]
            frame[64 + s * 8 : 64 + s * 8 + 4, :] = below[8:12]
            frame[64 + s * 8 + 4 : 64 + s * 8 + 8, :] = diag[k + r].astype(F32)

    mine = reg[...].astype(F32)
    labels[...] = jnp.zeros_like(labels)
    labels[0:4, 0:12] = mine[4:8, 4:16]
    labels[0:4, 12:16] = left[8, 0:4, 0:16].astype(F32)[:, 0:4]
    labels[4:8, 0:12] = up[8, 0:4, 0:16].astype(F32)[:, 4:16]
    labels[4:8, 12:16] = diag[8, 0:4, 0:16].astype(F32)[:, 0:4]
    row_tile = (lax.axis_index("y") * 2 + lax.axis_index("zh")) * 2 + lax.axis_index("core")
    last = (row_tile == NROWS - 1).astype(F32)
    flags = jnp.where(iota((8, 128), 0) >= 4, 2.0, 0.0) * last
    coded = labels[...] + flags + jnp.where(iota((8, 128), 1) >= 8, 4.0, 0.0)
    token_lane = iota((128, 128), 1)
    token_row = iota((128, 128), 0)

    def column_of(token):
        return (token // 64) * 8 + token % 8

    def row_of(token):
        return (token // 8) % 8

    pick_lane = (column_of(token_lane) == token_row).astype(BF16)
    wide = dot(coded.astype(BF16), pick_lane)
    code_row = jnp.sum(
        jnp.where(row_of(iota((8, 128), 1)) == iota((8, 128), 0), wide, 0.0), axis=0, keepdims=True
    )
    pick_row = (column_of(token_row) == token_lane).astype(BF16)
    padded_codes = jnp.concatenate([coded, jnp.zeros((120, 128), F32)], axis=0).astype(BF16)
    tall = dot_nt(pick_row, padded_codes)
    code_col = jnp.sum(
        jnp.where(row_of(token_row) == token_lane, tall, 0.0), axis=1, keepdims=True
    )
    allowed = jnp.broadcast_to(code_col, (128, 128)) == jnp.broadcast_to(code_row, (128, 128))
    allowed4 = jnp.concatenate([allowed.astype(F32)] * GROUP, axis=0) > 0.5

    hat, _ = layer_stats(frame_t[...])
    normed = (hat * gain[...]).astype(BF16)
    cots = frame_c[...].astype(BF16)
    packed[...] = dot(normed, wqkv[...]).astype(BF16)
    grad_att[...] = dot_nt(cots, wout[...]).astype(BF16)
    send[0:TOKENS, 3 * D : 4 * D] = cots

    lane_head = iota((TOKENS, 128), 1) // HEAD_DIM
    masks = [lane_head == h for h in range(GROUP)]

    def stacked(value):
        return jnp.concatenate(
            [jnp.where(m, value, jnp.zeros_like(value)) for m in masks], axis=0
        )

    def beside(value):
        return jnp.concatenate([value[h * 128 : h * 128 + 128] for h in range(GROUP)], axis=1)

    for g in range(HEADS // GROUP):
        at = g * 128
        query = packed[:, at : at + 128]
        key = packed[:, D + at : D + at + 128]
        value = packed[:, 2 * D + at : 2 * D + at + 128]
        outer = grad_att[:, at : at + 128]
        query_s = stacked(query)
        outer_s = stacked(outer)
        biases = []
        for h in range(GROUP):
            one = bias[g * GROUP + h]
            biases += [one, one]
        scores = dot_nt(query_s, key) * SCALE + jnp.concatenate(biases, axis=0)
        scores = jnp.where(allowed4, scores, -1e30)
        raised = jnp.exp(scores - jnp.max(scores, axis=-1, keepdims=True))
        probs = raised / jnp.sum(raised, axis=-1, keepdims=True)
        probs_low = probs.astype(BF16)
        grad_probs = dot_nt(outer_s, value)
        inner = probs * grad_probs
        grad_scores = probs * (grad_probs - jnp.sum(inner, axis=-1, keepdims=True))
        grad_scaled = (grad_scores * SCALE).astype(BF16)
        attended[:, at : at + 128] = dot(beside(probs_low), stacked(value)).astype(BF16)
        send[0:TOKENS, at : at + 128] = dot(beside(grad_scaled), stacked(key)).astype(BF16)
        send[0:TOKENS, D + at : D + at + 128] = dot_tn(grad_scaled, query_s).astype(BF16)
        send[0:TOKENS, 2 * D + at : 2 * D + at + 128] = dot_tn(probs_low, outer_s).astype(BF16)
        for h in range(GROUP):
            one = grad_scores[h * 128 : h * 128 + 128]
            pairs[g * GROUP + h] = one[0:64] + one[64:128]

    core = lax.axis_index("core")
    for k, matrix in ((0, normed), (1, attended[...])):
        turned = matrix.astype(F32).T.reshape(16, 2, 16, TOKENS)
        even, odd = turned[:, 0].reshape(256, TOKENS), turned[:, 1].reshape(256, TOKENS)
        kept = jnp.where(core == 0, even, odd).astype(BF16)
        sent = jnp.where(core == 0, odd, even).astype(BF16)
        for b in range(2):
            lane = (2 * k + b) * 128
            keep[:, lane : lane + 128] = kept[b * 128 : b * 128 + 128]
            send[0:TOKENS, 4 * D + lane : 4 * D + lane + 128] = sent[b * 128 : b * 128 + 128]

    grad_normed = dot_nt(send[0:TOKENS, 0 : 3 * D], wqkv[...])
    grad_in[...] = grad_normed
    gain_sum = jnp.sum(grad_normed * hat, axis=0, keepdims=True)

    bucket_of = iota((256, 128), 0)

    def add_row(i, total):
        high, low = split_high_low(pairs[:, i, :])
        hot = (bucket_of == jnp.broadcast_to(bucket2[pl.ds(i, 1), :], (256, 128))).astype(BF16)
        return total + dot_nt(jnp.concatenate([high, low], axis=0), hot)

    sums = lax.fori_loop(0, AREA, add_row, jnp.zeros((2 * HEADS, 256), F32), unroll=8)
    table = sums[0:HEADS] + sums[HEADS : 2 * HEADS]
    high, low = split_high_low(table)
    send[TOKENS : TOKENS + 16, 0:256] = high
    send[TOKENS : TOKENS + 16, 256:512] = low
    high, low = split_high_low(jnp.concatenate([gain_sum, jnp.zeros((15, D), F32)], axis=0))
    send[TOKENS : TOKENS + 16, 512:1024] = high
    send[TOKENS : TOKENS + 16, 1024:1536] = low
    send[TOKENS : TOKENS + 16, 1536:2560] = jnp.zeros((16, 1024), BF16)

    for r in range(SHIFT):
        s = SHIFT + r
        own_grad[r, 0:8, :] = grad_in[r * 8 : r * 8 + 8, :]
        own_grad[r, 8:12, :] = grad_in[64 + r * 8 : 64 + r * 8 + 4, :]
        right_grad[r] = grad_in[64 + r * 8 : 64 + r * 8 + 8, :][4:8].astype(BF16)
        down_grad[r] = jnp.concatenate(
            [grad_in[s * 8 : s * 8 + 8, :], grad_in[64 + s * 8 : 64 + s * 8 + 8, :][0:4]], axis=0
        ).astype(BF16)
        diag_grad[r] = grad_in[64 + s * 8 : 64 + s * 8 + 8, :][4:8].astype(BF16)


def product_kernel(mine, other, keep, out):
    def rows(block):
        lane = block * 128
        return jnp.concatenate(
            [keep[:, lane : lane + 128], other[0:TOKENS, 4 * D + lane : 4 * D + lane + 128]], axis=1
        )

    right = jnp.concatenate([mine[0:TOKENS, 0 : 4 * D], other[0:TOKENS, 0 : 4 * D]], axis=0)
    for half in range(2):
        qkv = dot(rows(half), right[:, 0 : 3 * D]).astype(BF16)
        proj = dot(rows(2 + half), right[:, 3 * D : 4 * D]).astype(BF16)
        for k in range(4):
            y = half * 4 + k
            for x in range(4):
                out[y, x, :, 0:384] = qkv[k * 32 : k * 32 + 32, x * 384 : x * 384 + 384]
                out[y, x, :, 384:512] = proj[k * 32 : k * 32 + 32, x * 128 : x * 128 + 128]
    small = mine[TOKENS : TOKENS + 16, 0:1536].astype(F32) + other[TOKENS : TOKENS + 16, 0:1536].astype(F32)
    table = small[:, 0:256] + small[:, 256:512]
    gain = small[0:8, 512:1024] + small[0:8, 1024:1536]
    for x in range(4):
        part = jnp.concatenate(
            [
                table[4 * x : 4 * x + 4, 0:128],
                table[4 * x : 4 * x + 4, 128:256],
                gain[:, x * 128 : x * 128 + 128],
            ],
            axis=0,
        )
        high, low = split_high_low(part)
        both = jnp.concatenate([high, low], axis=0)
        for y in range(8):
            out[y, x, :, 512:640] = both


def plane_sum_kernel(parts, out):
    total = jnp.sum(parts[...].astype(F32), axis=0)
    small = (total[0:16, 512:640] + total[16:32, 512:640]).astype(BF16)
    for zh in range(2):
        rows = total[zh * 16 : zh * 16 + 16]
        proj = rows[:, 384:512].astype(BF16)
        for zl in range(6):
            lane = (zl // 2) * 128
            qkv = rows[:, lane : lane + 128]
            if zl % 2 == 1:
                qkv = pltpu.roll(qkv, 64, 1)
            out[zh * 6 + zl, :, 0:128] = proj
            out[zh * 6 + zl, :, 128:256] = qkv.astype(BF16)
            out[zh * 6 + zl, :, 256:384] = small


def line_sum_kernel(parts, qkv, out):
    total = jnp.sum(parts[...].astype(F32), axis=0)
    qkv[...] = total[:, 128:192]
    for x in range(4):
        out[x, 0:16, :] = total[:, 0:128]
        out[x, 16:32, :] = total[:, 256:384]


def finish_kernel(parts, proj, gain, table):
    low, high = [], []
    for x in range(4):
        proj[:, x * 128 : x * 128 + 128] = parts[x, 0:16, :]
        gain[:, x * 128 : x * 128 + 128] = parts[x, 24:25, :]
        low.append(parts[x, 16:20, :])
        high.append(parts[x, 20:24, :])
    pad = jnp.zeros((112, 128), F32)
    low = jnp.concatenate(low + [pad], axis=0)
    high = jnp.concatenate(high + [pad], axis=0)
    table[0:128, :] = low.T[:, 0:HEADS]
    table[128:NBIAS, :] = high.T[0 : NBIAS - 128, 0:HEADS]


def token_kernel(tok, cot, gain, own, above, left, diag, out, grads):
    for r in range(SHIFT):
        grads[r, 0:4, :] = diag[r].astype(F32)
        grads[r, 4:16, :] = above[r].astype(F32)
        grads[SHIFT + r, 0:4, :] = left[r].astype(F32)
        grads[SHIFT + r, 4:16, :] = own[r]
    hat, inv_std = layer_stats(tok[...].astype(F32))
    grad_hat = grads[...] * gain[...].reshape(1, 1, D)
    moved = (
        grad_hat
        - jnp.mean(grad_hat, axis=-1, keepdims=True)
        - hat * jnp.mean(grad_hat * hat, axis=-1, keepdims=True)
    )
    out[...] = (cot[...].astype(F32) + inv_std * moved).astype(BF16)


def shape(dims, dtype):
    return jax.ShapeDtypeStruct(dims, dtype)


def call(kernel, outs, args, scratch=(), flops=0, moved=0):
    return pl.pallas_call(
        kernel,
        out_shape=outs,
        scratch_shapes=list(scratch),
        compiler_params=ANY_PARAMS,
        cost_estimate=pl.CostEstimate(flops=flops, bytes_accessed=moved, transcendentals=0),
    )(*args)


def neighbour(value, down, right):
    pairs = [
        (r * NCOLS + c, ((r + down) % NROWS) * NCOLS + (c + right) % NCOLS)
        for r in range(NROWS)
        for c in range(NCOLS)
    ]
    return lax.ppermute(value, ROWS + COLS, pairs)


def local(tokens, cotangent, region, norm_gain, qkv_weight, out_weight, bias_table, bias_bucket):
    gain = norm_gain.reshape(1, D)
    to_up, to_left, to_diag = call(
        pack_kernel,
        [shape((9, 12, D), BF16), shape((9, 4, D), BF16), shape((9, 4, D), BF16)],
        (tokens, cotangent, region),
        moved=1 << 19,
    )
    up = neighbour(to_up, -1, 0)
    diag = neighbour(to_diag, -1, -1)
    left = neighbour(to_left, 0, -1)
    bias, bucket2 = call(
        bias_kernel,
        [shape((HEADS, AREA, 128), F32), shape((AREA, 128), jnp.int32)],
        (bias_table, bias_bucket),
        [pltpu.VMEM((256, 128), F32)],
        moved=1 << 23,
    )
    send, keep, own_grad, down_grad, right_grad, diag_grad = call(
        window_kernel,
        [
            shape((TOKENS + 16, 5 * D), BF16),
            shape((TOKENS, D), BF16),
            shape((4, 12, D), F32),
            shape((4, 12, D), BF16),
            shape((4, 4, D), BF16),
            shape((4, 4, D), BF16),
        ],
        (tokens, cotangent, region, up, left, diag, gain, qkv_weight, out_weight, bias, bucket2),
        [
            pltpu.VMEM((TOKENS, D), F32),
            pltpu.VMEM((TOKENS, D), F32),
            pltpu.VMEM((8, 128), F32),
            pltpu.VMEM((TOKENS, 3 * D), BF16),
            pltpu.VMEM((TOKENS, D), BF16),
            pltpu.VMEM((TOKENS, D), BF16),
            pltpu.VMEM((HEADS, AREA, 128), F32),
            pltpu.VMEM((TOKENS, D), F32),
        ],
        flops=1 << 30,
        moved=1 << 23,
    )
    other = lax.ppermute(send, "core", [(0, 1), (1, 0)])
    above_grad = neighbour(down_grad, 1, 0)
    left_grad = neighbour(right_grad, 0, 1)
    corner_grad = neighbour(diag_grad, 1, 1)
    products = call(
        product_kernel,
        shape((8, 4, 32, 640), BF16),
        (send, other, keep),
        flops=1 << 29,
        moved=1 << 21,
    )
    planes = lax.all_to_all(products.reshape(32, 32, 640), ("y", "x"), 0, 0)
    chunks = call(plane_sum_kernel, shape((12, 16, 384), BF16), (planes,), moved=1 << 21)
    lines = lax.all_to_all(chunks, ("zh", "zl"), 0, 0)
    grad_qkv, finals = call(
        line_sum_kernel, [shape((16, 64), F32), shape((4, 32, 128), F32)], (lines,), moved=1 << 18
    )
    finals = lax.all_to_all(finals, "x", 0, 0)
    grad_out_weight, grad_gain, grad_bias_table = call(
        finish_kernel,
        [shape((16, D), F32), shape((1, D), F32), shape((NBIAS, HEADS), F32)],
        (finals,),
        moved=1 << 17,
    )
    grad_tokens = call(
        token_kernel,
        shape((8, 16, D), BF16),
        (tokens, cotangent, gain, own_grad, above_grad, left_grad, corner_grad),
        [pltpu.VMEM((8, 16, D), F32)],
        moved=1 << 20,
    )
    return (grad_tokens, grad_qkv, grad_out_weight, grad_gain.reshape(D), grad_bias_table)


def solution(mesh):
    parts = Mesh(mesh.devices.reshape([n for _, n in PARTS]), [name for name, _ in PARTS])
    return jax.shard_map(
        local,
        mesh=parts,
        in_specs=(P(ROWS, COLS, None), P(ROWS, COLS, None), P(ROWS, COLS), P(), P(), P(), P(), P()),
        out_specs=(P(ROWS, COLS, None), P(ROWS, COLS), P(ROWS, None), P(), P()),
        check_vma=False,
    )
```

time: 539 us -> 137 us (0.25)
  the two profiles are of different devices: /device:TPU:32 before, /device:TPU:1 now
where the time goes in v1:
time: 137 us; the launch traced here: 136 us
  starting transfers between devices  63.7 us (46%)
  blocking collectives  41.5 us (30%)
  Pallas kernels  10.5 us (8%)
  local copies, waits for them, and re-layouts  10.4 us (8%)
  waiting for transfers between devices  9.2 us (7%)
    ppermute x6, starting transfers between devices, neighbour(): return lax.ppermute(value, ROWS + COLS, pairs)  52.2 us
    all_to_all x1, blocking collectives, local(): planes = lax.all_to_all(products.reshape(32, 32, 640), ('y', 'x'), 0, 0)  41.5 us
    pallas_call x8, Pallas kernels, call(): pl.pallas_call(kernel, out_shape=outs, scratch_shapes=list(scratch), comp...  10.5 us
    unnamed x28, local copies, waits for them, and re-layouts  10.4 us
    ppermute x6, waiting for transfers between devices, neighbour(): return lax.ppermute(value, ROWS + COLS, pairs)  7.38 us
    all_to_all x1, starting transfers between devices, local(): lines = lax.all_to_all(chunks, ('zh', 'zl'), 0, 0)  5.83 us
    all_to_all x1, starting transfers between devices, local(): finals = lax.all_to_all(finals, 'x', 0, 0)  3.28 us
  transfers between devices with their start and end apart: 9, of which 3 were waited for; matrix products, arithmetic and copies ran while one was open for 1% of the time, Pallas kernels for 2%

profile of v1, /device:TPU:1, one launch (start us, length us, event | category | flops | bytes accessed | tf_op | source)
XLA Modules:
  0.0 136.1 jit_solution(17818986655121822515)
XLA Ops:
  0.6 0.0 copy-start
  0.6 0.9 copy-done
  1.5 0.0 copy-start.3
  1.5 0.9 copy-done.3
  2.4 0.0 copy-start.7
  2.4 0.7 copy-done.7
  3.2 12.4 %collective-permute-start = (bf16[9,12,512]{2,1,0:T(8,128)(2,1)S(1)}, bf16[9,12,512]{2,1,0:T(8,128)(2,1)S(1)}, u32[]{:S(2)}, u32[]{:S(2)}) collective-permute-start(bf16[9,12,512]{2,1,0:T(8,128)(2,1)S(1)} %get-tuple-element.21), channel_id=1, source_target_pairs={{0,744},{1,745},{2,746},{3,747},{4,748},{5,749},{6,750},{7,751},{8... | collective-permute-start | bytes 331784 | tf_op jit(solution)/shard_map/ppermute | solution.py:346
  15.6 5.6 %collective-permute-start.1 = (bf16[9,4,512]{2,1,0:T(4,128)(2,1)S(1)}, bf16[9,4,512]{2,1,0:T(4,128)(2,1)S(1)}, u32[]{:S(2)}, u32[]{:S(2)}) collective-permute-start(bf16[9,4,512]{2,1,0:T(4,128)(2,1)S(1)} %get-tuple-element.22), channel_id=1, source_target_pairs={{0,23},{1,0},{2,1},{3,2},{4,3},{5,4},{6,5},{7,6},{8,7},{9,8},{10,9... | collective-permute-start | bytes 110600 | tf_op jit(solution)/shard_map/ppermute | solution.py:346
  21.2 12.8 %collective-permute-start.2 = (bf16[9,4,512]{2,1,0:T(4,128)(2,1)S(1)}, bf16[9,4,512]{2,1,0:T(4,128)(2,1)S(1)}, u32[]{:S(2)}, u32[]{:S(2)}) collective-permute-start(bf16[9,4,512]{2,1,0:T(4,128)(2,1)S(1)} %get-tuple-element.23), channel_id=1, source_target_pairs={{0,767},{1,744},{2,745},{3,746},{4,747},{5,748},{6,749},{7,750},{8... | collective-permute-start | bytes 110600 | tf_op jit(solution)/shard_map/ppermute | solution.py:346
  34.1 0.8 copy.13.table
  34.9 0.0 copy-start.6
  34.9 0.8 copy-done.6
  35.6 0.5 shard_map.120
  36.1 0.0 collective-permute-done.1.left
  36.1 0.0 collective-permute-done.2.diag
  36.2 0.0 collective-permute-done.up
  36.2 0.0 copy-start.1
  36.2 0.9 copy-done.1
  37.1 0.0 copy-start.4
  37.1 0.9 copy-done.4
  38.0 0.0 copy-start.8
  38.0 0.7 copy-done.8
  38.7 0.7 copy-done.9
  39.4 1.4 %copy-done.11 = bf16[512,1536]{1,0:T(8,128)(2,1)S(1)} copy-done((bf16[512,1536]{1,0:T(8,128)(2,1)S(1)}, bf16[512,1536]{1,0:T(8,128)(2,1)}, u32[]{:S(2)}) %copy-start.11) | copy-done | bytes 1572888
  40.8 1.0 copy-done.12
  41.8 6.4 %shard_map.121 = (bf16[144,2560]{1,0:T(8,128)(2,1)S(1)}, bf16[128,512]{1,0:T(8,128)(2,1)S(1)}, f32[4,12,512]{2,1,0:T(8,128)S(1)}, bf16[4,12,512]{2,1,0:T(8,128)(...) custom-call(bf16[8,16,512]{2,1,0:T(8,128)(2,1)S(1)} %copy-done.1, ...), custom_call_target="tpu_custom_call" | custom-call | flops 1073741824 | bytes 8388608 | tf_op jit(solution)/shard_map/pallas_call | solution.py:331
  48.2 2.4 %collective-permute-start.6 = (bf16[144,2560]{1,0:T(8,128)(2,1)S(1)}, bf16[144,2560]{1,0:T(8,128)(2,1)S(1)}, u32[]{:S(2)}, u32[]{:S(2)}) collective-permute-start(bf16[144,2560]{1,0:T(8,128)(2,1)S(1)} %get-tuple-element.30.mine), channel_id=1, source_target_pairs={{0,24},{24,0},{1,25},{25,1},{2,26},{26,2},{3,27},{27,3},{4,28},{28... | collective-permute-start | bytes 2211848 | tf_op jit(solution)/shard_map/ppermute | solution.py:391
  50.6 1.8 %collective-permute-done.6.other = bf16[144,2560]{1,0:T(8,128)(2,1)S(1)} collective-permute-done((bf16[144,2560]{1,0:T(8,128)(2,1)S(1)}, bf16[144,2560]{1,0:T(8,128)(2,1)S(1)}, u32[]{:S(2)}, u32[]{:S(2)}) %collective-permute-start.6) | collective-permute-done | bytes 737312 | tf_op jit(solution)/shard_map/ppermute | solution.py:391
  52.4 0.4 shard_map.123
  52.9 41.5 %all_to_all.15.parts = bf16[32,32,640]{2,1,0:T(8,128)(2,1)S(1)} all-to-all(bf16[32,32,640]{2,1,0:T(8,128)(2,1)S(1)} %bitcast.3), channel_id=1, replica_groups=mesh['y'=8,'zh'=2,'core'=2,'x'=4,'zl'=6] {'y','x'}, dimensions={0} | all-to-all | bytes 2621440 | tf_op jit(solution)/shard_map/all_to_all | solution.py:402
  94.4 0.9 shard_map.124
  95.3 5.8 %all-to-all-start.1 = ((bf16[12,16,384]{2,1,0:T(8,128)(2,1)}), bf16[12,16,384]{2,1,0:T(8,128)(2,1)S(1)}, u32[]{:S(2)}, u32[]{:S(2)}) async-start(bf16[12,16,384]{2,1,0:T(8,128)(2,1)} %shard_map.124), calls=%async_computation.1 | async-start | bytes 294912 | tf_op jit(solution)/shard_map/all_to_all | solution.py:404
  101.2 12.1 %collective-permute-start.3 = (bf16[4,12,512]{2,1,0:T(8,128)(2,1)S(1)}, bf16[4,12,512]{2,1,0:T(8,128)(2,1)S(1)}, u32[]{:S(2)}, u32[]{:S(2)}) collective-permute-start(bf16[4,12,512]{2,1,0:T(8,128)(2,1)S(1)} %get-tuple-element.27), channel_id=1, source_target_pairs={{0,24},{1,25},{2,26},{3,27},{4,28},{5,29},{6,30},{7,31},{8,32},{9,... | collective-permute-start | bytes 147464 | tf_op jit(solution)/shard_map/ppermute | solution.py:346
  113.3 0.0 all-to-all-done.1.parts
  113.3 0.7 shard_map.125
  113.9 3.3 %all-to-all-start.2 = ((f32[4,32,128]{2,1,0:T(8,128)}), f32[4,32,128]{2,1,0:T(8,128)S(1)}, u32[]{:S(2)}, u32[]{:S(2)}) async-start(f32[4,32,128]{2,1,0:T(8,128)} %get-tuple-element.33), calls=%async_computation.2 | async-start | bytes 131072 | tf_op jit(solution)/shard_map/all_to_all | solution.py:408
  117.2 2.2 %collective-permute-start.4 = (bf16[4,4,512]{2,1,0:T(4,128)(2,1)S(1)}, bf16[4,4,512]{2,1,0:T(4,128)(2,1)S(1)}, u32[]{:S(2)}, u32[]{:S(2)}) collective-permute-start(bf16[4,4,512]{2,1,0:T(4,128)(2,1)S(1)} %get-tuple-element.28), channel_id=1, source_target_pairs={{0,1},{1,2},{2,3},{3,4},{4,5},{5,6},{6,7},{7,8},{8,9},{9,10},{10,1... | collective-permute-start | bytes 49160 | tf_op jit(solution)/shard_map/ppermute | solution.py:346
  119.4 7.0 %collective-permute-start.5 = (bf16[4,4,512]{2,1,0:T(4,128)(2,1)S(1)}, bf16[4,4,512]{2,1,0:T(4,128)(2,1)S(1)}, u32[]{:S(2)}, u32[]{:S(2)}) collective-permute-start(bf16[4,4,512]{2,1,0:T(4,128)(2,1)S(1)} %get-tuple-element.29), channel_id=1, source_target_pairs={{0,25},{1,26},{2,27},{3,28},{4,29},{5,30},{6,31},{7,32},{8,33},{9,... | collective-permute-start | bytes 49160 | tf_op jit(solution)/shard_map/ppermute | solution.py:346
  126.5 2.2 %collective-permute-done.4.left = bf16[4,4,512]{2,1,0:T(4,128)(2,1)S(1)} collective-permute-done((bf16[4,4,512]{2,1,0:T(4,128)(2,1)S(1)}, bf16[4,4,512]{2,1,0:T(4,128)(2,1)S(1)}, u32[]{:S(2)}, u32[]{:S(2)}) %collective-permute-start.4) | collective-permute-done | bytes 16416 | tf_op jit(solution)/shard_map/ppermute | solution.py:346
  128.6 5.2 %collective-permute-done.5.diag = bf16[4,4,512]{2,1,0:T(4,128)(2,1)S(1)} collective-permute-done((bf16[4,4,512]{2,1,0:T(4,128)(2,1)S(1)}, bf16[4,4,512]{2,1,0:T(4,128)(2,1)S(1)}, u32[]{:S(2)}, u32[]{:S(2)}) %collective-permute-start.5) | collective-permute-done | bytes 16416 | tf_op jit(solution)/shard_map/ppermute | solution.py:346
  133.8 0.0 collective-permute-done.3.above
  133.9 0.0 copy-done.2
  133.9 0.0 copy-done.5
  133.9 0.0 copy-done.10
  133.9 1.0 shard_map.122
  134.8 0.0 all-to-all-done.2.parts
  134.8 0.6 shard_map.126
  135.5 0.7 copy.14
  (7 shorter events, 0.0 us)
Async XLA Ops:
  0.6 0.9 copy-start
  1.5 0.9 copy-start.3
  2.4 0.7 copy-start.7
  3.2 33.0 %collective-permute-start = (bf16[9,12,512]{2,1,0:T(8,128)(2,1)S(1)}, bf16[9,12,512]{2,1,0:T(8,128)(2,1)S(1)}, u32[]{:S(2)}, u32[]{:S(2)}) collective-permute-start(bf16[9,12,512]{2,1,0:T(8,128)(2,1)S(1)} %get-tuple-element.21), channel_id=1, source_target_pairs={{0,744},{1,745},{2,746},{3,747},{4,748},{5,749},{6,750},{7,751},{8... | collective-permute-start | bytes 331784 | tf_op jit(solution)/shard_map/ppermute | solution.py:346
  15.6 20.5 %collective-permute-start.1 = (bf16[9,4,512]{2,1,0:T(4,128)(2,1)S(1)}, bf16[9,4,512]{2,1,0:T(4,128)(2,1)S(1)}, u32[]{:S(2)}, u32[]{:S(2)}) collective-permute-start(bf16[9,4,512]{2,1,0:T(4,128)(2,1)S(1)} %get-tuple-element.22), channel_id=1, source_target_pairs={{0,23},{1,0},{2,1},{3,2},{4,3},{5,4},{6,5},{7,6},{8,7},{9,8},{10,9... | collective-permute-start | bytes 110600 | tf_op jit(solution)/shard_map/ppermute | solution.py:346
  21.2 14.9 %collective-permute-start.2 = (bf16[9,4,512]{2,1,0:T(4,128)(2,1)S(1)}, bf16[9,4,512]{2,1,0:T(4,128)(2,1)S(1)}, u32[]{:S(2)}, u32[]{:S(2)}) collective-permute-start(bf16[9,4,512]{2,1,0:T(4,128)(2,1)S(1)} %get-tuple-element.23), channel_id=1, source_target_pairs={{0,767},{1,744},{2,745},{3,746},{4,747},{5,748},{6,749},{7,750},{8... | collective-permute-start | bytes 110600 | tf_op jit(solution)/shard_map/ppermute | solution.py:346
  34.9 0.8 copy-start.6
  36.2 0.9 copy-start.1
  37.1 0.9 copy-start.4
  38.0 0.7 copy-start.8
  38.7 0.7 copy-start.9
  39.3 1.4 %copy-start.11 = (bf16[512,1536]{1,0:T(8,128)(2,1)S(1)}, bf16[512,1536]{1,0:T(8,128)(2,1)}, u32[]{:S(2)}) copy-start(bf16[512,1536]{1,0:T(8,128)(2,1)} %wqkv.1) | copy-start | bytes 4718596
  40.8 1.0 copy-start.12
  48.2 4.2 %collective-permute-start.6 = (bf16[144,2560]{1,0:T(8,128)(2,1)S(1)}, bf16[144,2560]{1,0:T(8,128)(2,1)S(1)}, u32[]{:S(2)}, u32[]{:S(2)}) collective-permute-start(bf16[144,2560]{1,0:T(8,128)(2,1)S(1)} %get-tuple-element.30.mine), channel_id=1, source_target_pairs={{0,24},{24,0},{1,25},{25,1},{2,26},{26,2},{3,27},{27,3},{4,28},{28... | collective-permute-start | bytes 2211848 | tf_op jit(solution)/shard_map/ppermute | solution.py:391
  94.4 39.5 %copy-start.2 = (bf16[8,16,512]{2,1,0:T(8,128)(2,1)S(1)}, bf16[8,16,512]{2,1,0:T(8,128)(2,1)}, u32[]{:S(2)}) copy-start(bf16[8,16,512]{2,1,0:T(8,128)(2,1)} %tok.5) | copy-start | bytes 393220
  94.4 39.5 %copy-start.5 = (bf16[8,16,512]{2,1,0:T(8,128)(2,1)S(1)}, bf16[8,16,512]{2,1,0:T(8,128)(2,1)}, u32[]{:S(2)}) copy-start(bf16[8,16,512]{2,1,0:T(8,128)(2,1)} %cot.5) | copy-start | bytes 393220
  94.4 39.5 %copy-start.10 = (f32[512]{0:T(512)S(1)}, f32[512]{0:T(512)}, u32[]{:S(2)}) copy-start(f32[512]{0:T(512)} %param.11) | copy-start | bytes 6148
  95.3 18.0 %all-to-all-start.1 = ((bf16[12,16,384]{2,1,0:T(8,128)(2,1)}), bf16[12,16,384]{2,1,0:T(8,128)(2,1)S(1)}, u32[]{:S(2)}, u32[]{:S(2)}) async-start(bf16[12,16,384]{2,1,0:T(8,128)(2,1)} %shard_map.124), calls=%async_computation.1 | async-start | bytes 294912 | tf_op jit(solution)/shard_map/all_to_all | solution.py:404
  101.2 32.7 %collective-permute-start.3 = (bf16[4,12,512]{2,1,0:T(8,128)(2,1)S(1)}, bf16[4,12,512]{2,1,0:T(8,128)(2,1)S(1)}, u32[]{:S(2)}, u32[]{:S(2)}) collective-permute-start(bf16[4,12,512]{2,1,0:T(8,128)(2,1)S(1)} %get-tuple-element.27), channel_id=1, source_target_pairs={{0,24},{1,25},{2,26},{3,27},{4,28},{5,29},{6,30},{7,31},{8,32},{9,... | collective-permute-start | bytes 147464 | tf_op jit(solution)/shard_map/ppermute | solution.py:346
  113.9 20.9 %all-to-all-start.2 = ((f32[4,32,128]{2,1,0:T(8,128)}), f32[4,32,128]{2,1,0:T(8,128)S(1)}, u32[]{:S(2)}, u32[]{:S(2)}) async-start(f32[4,32,128]{2,1,0:T(8,128)} %get-tuple-element.33), calls=%async_computation.2 | async-start | bytes 131072 | tf_op jit(solution)/shard_map/all_to_all | solution.py:408
  117.2 11.4 %collective-permute-start.4 = (bf16[4,4,512]{2,1,0:T(4,128)(2,1)S(1)}, bf16[4,4,512]{2,1,0:T(4,128)(2,1)S(1)}, u32[]{:S(2)}, u32[]{:S(2)}) collective-permute-start(bf16[4,4,512]{2,1,0:T(4,128)(2,1)S(1)} %get-tuple-element.28), channel_id=1, source_target_pairs={{0,1},{1,2},{2,3},{3,4},{4,5},{5,6},{6,7},{7,8},{8,9},{9,10},{10,1... | collective-permute-start | bytes 49160 | tf_op jit(solution)/shard_map/ppermute | solution.py:346
  119.4 14.4 %collective-permute-start.5 = (bf16[4,4,512]{2,1,0:T(4,128)(2,1)S(1)}, bf16[4,4,512]{2,1,0:T(4,128)(2,1)S(1)}, u32[]{:S(2)}, u32[]{:S(2)}) collective-permute-start(bf16[4,4,512]{2,1,0:T(4,128)(2,1)S(1)} %get-tuple-element.29), channel_id=1, source_target_pairs={{0,25},{1,26},{2,27},{3,28},{4,29},{5,30},{6,31},{7,32},{8,33},{9,... | collective-permute-start | bytes 49160 | tf_op jit(solution)/shard_map/ppermute | solution.py:346

commit v2 on v1

--- a/solution.py
+++ b/solution.py
@@ -60,27 +60,41 @@
     return centred * inv_std, inv_std
 
 
-def pack_kernel(tok, cot, reg, to_up, to_left, to_diag):
-    to_up[8] = jnp.zeros((12, D), BF16)
+def pack_kernel(tok, cot, reg, to_up, to_left, to_diag, tok_v, cot_v, reg_v, sem):
+    copies = [
+        pltpu.make_async_copy(src, dst, sem.at[k])
+        for k, (src, dst) in enumerate(((tok, tok_v), (cot, cot_v), (reg, reg_v)))
+    ]
+    for copy in copies:
+        copy.start()
+    to_up[96:112] = jnp.zeros((16, D), BF16)
     to_left[8] = jnp.zeros((4, D), BF16)
     to_diag[8] = jnp.zeros((4, D), BF16)
-    for k, src in ((0, tok), (4, cot)):
+    for copy in copies:
+        copy.wait()
+    for k, src in ((0, tok_v), (4, cot_v)):
+        for r in range(0, SHIFT, 2):
+            first = src[r].astype(F32)
+            second = src[r + 1].astype(F32)
+            at = (k + r) * 12
+            to_up[at : at + 24] = jnp.concatenate([first[4:16], second[4:16]], axis=0).astype(BF16)
         for r in range(SHIFT):
-            top = src[r].astype(F32)
-            low = src[SHIFT + r].astype(F32)
-            to_up[k + r] = top[4:16].astype(BF16)
-            to_diag[k + r] = top[0:4].astype(BF16)
-            to_left[k + r] = low[0:4].astype(BF16)
-    labels = reg[...].astype(F32)
-    to_up[8, 0:4, 0:16] = labels[0:4].astype(BF16)
-    to_diag[8, 0:4, 0:16] = labels[0:4].astype(BF16)
-    to_left[8, 0:4, 0:16] = labels[4:8].astype(BF16)
-
-
-def bias_kernel(table, bucket, bias, bucket2, padded):
-    padded[...] = jnp.zeros_like(padded)
-    padded[0:NBIAS, 0:HEADS] = table[...]
-    turned = padded[...].T
+            to_diag[k + r] = src[r].astype(F32)[0:4].astype(BF16)
+            to_left[k + r] = src[SHIFT + r].astype(F32)[0:4].astype(BF16)
+    classes = reg_v[...].astype(F32)
+    to_up[96:104, 0:16] = classes.astype(BF16)
+    to_diag[8, 0:4, 0:16] = classes[0:4].astype(BF16)
+    to_left[8, 0:4, 0:16] = classes[4:8].astype(BF16)
+
+
+def bias_kernel(table, bucket, wqkv, wout, bias, bucket2, wqkv_out, wout_out, sem):
+    copies = [
+        pltpu.make_async_copy(wqkv, wqkv_out, sem.at[0]),
+        pltpu.make_async_copy(wout, wout_out, sem.at[1]),
+    ]
+    for copy in copies:
+        copy.start()
+    turned = jnp.concatenate([table[...], jnp.zeros((HEADS, 256 - NBIAS), F32)], axis=1)
     both = jnp.concatenate([bucket[...], bucket[...]], axis=1)
     bucket2[...] = both
     for block in range(AREA // 8):
@@ -93,6 +107,8 @@
             got_first = jnp.take_along_axis(first, within, axis=1, mode="promise_in_bounds")
             got_second = jnp.take_along_axis(second, within, axis=1, mode="promise_in_bounds")
             bias[h, block * 8 : block * 8 + 8, :] = jnp.where(upper, got_second, got_first)
+    for copy in copies:
+        copy.wait()
 
 
 def window_kernel(
@@ -100,6 +116,7 @@
     send, keep, own_grad, down_grad, right_grad, diag_grad,
     frame_t, frame_c, labels, packed, attended, grad_att, pairs, grad_in,
 ):
+    up_f = up[...].astype(F32)
     for src, k, frame in ((tok, 0, frame_t), (cot, 4, frame_c)):
         for r in range(SHIFT):
             own = src[SHIFT + r].astype(F32)
@@ -107,7 +124,7 @@
             frame[64 + r * 8 : 64 + r * 8 + 4, :] = own[12:16]
             frame[64 + r * 8 + 4 : 64 + r * 8 + 8, :] = left[k + r].astype(F32)
             s = SHIFT + r
-            below = up[k + r].astype(F32)
+            below = up_f[(k + r) * 12 : (k + r) * 12 + 12]
             frame[s * 8 : s * 8 + 8, :] = below[0:8]
             frame[64 + s * 8 : 64 + s * 8 + 4, :] = below[8:12]
             frame[64 + s * 8 + 4 : 64 + s * 8 + 8, :] = diag[k + r].astype(F32)
@@ -116,7 +133,7 @@
     labels[...] = jnp.zeros_like(labels)
     labels[0:4, 0:12] = mine[4:8, 4:16]
     labels[0:4, 12:16] = left[8, 0:4, 0:16].astype(F32)[:, 0:4]
-    labels[4:8, 0:12] = up[8, 0:4, 0:16].astype(F32)[:, 4:16]
+    labels[4:8, 0:12] = up_f[96:100, 4:16]
     labels[4:8, 12:16] = diag[8, 0:4, 0:16].astype(F32)[:, 0:4]
     row_tile = (lax.axis_index("y") * 2 + lax.axis_index("zh")) * 2 + lax.axis_index("core")
     last = (row_tile == NROWS - 1).astype(F32)
@@ -244,13 +261,12 @@
 
     right = jnp.concatenate([mine[0:TOKENS, 0 : 4 * D], other[0:TOKENS, 0 : 4 * D]], axis=0)
     for half in range(2):
+        at = half * 128
         qkv = dot(rows(half), right[:, 0 : 3 * D]).astype(BF16)
         proj = dot(rows(2 + half), right[:, 3 * D : 4 * D]).astype(BF16)
-        for k in range(4):
-            y = half * 4 + k
-            for x in range(4):
-                out[y, x, :, 0:384] = qkv[k * 32 : k * 32 + 32, x * 384 : x * 384 + 384]
-                out[y, x, :, 384:512] = proj[k * 32 : k * 32 + 32, x * 128 : x * 128 + 128]
+        for x in range(4):
+            out[x, at : at + 128, 0:384] = qkv[:, x * 384 : x * 384 + 384]
+            out[x, at : at + 128, 384:512] = proj[:, x * 128 : x * 128 + 128]
     small = mine[TOKENS : TOKENS + 16, 0:1536].astype(F32) + other[TOKENS : TOKENS + 16, 0:1536].astype(F32)
     table = small[:, 0:256] + small[:, 256:512]
     gain = small[0:8, 512:1024] + small[0:8, 1024:1536]
@@ -264,9 +280,19 @@
             axis=0,
         )
         high, low = split_high_low(part)
-        both = jnp.concatenate([high, low], axis=0)
-        for y in range(8):
-            out[y, x, :, 512:640] = both
+        out[x, 256:272, 0:128] = high
+        out[x, 256:272, 128:256] = low
+        out[x, 256:272, 256:512] = jnp.zeros((16, 256), BF16)
+
+
+def across_sum_kernel(parts, out):
+    small = jnp.sum(parts[:, 256:272, 0:256].astype(F32), axis=0)
+    high, low = split_high_low(small[:, 0:128] + small[:, 128:256])
+    both = jnp.concatenate([high, low], axis=0)
+    for y in range(8):
+        total = jnp.sum(parts[:, y * 32 : y * 32 + 32, :].astype(F32), axis=0)
+        out[y, :, 0:512] = total.astype(BF16)
+        out[y, :, 512:640] = both
 
 
 def plane_sum_kernel(parts, out):
@@ -300,11 +326,8 @@
         gain[:, x * 128 : x * 128 + 128] = parts[x, 24:25, :]
         low.append(parts[x, 16:20, :])
         high.append(parts[x, 20:24, :])
-    pad = jnp.zeros((112, 128), F32)
-    low = jnp.concatenate(low + [pad], axis=0)
-    high = jnp.concatenate(high + [pad], axis=0)
-    table[0:128, :] = low.T[:, 0:HEADS]
-    table[128:NBIAS, :] = high.T[0 : NBIAS - 128, 0:HEADS]
+    table[:, 0:128] = jnp.concatenate(low, axis=0)
+    table[:, 128:NBIAS] = jnp.concatenate(high, axis=0)[:, 0 : NBIAS - 128]
 
 
 def token_kernel(tok, cot, gain, own, above, left, diag, out, grads):
@@ -327,12 +350,16 @@
     return jax.ShapeDtypeStruct(dims, dtype)
 
 
-def call(kernel, outs, args, scratch=(), flops=0, moved=0):
+def call(kernel, outs, args, scratch=(), flops=0, moved=0, remain=(), params=ANY_PARAMS):
     return pl.pallas_call(
         kernel,
+        in_specs=[
+            pl.BlockSpec(memory_space=pltpu.HBM if k in remain else pltpu.VMEM)
+            for k in range(len(args))
+        ],
         out_shape=outs,
         scratch_shapes=list(scratch),
-        compiler_params=ANY_PARAMS,
+        compiler_params=params,
         cost_estimate=pl.CostEstimate(flops=flops, bytes_accessed=moved, transcendentals=0),
     )(*args)
 
@@ -350,19 +377,33 @@
     gain = norm_gain.reshape(1, D)
     to_up, to_left, to_diag = call(
         pack_kernel,
-        [shape((9, 12, D), BF16), shape((9, 4, D), BF16), shape((9, 4, D), BF16)],
+        [shape((112, D), BF16), shape((9, 4, D), BF16), shape((9, 4, D), BF16)],
         (tokens, cotangent, region),
+        [
+            pltpu.VMEM((8, 16, D), BF16),
+            pltpu.VMEM((8, 16, D), BF16),
+            pltpu.VMEM((8, 16), jnp.int32),
+            pltpu.SemaphoreType.DMA((3,)),
+        ],
         moved=1 << 19,
+        remain=(0, 1, 2),
+        params=pltpu.CompilerParams(),
     )
     up = neighbour(to_up, -1, 0)
     diag = neighbour(to_diag, -1, -1)
     left = neighbour(to_left, 0, -1)
-    bias, bucket2 = call(
+    bias, bucket2, wqkv, wout = call(
         bias_kernel,
-        [shape((HEADS, AREA, 128), F32), shape((AREA, 128), jnp.int32)],
-        (bias_table, bias_bucket),
-        [pltpu.VMEM((256, 128), F32)],
+        [
+            shape((HEADS, AREA, 128), F32),
+            shape((AREA, 128), jnp.int32),
+            shape((D, 3 * D), BF16),
+            shape((D, D), BF16),
+        ],
+        (bias_table.T, bias_bucket, qkv_weight, out_weight),
+        [pltpu.SemaphoreType.DMA((2,))],
         moved=1 << 23,
+        remain=(2, 3),
     )
     send, keep, own_grad, down_grad, right_grad, diag_grad = call(
         window_kernel,
@@ -374,7 +415,7 @@
             shape((4, 4, D), BF16),
             shape((4, 4, D), BF16),
         ],
-        (tokens, cotangent, region, up, left, diag, gain, qkv_weight, out_weight, bias, bucket2),
+        (tokens, cotangent, region, up, left, diag, gain, wqkv, wout, bias, bucket2),
         [
             pltpu.VMEM((TOKENS, D), F32),
             pltpu.VMEM((TOKENS, D), F32),
@@ -389,29 +430,31 @@
         moved=1 << 23,
     )
     other = lax.ppermute(send, "core", [(0, 1), (1, 0)])
+    products = call(
+        product_kernel,
+        shape((4, 272, D), BF16),
+        (send, other, keep),
+        flops=1 << 29,
+        moved=1 << 21,
+    )
+    across = lax.all_to_all(products, "x", 0, 0)
+    halves = call(across_sum_kernel, shape((8, 32, 640), BF16), (across,), moved=1 << 21)
+    planes = lax.all_to_all(halves, "y", 0, 0)
+    chunks = call(plane_sum_kernel, shape((12, 16, 384), BF16), (planes,), moved=1 << 21)
+    chunks, down_grad, right_grad, diag_grad = lax.optimization_barrier(
+        (chunks, down_grad, right_grad, diag_grad)
+    )
+    lines = lax.all_to_all(chunks, ("zh", "zl"), 0, 0)
     above_grad = neighbour(down_grad, 1, 0)
     left_grad = neighbour(right_grad, 0, 1)
     corner_grad = neighbour(diag_grad, 1, 1)
-    products = call(
-        product_kernel,
-        shape((8, 4, 32, 640), BF16),
-        (send, other, keep),
-        flops=1 << 29,
-        moved=1 << 21,
-    )
-    planes = lax.all_to_all(products.reshape(32, 32, 640), ("y", "x"), 0, 0)
-    chunks = call(plane_sum_kernel, shape((12, 16, 384), BF16), (planes,), moved=1 << 21)
-    lines = lax.all_to_all(chunks, ("zh", "zl"), 0, 0)
     grad_qkv, finals = call(
         line_sum_kernel, [shape((16, 64), F32), shape((4, 32, 128), F32)], (lines,), moved=1 << 18
     )
+    finals, above_grad, left_grad, corner_grad = lax.optimization_barrier(
+        (finals, above_grad, left_grad, corner_grad)
+    )
     finals = lax.all_to_all(finals, "x", 0, 0)
-    grad_out_weight, grad_gain, grad_bias_table = call(
-        finish_kernel,
-        [shape((16, D), F32), shape((1, D), F32), shape((NBIAS, HEADS), F32)],
-        (finals,),
-        moved=1 << 17,
-    )
     grad_tokens = call(
         token_kernel,
         shape((8, 16, D), BF16),
@@ -419,7 +462,13 @@
         [pltpu.VMEM((8, 16, D), F32)],
         moved=1 << 20,
     )
-    return (grad_tokens, grad_qkv, grad_out_weight, grad_gain.reshape(D), grad_bias_table)
+    grad_out_weight, grad_gain, grad_bias_table = call(
+        finish_kernel,
+        [shape((16, D), F32), shape((1, D), F32), shape((HEADS, NBIAS), F32)],
+        (finals,),
+        moved=1 << 17,
+    )
+    return (grad_tokens, grad_qkv, grad_out_weight, grad_gain.reshape(D), grad_bias_table.T)
 
 
 def solution(mesh):

time: 137 us -> 125 us (0.912)
  blocking collectives: 41.5 us -> 33.1 us
  local copies, waits for them, and re-layouts: 10.4 us -> 3.94 us
  waiting for transfers between devices: 9.2 us -> 15.1 us
  starting transfers between devices: 63.7 us -> 59.2 us
  Pallas kernels: 10.5 us -> 12.3 us
    all_to_all x1 -> x2, blocking collectives: 41.5 us -> 33.1 us  [the longest x1 18.2 us: local(): across = lax.all_to_all(products, 'x', 0, 0)]
    unnamed x28 -> x16, local copies, waits for them, and re-layouts: 10.4 us -> 3.94 us
    ppermute x6, starting transfers between devices: 52.2 us -> 48.1 us  [neighbour(): return lax.ppermute(value, ROWS + COLS, pairs)]
    all_to_all x1, waiting for transfers between devices: 0.01 us -> 3.48 us  [local(): finals = lax.all_to_all(finals, 'x', 0, 0)]
    ppermute x6, waiting for transfers between devices: 7.38 us -> 9.4 us  [neighbour(): return lax.ppermute(value, ROWS + COLS, pairs)]
    pallas_call x8 -> x9, Pallas kernels: 10.5 us -> 12.3 us  [call(): pl.pallas_call(kernel, in_specs=[pl.BlockSpec(memory_space=pltpu.HBM if k...]
  transfers between devices with their start and end apart: 9 -> 9, of which waited for: 3 -> 4; matrix products, arithmetic and copies ran while one was open for 1% -> 0% of each run, Pallas kernels for 2% -> 2%
where the time goes in v2:
time: 125 us; the launch traced here: 124 us
  starting transfers between devices  59.2 us (47%)
  blocking collectives  33.1 us (26%)
  waiting for transfers between devices  15.1 us (12%)
  Pallas kernels  12.3 us (10%)
  local copies, waits for them, and re-layouts  3.94 us (3%)
    ppermute x6, starting transfers between devices, neighbour(): return lax.ppermute(value, ROWS + COLS, pairs)  48.1 us
    all_to_all x1, blocking collectives, local(): across = lax.all_to_all(products, 'x', 0, 0)  18.2 us
    all_to_all x1, blocking collectives, local(): planes = lax.all_to_all(halves, 'y', 0, 0)  14.9 us
    pallas_call x9, Pallas kernels, call(): pl.pallas_call(kernel, in_specs=[pl.BlockSpec(memory_space=pltpu.HBM if k...  12.3 us
    ppermute x6, waiting for transfers between devices, neighbour(): return lax.ppermute(value, ROWS + COLS, pairs)  9.4 us
    all_to_all x1, starting transfers between devices, local(): lines = lax.all_to_all(chunks, ('zh', 'zl'), 0, 0)  5.85 us
    unnamed x16, local copies, waits for them, and re-layouts  3.94 us
    all_to_all x1, waiting for transfers between devices, local(): finals = lax.all_to_all(finals, 'x', 0, 0)  3.48 us
  transfers between devices with their start and end apart: 9, of which 4 were waited for; matrix products, arithmetic and copies ran while one was open for 0% of the time, Pallas kernels for 2%

profile of v2, /device:TPU:1, one launch (start us, length us, event | category | flops | bytes accessed | tf_op | source)
XLA Modules:
  0.0 124.4 jit_solution(15339052731794532754)
XLA Ops:
  0.6 0.0 copy-start.2
  0.6 0.0 copy-start.1
  0.7 0.0 copy-start.6
  0.7 0.0 copy-start.7
  0.7 1.7 %shard_map.119 = (bf16[112,512]{1,0:T(8,128)(2,1)}, bf16[9,4,512]{2,1,0:T(4,128)(2,1)}, bf16[9,4,512]{2,1,0:T(4,128)(2,1)}) custom-call(bf16[8,16,512]{2,1,0:T(8,128)(2,1)} %tok.5, bf16[8,16,512]{2,1,0:T(8,128)(2,1)} %cot.5, s32[8,16]{1,0:T(8,128)} %reg.3), custom_call_target="tpu_custom_call" | custom-call | bytes 524288 | tf_op jit(solution)/shard_map/pallas_call | solution.py:354
  2.4 12.4 %collective-permute-start = (bf16[112,512]{1,0:T(8,128)(2,1)}, bf16[112,512]{1,0:T(8,128)(2,1)S(1)}, u32[]{:S(2)}, u32[]{:S(2)}) collective-permute-start(bf16[112,512]{1,0:T(8,128)(2,1)} %get-tuple-element.31), channel_id=1, source_target_pairs={{0,744},{1,745},{2,746},{3,747},{4,748},{5,749},{6,750},{7,751},{8... | collective-permute-start | bytes 344072 | tf_op jit(solution)/shard_map/ppermute | solution.py:373
  14.8 5.6 %collective-permute-start.1 = (bf16[9,4,512]{2,1,0:T(4,128)(2,1)}, bf16[9,4,512]{2,1,0:T(4,128)(2,1)S(1)}, u32[]{:S(2)}, u32[]{:S(2)}) collective-permute-start(bf16[9,4,512]{2,1,0:T(4,128)(2,1)} %get-tuple-element.32), channel_id=1, source_target_pairs={{0,23},{1,0},{2,1},{3,2},{4,3},{5,4},{6,5},{7,6},{8,7},{9,8},{10,9... | collective-permute-start | bytes 110600 | tf_op jit(solution)/shard_map/ppermute | solution.py:373
  20.5 12.8 %collective-permute-start.2 = (bf16[9,4,512]{2,1,0:T(4,128)(2,1)}, bf16[9,4,512]{2,1,0:T(4,128)(2,1)S(1)}, u32[]{:S(2)}, u32[]{:S(2)}) collective-permute-start(bf16[9,4,512]{2,1,0:T(4,128)(2,1)} %get-tuple-element.33), channel_id=1, source_target_pairs={{0,767},{1,744},{2,745},{3,746},{4,747},{5,748},{6,749},{7,750},{8... | collective-permute-start | bytes 110600 | tf_op jit(solution)/shard_map/ppermute | solution.py:373
  33.3 0.0 copy-start
  33.3 1.4 %copy-done = bf16[512,1536]{1,0:T(8,128)(2,1)S(1)} copy-done((bf16[512,1536]{1,0:T(8,128)(2,1)S(1)}, bf16[512,1536]{1,0:T(8,128)(2,1)}, u32[]{:S(2)}) %copy-start) | copy-done | bytes 1572888
  34.7 0.0 copy-start.3
  34.7 1.0 copy-done.3
  35.8 0.0 copy-start.4
  35.8 0.8 copy-done.4
  36.5 0.0 copy-start.5
  36.5 0.7 copy-done.5
  37.2 0.6 shard_map.120
  37.8 0.0 collective-permute-done.1.left
  37.9 0.0 collective-permute-done.2.diag
  37.9 0.0 collective-permute-done.up
  37.9 0.0 copy-done.2
  37.9 0.0 copy-done.1
  37.9 0.0 copy-done.6
  37.9 0.0 copy-done.7
  37.9 6.4 %shard_map.121 = (bf16[144,2560]{1,0:T(8,128)(2,1)S(1)}, bf16[128,512]{1,0:T(8,128)(2,1)S(1)}, f32[4,12,512]{2,1,0:T(8,128)S(1)}, bf16[4,12,512]{2,1,0:T(8,128)(...) custom-call(bf16[8,16,512]{2,1,0:T(8,128)(2,1)S(1)} %copy-done.1, ...), custom_call_target="tpu_custom_call" | custom-call | flops 1073741824 | bytes 8388608 | tf_op jit(solution)/shard_map/pallas_call | solution.py:354
  44.3 1.9 %collective-permute-start.3 = (bf16[144,2560]{1,0:T(8,128)(2,1)S(1)}, bf16[144,2560]{1,0:T(8,128)(2,1)S(1)}, u32[]{:S(2)}, u32[]{:S(2)}) collective-permute-start(bf16[144,2560]{1,0:T(8,128)(2,1)S(1)} %get-tuple-element.39.mine), channel_id=1, source_target_pairs={{0,24},{24,0},{1,25},{25,1},{2,26},{26,2},{3,27},{27,3},{4,28},{28... | collective-permute-start | bytes 2211848 | tf_op jit(solution)/shard_map/ppermute | solution.py:432
  46.2 2.2 %collective-permute-done.3.other = bf16[144,2560]{1,0:T(8,128)(2,1)S(1)} collective-permute-done((bf16[144,2560]{1,0:T(8,128)(2,1)S(1)}, bf16[144,2560]{1,0:T(8,128)(2,1)S(1)}, u32[]{:S(2)}, u32[]{:S(2)}) %collective-permute-start.3) | collective-permute-done | bytes 737312 | tf_op jit(solution)/shard_map/ppermute | solution.py:432
  48.4 0.4 shard_map.122
  48.8 18.2 %all_to_all.20.parts = bf16[4,272,512]{2,1,0:T(8,128)(2,1)S(1)} all-to-all(bf16[4,272,512]{2,1,0:T(8,128)(2,1)S(1)} %shard_map.122), channel_id=1, replica_groups=mesh['y'=8,'zh'=2,'core'=2,'x'=4,'zl'=6] {'x'}, dimensions={0} | all-to-all | bytes 2228224 | tf_op jit(solution)/shard_map/all_to_all | solution.py:440
  67.0 0.1 shard_map.123
  67.2 14.9 %all_to_all.21.parts = bf16[8,32,640]{2,1,0:T(8,128)(2,1)S(1)} all-to-all(bf16[8,32,640]{2,1,0:T(8,128)(2,1)S(1)} %shard_map.123), channel_id=1, replica_groups=mesh['y'=8,'zh'=2,'core'=2,'x'=4,'zl'=6] {'y'}, dimensions={0} | all-to-all | bytes 655360 | tf_op jit(solution)/shard_map/all_to_all | solution.py:442
  82.1 0.8 shard_map.124
  82.8 5.8 %all-to-all-start.2 = ((bf16[12,16,384]{2,1,0:T(8,128)(2,1)}), bf16[12,16,384]{2,1,0:T(8,128)(2,1)S(1)}, u32[]{:S(2)}, u32[]{:S(2)}) async-start(bf16[12,16,384]{2,1,0:T(8,128)(2,1)} %shard_map.124), calls=%async_computation.2 | async-start | bytes 294912 | tf_op jit(solution)/shard_map/all_to_all | solution.py:447
  88.7 13.1 %collective-permute-start.4 = (bf16[4,12,512]{2,1,0:T(8,128)(2,1)S(1)}, bf16[4,12,512]{2,1,0:T(8,128)(2,1)S(1)}, u32[]{:S(2)}, u32[]{:S(2)}) collective-permute-start(bf16[4,12,512]{2,1,0:T(8,128)(2,1)S(1)} %get-tuple-element.46), channel_id=1, source_target_pairs={{0,24},{1,25},{2,26},{3,27},{4,28},{5,29},{6,30},{7,31},{8,32},{9,... | collective-permute-start | bytes 147464 | tf_op jit(solution)/shard_map/ppermute | solution.py:373
  101.9 2.2 %collective-permute-start.5 = (bf16[4,4,512]{2,1,0:T(4,128)(2,1)S(1)}, bf16[4,4,512]{2,1,0:T(4,128)(2,1)S(1)}, u32[]{:S(2)}, u32[]{:S(2)}) collective-permute-start(bf16[4,4,512]{2,1,0:T(4,128)(2,1)S(1)} %get-tuple-element.47), channel_id=1, source_target_pairs={{0,1},{1,2},{2,3},{3,4},{4,5},{5,6},{6,7},{7,8},{8,9},{9,10},{10,1... | collective-permute-start | bytes 49160 | tf_op jit(solution)/shard_map/ppermute | solution.py:373
  104.1 1.9 %collective-permute-start.6 = (bf16[4,4,512]{2,1,0:T(4,128)(2,1)S(1)}, bf16[4,4,512]{2,1,0:T(4,128)(2,1)S(1)}, u32[]{:S(2)}, u32[]{:S(2)}) collective-permute-start(bf16[4,4,512]{2,1,0:T(4,128)(2,1)S(1)} %get-tuple-element.48), channel_id=1, source_target_pairs={{0,25},{1,26},{2,27},{3,28},{4,29},{5,30},{6,31},{7,32},{8,33},{9,... | collective-permute-start | bytes 49160 | tf_op jit(solution)/shard_map/ppermute | solution.py:373
  106.0 0.0 all-to-all-done.2.parts
  106.0 0.6 shard_map.125
  106.6 6.6 %collective-permute-done.5.left = bf16[4,4,512]{2,1,0:T(4,128)(2,1)S(1)} collective-permute-done((bf16[4,4,512]{2,1,0:T(4,128)(2,1)S(1)}, bf16[4,4,512]{2,1,0:T(4,128)(2,1)S(1)}, u32[]{:S(2)}, u32[]{:S(2)}) %collective-permute-start.5) | collective-permute-done | bytes 16416 | tf_op jit(solution)/shard_map/ppermute | solution.py:373
  113.3 2.8 %collective-permute-done.6.diag = bf16[4,4,512]{2,1,0:T(4,128)(2,1)S(1)} collective-permute-done((bf16[4,4,512]{2,1,0:T(4,128)(2,1)S(1)}, bf16[4,4,512]{2,1,0:T(4,128)(2,1)S(1)}, u32[]{:S(2)}, u32[]{:S(2)}) %collective-permute-start.6) | collective-permute-done | bytes 16416 | tf_op jit(solution)/shard_map/ppermute | solution.py:373
  116.0 0.0 collective-permute-done.4.above
  116.0 3.3 %all-to-all-start.3 = ((f32[4,32,128]{2,1,0:T(8,128)}), f32[4,32,128]{2,1,0:T(8,128)S(1)}, u32[]{:S(2)}, u32[]{:S(2)}) async-start(f32[4,32,128]{2,1,0:T(8,128)} %get-tuple-element.53), calls=%async_computation.3 | async-start | bytes 131072 | tf_op jit(solution)/shard_map/all_to_all | solution.py:457
  119.3 1.0 shard_map.126
  120.3 3.5 %all-to-all-done.3.parts = f32[4,32,128]{2,1,0:T(8,128)S(1)} async-done(((f32[4,32,128]{2,1,0:T(8,128)}), f32[4,32,128]{2,1,0:T(8,128)S(1)}, u32[]{:S(2)}, u32[]{:S(2)}) %all-to-all-start.3) | async-done | bytes 65568 | tf_op jit(solution)/shard_map/all_to_all | solution.py:457
  123.8 0.6 shard_map.127
Async XLA Ops:
  0.6 37.2 %copy-start.2 = (bf16[8,16,512]{2,1,0:T(8,128)(2,1)S(1)}, bf16[8,16,512]{2,1,0:T(8,128)(2,1)}, u32[]{:S(2)}) copy-start(bf16[8,16,512]{2,1,0:T(8,128)(2,1)} %cot.5) | copy-start | bytes 393220
  0.6 37.2 %copy-start.1 = (bf16[8,16,512]{2,1,0:T(8,128)(2,1)S(1)}, bf16[8,16,512]{2,1,0:T(8,128)(2,1)}, u32[]{:S(2)}) copy-start(bf16[8,16,512]{2,1,0:T(8,128)(2,1)} %tok.5) | copy-start | bytes 393220
  0.7 37.2 %copy-start.6 = (s32[8,16]{1,0:T(8,128)S(1)}, s32[8,16]{1,0:T(8,128)}, u32[]{:S(2)}) copy-start(s32[8,16]{1,0:T(8,128)} %reg.3) | copy-start | bytes 1540
  0.7 37.2 %copy-start.7 = (f32[512]{0:T(512)S(1)}, f32[512]{0:T(512)}, u32[]{:S(2)}) copy-start(f32[512]{0:T(512)} %param.11) | copy-start | bytes 6148
  2.4 35.4 %collective-permute-start = (bf16[112,512]{1,0:T(8,128)(2,1)}, bf16[112,512]{1,0:T(8,128)(2,1)S(1)}, u32[]{:S(2)}, u32[]{:S(2)}) collective-permute-start(bf16[112,512]{1,0:T(8,128)(2,1)} %get-tuple-element.31), channel_id=1, source_target_pairs={{0,744},{1,745},{2,746},{3,747},{4,748},{5,749},{6,750},{7,751},{8... | collective-permute-start | bytes 344072 | tf_op jit(solution)/shard_map/ppermute | solution.py:373
  14.8 23.0 %collective-permute-start.1 = (bf16[9,4,512]{2,1,0:T(4,128)(2,1)}, bf16[9,4,512]{2,1,0:T(4,128)(2,1)S(1)}, u32[]{:S(2)}, u32[]{:S(2)}) collective-permute-start(bf16[9,4,512]{2,1,0:T(4,128)(2,1)} %get-tuple-element.32), channel_id=1, source_target_pairs={{0,23},{1,0},{2,1},{3,2},{4,3},{5,4},{6,5},{7,6},{8,7},{9,8},{10,9... | collective-permute-start | bytes 110600 | tf_op jit(solution)/shard_map/ppermute | solution.py:373
  20.5 17.4 %collective-permute-start.2 = (bf16[9,4,512]{2,1,0:T(4,128)(2,1)}, bf16[9,4,512]{2,1,0:T(4,128)(2,1)S(1)}, u32[]{:S(2)}, u32[]{:S(2)}) collective-permute-start(bf16[9,4,512]{2,1,0:T(4,128)(2,1)} %get-tuple-element.33), channel_id=1, source_target_pairs={{0,767},{1,744},{2,745},{3,746},{4,747},{5,748},{6,749},{7,750},{8... | collective-permute-start | bytes 110600 | tf_op jit(solution)/shard_map/ppermute | solution.py:373
  33.3 1.4 %copy-start = (bf16[512,1536]{1,0:T(8,128)(2,1)S(1)}, bf16[512,1536]{1,0:T(8,128)(2,1)}, u32[]{:S(2)}) copy-start(bf16[512,1536]{1,0:T(8,128)(2,1)} %wqkv.1) | copy-start | bytes 4718596
  34.7 1.0 copy-start.3
  35.8 0.8 copy-start.4
  36.5 0.7 copy-start.5
  44.3 4.1 %collective-permute-start.3 = (bf16[144,2560]{1,0:T(8,128)(2,1)S(1)}, bf16[144,2560]{1,0:T(8,128)(2,1)S(1)}, u32[]{:S(2)}, u32[]{:S(2)}) collective-permute-start(bf16[144,2560]{1,0:T(8,128)(2,1)S(1)} %get-tuple-element.39.mine), channel_id=1, source_target_pairs={{0,24},{24,0},{1,25},{25,1},{2,26},{26,2},{3,27},{27,3},{4,28},{28... | collective-permute-start | bytes 2211848 | tf_op jit(solution)/shard_map/ppermute | solution.py:432
  82.8 23.1 %all-to-all-start.2 = ((bf16[12,16,384]{2,1,0:T(8,128)(2,1)}), bf16[12,16,384]{2,1,0:T(8,128)(2,1)S(1)}, u32[]{:S(2)}, u32[]{:S(2)}) async-start(bf16[12,16,384]{2,1,0:T(8,128)(2,1)} %shard_map.124), calls=%async_computation.2 | async-start | bytes 294912 | tf_op jit(solution)/shard_map/all_to_all | solution.py:447
  88.7 27.3 %collective-permute-start.4 = (bf16[4,12,512]{2,1,0:T(8,128)(2,1)S(1)}, bf16[4,12,512]{2,1,0:T(8,128)(2,1)S(1)}, u32[]{:S(2)}, u32[]{:S(2)}) collective-permute-start(bf16[4,12,512]{2,1,0:T(8,128)(2,1)S(1)} %get-tuple-element.46), channel_id=1, source_target_pairs={{0,24},{1,25},{2,26},{3,27},{4,28},{5,29},{6,30},{7,31},{8,32},{9,... | collective-permute-start | bytes 147464 | tf_op jit(solution)/shard_map/ppermute | solution.py:373
  101.9 11.4 %collective-permute-start.5 = (bf16[4,4,512]{2,1,0:T(4,128)(2,1)S(1)}, bf16[4,4,512]{2,1,0:T(4,128)(2,1)S(1)}, u32[]{:S(2)}, u32[]{:S(2)}) collective-permute-start(bf16[4,4,512]{2,1,0:T(4,128)(2,1)S(1)} %get-tuple-element.47), channel_id=1, source_target_pairs={{0,1},{1,2},{2,3},{3,4},{4,5},{5,6},{6,7},{7,8},{8,9},{9,10},{10,1... | collective-permute-start | bytes 49160 | tf_op jit(solution)/shard_map/ppermute | solution.py:373
  104.1 12.0 %collective-permute-start.6 = (bf16[4,4,512]{2,1,0:T(4,128)(2,1)S(1)}, bf16[4,4,512]{2,1,0:T(4,128)(2,1)S(1)}, u32[]{:S(2)}, u32[]{:S(2)}) collective-permute-start(bf16[4,4,512]{2,1,0:T(4,128)(2,1)S(1)} %get-tuple-element.48), channel_id=1, source_target_pairs={{0,25},{1,26},{2,27},{3,28},{4,29},{5,30},{6,31},{7,32},{8,33},{9,... | collective-permute-start | bytes 49160 | tf_op jit(solution)/shard_map/ppermute | solution.py:373
  116.0 7.7 %all-to-all-start.3 = ((f32[4,32,128]{2,1,0:T(8,128)}), f32[4,32,128]{2,1,0:T(8,128)S(1)}, u32[]{:S(2)}, u32[]{:S(2)}) async-start(f32[4,32,128]{2,1,0:T(8,128)} %get-tuple-element.53), calls=%async_computation.3 | async-start | bytes 131072 | tf_op jit(solution)/shard_map/all_to_all | solution.py:457

commit v3 on v2

--- a/solution.py
+++ b/solution.py
@@ -87,13 +87,15 @@
     to_left[8, 0:4, 0:16] = classes[4:8].astype(BF16)
 
 
-def bias_kernel(table, bucket, wqkv, wout, bias, bucket2, wqkv_out, wout_out, sem):
+def bias_kernel(table_far, bucket_far, bias, bucket2, table, bucket, sem):
     copies = [
-        pltpu.make_async_copy(wqkv, wqkv_out, sem.at[0]),
-        pltpu.make_async_copy(wout, wout_out, sem.at[1]),
+        pltpu.make_async_copy(table_far, table, sem.at[0]),
+        pltpu.make_async_copy(bucket_far, bucket, sem.at[1]),
     ]
     for copy in copies:
         copy.start()
+    for copy in copies:
+        copy.wait()
     turned = jnp.concatenate([table[...], jnp.zeros((HEADS, 256 - NBIAS), F32)], axis=1)
     both = jnp.concatenate([bucket[...], bucket[...]], axis=1)
     bucket2[...] = both
@@ -107,15 +109,24 @@
             got_first = jnp.take_along_axis(first, within, axis=1, mode="promise_in_bounds")
             got_second = jnp.take_along_axis(second, within, axis=1, mode="promise_in_bounds")
             bias[h, block * 8 : block * 8 + 8, :] = jnp.where(upper, got_second, got_first)
-    for copy in copies:
-        copy.wait()
 
 
 def window_kernel(
-    tok, cot, reg, up, left, diag, gain, wqkv, wout, bias, bucket2,
+    tok_far, cot_far, reg_far, wqkv_far, wout_far, gain_far, bias, bucket2, up, left, diag,
     send, keep, own_grad, down_grad, right_grad, diag_grad,
     frame_t, frame_c, labels, packed, attended, grad_att, pairs, grad_in,
+    tok, cot, reg, wqkv, wout, gain, sem,
 ):
+    moves = (
+        (tok_far, tok), (cot_far, cot), (reg_far, reg), (wqkv_far, wqkv),
+        (wout_far, wout), (gain_far, gain),
+    )
+    copies = [pltpu.make_async_copy(src, dst, sem.at[k]) for k, (src, dst) in enumerate(moves)]
+    for copy in copies:
+        copy.start()
+    for copy in copies[0:3]:
+        copy.wait()
+
     up_f = up[...].astype(F32)
     for src, k, frame in ((tok, 0, frame_t), (cot, 4, frame_c)):
         for r in range(SHIFT):
@@ -163,8 +174,11 @@
     allowed4 = jnp.concatenate([allowed.astype(F32)] * GROUP, axis=0) > 0.5
 
     hat, _ = layer_stats(frame_t[...])
+    copies[5].wait()
     normed = (hat * gain[...]).astype(BF16)
     cots = frame_c[...].astype(BF16)
+    for copy in copies[3:5]:
+        copy.wait()
     packed[...] = dot(normed, wqkv[...]).astype(BF16)
     grad_att[...] = dot_nt(cots, wout[...]).astype(BF16)
     send[0:TOKENS, 3 * D : 4 * D] = cots
@@ -351,6 +365,10 @@
 
 
 def call(kernel, outs, args, scratch=(), flops=0, moved=0, remain=(), params=ANY_PARAMS):
+    args = [
+        pltpu.with_memory_space_constraint(arg, pltpu.HBM) if k in remain else arg
+        for k, arg in enumerate(args)
+    ]
     return pl.pallas_call(
         kernel,
         in_specs=[
@@ -387,23 +405,24 @@
         ],
         moved=1 << 19,
         remain=(0, 1, 2),
-        params=pltpu.CompilerParams(),
     )
     up = neighbour(to_up, -1, 0)
     diag = neighbour(to_diag, -1, -1)
     left = neighbour(to_left, 0, -1)
-    bias, bucket2, wqkv, wout = call(
+    bias, bucket2 = call(
         bias_kernel,
         [
             shape((HEADS, AREA, 128), F32),
             shape((AREA, 128), jnp.int32),
-            shape((D, 3 * D), BF16),
-            shape((D, D), BF16),
         ],
-        (bias_table.T, bias_bucket, qkv_weight, out_weight),
-        [pltpu.SemaphoreType.DMA((2,))],
+        (bias_table.T, bias_bucket),
+        [
+            pltpu.VMEM((HEADS, NBIAS), F32),
+            pltpu.VMEM((AREA, AREA), jnp.int32),
+            pltpu.SemaphoreType.DMA((2,)),
+        ],
         moved=1 << 23,
-        remain=(2, 3),
+        remain=(0, 1),
     )
     send, keep, own_grad, down_grad, right_grad, diag_grad = call(
         window_kernel,
@@ -415,7 +434,7 @@
             shape((4, 4, D), BF16),
             shape((4, 4, D), BF16),
         ],
-        (tokens, cotangent, region, up, left, diag, gain, wqkv, wout, bias, bucket2),
+        (tokens, cotangent, region, qkv_weight, out_weight, gain, bias, bucket2, up, left, diag),
         [
             pltpu.VMEM((TOKENS, D), F32),
             pltpu.VMEM((TOKENS, D), F32),
@@ -425,9 +444,17 @@
             pltpu.VMEM((TOKENS, D), BF16),
             pltpu.VMEM((HEADS, AREA, 128), F32),
             pltpu.VMEM((TOKENS, D), F32),
+            pltpu.VMEM((8, 16, D), BF16),
+            pltpu.VMEM((8, 16, D), BF16),
+            pltpu.VMEM((8, 16), jnp.int32),
+            pltpu.VMEM((D, 3 * D), BF16),
+            pltpu.VMEM((D, D), BF16),
+            pltpu.VMEM((1, D), F32),
+            pltpu.SemaphoreType.DMA((6,)),
         ],
         flops=1 << 30,
         moved=1 << 23,
+        remain=tuple(range(6)),
     )
     other = lax.ppermute(send, "core", [(0, 1), (1, 0)])
     products = call(
@@ -437,22 +464,22 @@
         flops=1 << 29,
         moved=1 << 21,
     )
+    products, down_grad, right_grad, diag_grad = lax.optimization_barrier(
+        (products, down_grad, right_grad, diag_grad)
+    )
     across = lax.all_to_all(products, "x", 0, 0)
-    halves = call(across_sum_kernel, shape((8, 32, 640), BF16), (across,), moved=1 << 21)
-    planes = lax.all_to_all(halves, "y", 0, 0)
-    chunks = call(plane_sum_kernel, shape((12, 16, 384), BF16), (planes,), moved=1 << 21)
-    chunks, down_grad, right_grad, diag_grad = lax.optimization_barrier(
-        (chunks, down_grad, right_grad, diag_grad)
-    )
-    lines = lax.all_to_all(chunks, ("zh", "zl"), 0, 0)
     above_grad = neighbour(down_grad, 1, 0)
     left_grad = neighbour(right_grad, 0, 1)
     corner_grad = neighbour(diag_grad, 1, 1)
+    halves = call(across_sum_kernel, shape((8, 32, 640), BF16), (across,), moved=1 << 21)
+    halves, above_grad, left_grad, corner_grad = lax.optimization_barrier(
+        (halves, above_grad, left_grad, corner_grad)
+    )
+    planes = lax.all_to_all(halves, "y", 0, 0)
+    chunks = call(plane_sum_kernel, shape((12, 16, 384), BF16), (planes,), moved=1 << 21)
+    lines = lax.all_to_all(chunks, ("zh", "zl"), 0, 0)
     grad_qkv, finals = call(
         line_sum_kernel, [shape((16, 64), F32), shape((4, 32, 128), F32)], (lines,), moved=1 << 18
-    )
-    finals, above_grad, left_grad, corner_grad = lax.optimization_barrier(
-        (finals, above_grad, left_grad, corner_grad)
     )
     finals = lax.all_to_all(finals, "x", 0, 0)
     grad_tokens = call(

time: 125 us -> 118 us (0.944); the launches traced: 124 us -> 116 us
  starting transfers between devices: 59.2 us -> 50.5 us
  local copies, waits for them, and re-layouts: 3.94 us -> 0.02 us
  blocking collectives: 33.1 us -> 35.3 us
  Pallas kernels: 12.3 us -> 14.1 us
    ppermute x6, starting transfers between devices: 48.1 us -> 40.4 us  [neighbour(): return lax.ppermute(value, ROWS + COLS, pairs)]
    all_to_all x1, waiting for transfers between devices: 0.01 us -> 6.02 us  [local(): across = lax.all_to_all(products, 'x', 0, 0)]
    ppermute x6, waiting for transfers between devices: 9.4 us -> 3.86 us  [neighbour(): return lax.ppermute(value, ROWS + COLS, pairs)]
    all_to_all x1, blocking collectives: 14.9 us -> 19.3 us  [local(): planes = lax.all_to_all(halves, 'y', 0, 0)]
    unnamed x16 -> x6, local copies, waits for them, and re-layouts: 3.94 us -> 0.02 us
    all_to_all x1, starting transfers between devices: 5.85 us -> 3.52 us  [local(): across = lax.all_to_all(products, 'x', 0, 0)]
    all_to_all x1, blocking collectives: 18.2 us -> 16 us  [local(): lines = lax.all_to_all(chunks, ('zh', 'zl'), 0, 0)]
    pallas_call x9, Pallas kernels: 12.3 us -> 14.1 us  [call(): pl.pallas_call(kernel, in_specs=[pl.BlockSpec(memory_space=pltpu.HBM if k...]
  transfers between devices with their start and end apart: 9 -> 9, of which waited for: 4 -> 5; matrix products, arithmetic and copies ran while one was open for 0% -> 0% of each run, Pallas kernels for 2% -> 2%
where the time goes in v3:
time: 118 us; the launch traced here: 116 us
  starting transfers between devices  50.5 us (43%)
  blocking collectives  35.3 us (30%)
  waiting for transfers between devices  15.1 us (13%)
  Pallas kernels  14.1 us (12%)
    ppermute x6, starting transfers between devices, neighbour(): return lax.ppermute(value, ROWS + COLS, pairs)  40.4 us
    all_to_all x1, blocking collectives, local(): planes = lax.all_to_all(halves, 'y', 0, 0)  19.3 us
    all_to_all x1, blocking collectives, local(): lines = lax.all_to_all(chunks, ('zh', 'zl'), 0, 0)  16 us
    pallas_call x9, Pallas kernels, call(): pl.pallas_call(kernel, in_specs=[pl.BlockSpec(memory_space=pltpu.HBM if k...  14.1 us
    all_to_all x1, waiting for transfers between devices, local(): across = lax.all_to_all(products, 'x', 0, 0)  6.02 us
    ppermute x6, waiting for transfers between devices, neighbour(): return lax.ppermute(value, ROWS + COLS, pairs)  3.86 us
    all_to_all x1, starting transfers between devices, local(): across = lax.all_to_all(products, 'x', 0, 0)  3.52 us
    all_to_all x1, waiting for transfers between devices, local(): finals = lax.all_to_all(finals, 'x', 0, 0)  3.45 us
  transfers between devices with their start and end apart: 9, of which 5 were waited for; matrix products, arithmetic and copies ran while one was open for 0% of the time, Pallas kernels for 2%

profile of v3, /device:TPU:1, one launch (start us, length us, event | category | flops | bytes accessed | tf_op | source)
XLA Modules:
  0.0 115.9 jit_solution(14831126042013839265)
XLA Ops:
  0.6 1.0 shard_map.120
  1.7 12.4 %collective-permute-start = (bf16[112,512]{1,0:T(8,128)(2,1)S(1)}, bf16[112,512]{1,0:T(8,128)(2,1)S(1)}, u32[]{:S(2)}, u32[]{:S(2)}) collective-permute-start(bf16[112,512]{1,0:T(8,128)(2,1)S(1)} %get-tuple-element.31), channel_id=1, source_target_pairs={{0,744},{1,745},{2,746},{3,747},{4,748},{5,749},{6,750},{7,751},{8... | collective-permute-start | bytes 344072 | tf_op jit(solution)/shard_map/ppermute | solution.py:391
  14.1 5.6 %collective-permute-start.1 = (bf16[9,4,512]{2,1,0:T(4,128)(2,1)S(1)}, bf16[9,4,512]{2,1,0:T(4,128)(2,1)S(1)}, u32[]{:S(2)}, u32[]{:S(2)}) collective-permute-start(bf16[9,4,512]{2,1,0:T(4,128)(2,1)S(1)} %get-tuple-element.32), channel_id=1, source_target_pairs={{0,23},{1,0},{2,1},{3,2},{4,3},{5,4},{6,5},{7,6},{8,7},{9,8},{10,9... | collective-permute-start | bytes 110600 | tf_op jit(solution)/shard_map/ppermute | solution.py:391
  19.7 12.8 %collective-permute-start.2 = (bf16[9,4,512]{2,1,0:T(4,128)(2,1)S(1)}, bf16[9,4,512]{2,1,0:T(4,128)(2,1)S(1)}, u32[]{:S(2)}, u32[]{:S(2)}) collective-permute-start(bf16[9,4,512]{2,1,0:T(4,128)(2,1)S(1)} %get-tuple-element.33), channel_id=1, source_target_pairs={{0,767},{1,744},{2,745},{3,746},{4,747},{5,748},{6,749},{7,750},{8... | collective-permute-start | bytes 110600 | tf_op jit(solution)/shard_map/ppermute | solution.py:391
  32.6 1.2 %shard_map.119 = (f32[16,64,128]{2,1,0:T(8,128)S(1)}, s32[64,128]{1,0:T(8,128)S(1)}) custom-call(f32[16,225]{1,0:T(8,128)} %bitcast.6, s32[64,64]{1,0:T(8,128)} %bucket_far.1), custom_call_target="tpu_custom_call" | custom-call | bytes 8388608 | tf_op jit(solution)/shard_map/pallas_call | solution.py:372
  33.8 0.0 collective-permute-done.1.left
  33.8 0.0 collective-permute-done.2.diag
  33.8 0.0 collective-permute-done.up
  33.8 7.9 %shard_map.121 = (bf16[144,2560]{1,0:T(8,128)(2,1)S(1)}, bf16[128,512]{1,0:T(8,128)(2,1)S(1)}, f32[4,12,512]{2,1,0:T(8,128)S(1)}, bf16[4,12,512]{2,1,0:T(8,128)(...) custom-call(bf16[8,16,512]{2,1,0:T(8,128)(2,1)} %tok.3, bf16[8,16,512]{2,1,0:T(8,128)(2,1)} %cot.3, ...), custom_call_target="tpu_custom_call" | custom-call | flops 1073741824 | bytes 8388608 | tf_op jit(solution)/shard_map/pallas_call | solution.py:372
  41.8 3.2 %collective-permute-start.3 = (bf16[144,2560]{1,0:T(8,128)(2,1)S(1)}, bf16[144,2560]{1,0:T(8,128)(2,1)S(1)}, u32[]{:S(2)}, u32[]{:S(2)}) collective-permute-start(bf16[144,2560]{1,0:T(8,128)(2,1)S(1)} %get-tuple-element.35.mine), channel_id=1, source_target_pairs={{0,24},{24,0},{1,25},{25,1},{2,26},{26,2},{3,27},{27,3},{4,28},{28... | collective-permute-start | bytes 2211848 | tf_op jit(solution)/shard_map/ppermute | solution.py:459
  45.0 1.8 %collective-permute-done.3.other = bf16[144,2560]{1,0:T(8,128)(2,1)S(1)} collective-permute-done((bf16[144,2560]{1,0:T(8,128)(2,1)S(1)}, bf16[144,2560]{1,0:T(8,128)(2,1)S(1)}, u32[]{:S(2)}, u32[]{:S(2)}) %collective-permute-start.3) | collective-permute-done | bytes 737312 | tf_op jit(solution)/shard_map/ppermute | solution.py:459
  46.8 1.5 %shard_map.122 = bf16[4,272,512]{2,1,0:T(8,128)(2,1)} custom-call(bf16[144,2560]{1,0:T(8,128)(2,1)S(1)} %get-tuple-element.35.mine, bf16[144,2560]{1,0:T(8,128)(2,1)S(1)} %collective-permute-done.3.other, bf16[128,512]{1,0:T(8,128)(2,1)S(1)} %get-tuple-element.36.keep), custom_call_target="tpu_custom_call" | custom-call | flops 536870912 | bytes 2097152 | tf_op jit(solution)/shard_map/pallas_call | solution.py:372
  48.3 3.5 %all-to-all-start = ((bf16[4,272,512]{2,1,0:T(8,128)(2,1)}), bf16[4,272,512]{2,1,0:T(8,128)(2,1)S(1)}, u32[]{:S(2)}, u32[]{:S(2)}) async-start(bf16[4,272,512]{2,1,0:T(8,128)(2,1)} %shard_map.122), calls=%async_computation | async-start | bytes 2228224 | tf_op jit(solution)/shard_map/all_to_all | solution.py:470
  51.8 5.7 %collective-permute-start.4 = (bf16[4,12,512]{2,1,0:T(8,128)(2,1)S(1)}, bf16[4,12,512]{2,1,0:T(8,128)(2,1)S(1)}, u32[]{:S(2)}, u32[]{:S(2)}) collective-permute-start(bf16[4,12,512]{2,1,0:T(8,128)(2,1)S(1)} %get-tuple-element.41), channel_id=1, source_target_pairs={{0,24},{1,25},{2,26},{3,27},{4,28},{5,29},{6,30},{7,31},{8,32},{9,... | collective-permute-start | bytes 147464 | tf_op jit(solution)/shard_map/ppermute | solution.py:391
  57.5 1.9 %collective-permute-start.5 = (bf16[4,4,512]{2,1,0:T(4,128)(2,1)S(1)}, bf16[4,4,512]{2,1,0:T(4,128)(2,1)S(1)}, u32[]{:S(2)}, u32[]{:S(2)}) collective-permute-start(bf16[4,4,512]{2,1,0:T(4,128)(2,1)S(1)} %get-tuple-element.42), channel_id=1, source_target_pairs={{0,1},{1,2},{2,3},{3,4},{4,5},{5,6},{6,7},{7,8},{8,9},{9,10},{10,1... | collective-permute-start | bytes 49160 | tf_op jit(solution)/shard_map/ppermute | solution.py:391
  59.5 1.9 %collective-permute-start.6 = (bf16[4,4,512]{2,1,0:T(4,128)(2,1)S(1)}, bf16[4,4,512]{2,1,0:T(4,128)(2,1)S(1)}, u32[]{:S(2)}, u32[]{:S(2)}) collective-permute-start(bf16[4,4,512]{2,1,0:T(4,128)(2,1)S(1)} %get-tuple-element.43), channel_id=1, source_target_pairs={{0,25},{1,26},{2,27},{3,28},{4,29},{5,30},{6,31},{7,32},{8,33},{9,... | collective-permute-start | bytes 49160 | tf_op jit(solution)/shard_map/ppermute | solution.py:391
  61.4 6.0 %all-to-all-done.parts = bf16[4,272,512]{2,1,0:T(8,128)(2,1)S(1)} async-done(((bf16[4,272,512]{2,1,0:T(8,128)(2,1)}), bf16[4,272,512]{2,1,0:T(8,128)(2,1)S(1)}, u32[]{:S(2)}, u32[]{:S(2)}) %all-to-all-start) | async-done | bytes 1114144 | tf_op jit(solution)/shard_map/all_to_all | solution.py:470
  67.4 0.1 shard_map.123
  67.5 0.0 copy-start
  67.6 0.0 copy-start.1
  67.6 0.0 copy-start.2
  67.6 1.3 %collective-permute-done.5.left = bf16[4,4,512]{2,1,0:T(4,128)(2,1)S(1)} collective-permute-done((bf16[4,4,512]{2,1,0:T(4,128)(2,1)S(1)}, bf16[4,4,512]{2,1,0:T(4,128)(2,1)S(1)}, u32[]{:S(2)}, u32[]{:S(2)}) %collective-permute-start.5) | collective-permute-done | bytes 16416 | tf_op jit(solution)/shard_map/ppermute | solution.py:391
  68.9 2.5 %collective-permute-done.6.diag = bf16[4,4,512]{2,1,0:T(4,128)(2,1)S(1)} collective-permute-done((bf16[4,4,512]{2,1,0:T(4,128)(2,1)S(1)}, bf16[4,4,512]{2,1,0:T(4,128)(2,1)S(1)}, u32[]{:S(2)}, u32[]{:S(2)}) %collective-permute-start.6) | collective-permute-done | bytes 16416 | tf_op jit(solution)/shard_map/ppermute | solution.py:391
  71.4 0.0 collective-permute-done.4.above
  71.4 19.3 %all_to_all.20.parts = bf16[8,32,640]{2,1,0:T(8,128)(2,1)S(1)} all-to-all(bf16[8,32,640]{2,1,0:T(8,128)(2,1)S(1)} %shard_map.123), channel_id=1, replica_groups=mesh['y'=8,'zh'=2,'core'=2,'x'=4,'zl'=6] {'y'}, dimensions={0} | all-to-all | bytes 655360 | tf_op jit(solution)/shard_map/all_to_all | solution.py:478
  90.8 0.1 shard_map.125
  90.9 16.0 %all_to_all.21.parts = bf16[12,16,384]{2,1,0:T(8,128)(2,1)S(1)} all-to-all(bf16[12,16,384]{2,1,0:T(8,128)(2,1)S(1)} %shard_map.125), channel_id=1, replica_groups=mesh['y'=8,'zh'=2,'core'=2,'x'=4,'zl'=6] {'zh','zl'}, dimensions={0} | all-to-all | bytes 294912 | tf_op jit(solution)/shard_map/all_to_all | solution.py:480
  106.8 0.7 shard_map.126
  107.5 3.3 %all-to-all-start.3 = ((f32[4,32,128]{2,1,0:T(8,128)}), f32[4,32,128]{2,1,0:T(8,128)S(1)}, u32[]{:S(2)}, u32[]{:S(2)}) async-start(f32[4,32,128]{2,1,0:T(8,128)} %get-tuple-element.49), calls=%async_computation.3 | async-start | bytes 131072 | tf_op jit(solution)/shard_map/all_to_all | solution.py:484
  110.8 0.0 copy-done
  110.8 0.0 copy-done.1
  110.8 0.0 copy-done.2
  110.8 1.0 shard_map.124
  111.8 3.4 %all-to-all-done.3.parts = f32[4,32,128]{2,1,0:T(8,128)S(1)} async-done(((f32[4,32,128]{2,1,0:T(8,128)}), f32[4,32,128]{2,1,0:T(8,128)S(1)}, u32[]{:S(2)}, u32[]{:S(2)}) %all-to-all-start.3) | async-done | bytes 65568 | tf_op jit(solution)/shard_map/all_to_all | solution.py:484
  115.2 0.6 shard_map.127
Async XLA Ops:
  1.7 32.2 %collective-permute-start = (bf16[112,512]{1,0:T(8,128)(2,1)S(1)}, bf16[112,512]{1,0:T(8,128)(2,1)S(1)}, u32[]{:S(2)}, u32[]{:S(2)}) collective-permute-start(bf16[112,512]{1,0:T(8,128)(2,1)S(1)} %get-tuple-element.31), channel_id=1, source_target_pairs={{0,744},{1,745},{2,746},{3,747},{4,748},{5,749},{6,750},{7,751},{8... | collective-permute-start | bytes 344072 | tf_op jit(solution)/shard_map/ppermute | solution.py:391
  14.1 19.7 %collective-permute-start.1 = (bf16[9,4,512]{2,1,0:T(4,128)(2,1)S(1)}, bf16[9,4,512]{2,1,0:T(4,128)(2,1)S(1)}, u32[]{:S(2)}, u32[]{:S(2)}) collective-permute-start(bf16[9,4,512]{2,1,0:T(4,128)(2,1)S(1)} %get-tuple-element.32), channel_id=1, source_target_pairs={{0,23},{1,0},{2,1},{3,2},{4,3},{5,4},{6,5},{7,6},{8,7},{9,8},{10,9... | collective-permute-start | bytes 110600 | tf_op jit(solution)/shard_map/ppermute | solution.py:391
  19.7 14.1 %collective-permute-start.2 = (bf16[9,4,512]{2,1,0:T(4,128)(2,1)S(1)}, bf16[9,4,512]{2,1,0:T(4,128)(2,1)S(1)}, u32[]{:S(2)}, u32[]{:S(2)}) collective-permute-start(bf16[9,4,512]{2,1,0:T(4,128)(2,1)S(1)} %get-tuple-element.33), channel_id=1, source_target_pairs={{0,767},{1,744},{2,745},{3,746},{4,747},{5,748},{6,749},{7,750},{8... | collective-permute-start | bytes 110600 | tf_op jit(solution)/shard_map/ppermute | solution.py:391
  41.8 5.1 %collective-permute-start.3 = (bf16[144,2560]{1,0:T(8,128)(2,1)S(1)}, bf16[144,2560]{1,0:T(8,128)(2,1)S(1)}, u32[]{:S(2)}, u32[]{:S(2)}) collective-permute-start(bf16[144,2560]{1,0:T(8,128)(2,1)S(1)} %get-tuple-element.35.mine), channel_id=1, source_target_pairs={{0,24},{24,0},{1,25},{25,1},{2,26},{26,2},{3,27},{27,3},{4,28},{28... | collective-permute-start | bytes 2211848 | tf_op jit(solution)/shard_map/ppermute | solution.py:459
  48.3 19.1 %all-to-all-start = ((bf16[4,272,512]{2,1,0:T(8,128)(2,1)}), bf16[4,272,512]{2,1,0:T(8,128)(2,1)S(1)}, u32[]{:S(2)}, u32[]{:S(2)}) async-start(bf16[4,272,512]{2,1,0:T(8,128)(2,1)} %shard_map.122), calls=%async_computation | async-start | bytes 2228224 | tf_op jit(solution)/shard_map/all_to_all | solution.py:470
  51.8 19.6 %collective-permute-start.4 = (bf16[4,12,512]{2,1,0:T(8,128)(2,1)S(1)}, bf16[4,12,512]{2,1,0:T(8,128)(2,1)S(1)}, u32[]{:S(2)}, u32[]{:S(2)}) collective-permute-start(bf16[4,12,512]{2,1,0:T(8,128)(2,1)S(1)} %get-tuple-element.41), channel_id=1, source_target_pairs={{0,24},{1,25},{2,26},{3,27},{4,28},{5,29},{6,30},{7,31},{8,32},{9,... | collective-permute-start | bytes 147464 | tf_op jit(solution)/shard_map/ppermute | solution.py:391
  57.5 11.4 %collective-permute-start.5 = (bf16[4,4,512]{2,1,0:T(4,128)(2,1)S(1)}, bf16[4,4,512]{2,1,0:T(4,128)(2,1)S(1)}, u32[]{:S(2)}, u32[]{:S(2)}) collective-permute-start(bf16[4,4,512]{2,1,0:T(4,128)(2,1)S(1)} %get-tuple-element.42), channel_id=1, source_target_pairs={{0,1},{1,2},{2,3},{3,4},{4,5},{5,6},{6,7},{7,8},{8,9},{9,10},{10,1... | collective-permute-start | bytes 49160 | tf_op jit(solution)/shard_map/ppermute | solution.py:391
  59.5 12.0 %collective-permute-start.6 = (bf16[4,4,512]{2,1,0:T(4,128)(2,1)S(1)}, bf16[4,4,512]{2,1,0:T(4,128)(2,1)S(1)}, u32[]{:S(2)}, u32[]{:S(2)}) collective-permute-start(bf16[4,4,512]{2,1,0:T(4,128)(2,1)S(1)} %get-tuple-element.43), channel_id=1, source_target_pairs={{0,25},{1,26},{2,27},{3,28},{4,29},{5,30},{6,31},{7,32},{8,33},{9,... | collective-permute-start | bytes 49160 | tf_op jit(solution)/shard_map/ppermute | solution.py:391
  67.5 43.2 %copy-start = (bf16[8,16,512]{2,1,0:T(8,128)(2,1)S(1)}, bf16[8,16,512]{2,1,0:T(8,128)(2,1)}, u32[]{:S(2)}) copy-start(bf16[8,16,512]{2,1,0:T(8,128)(2,1)} %tok.3) | copy-start | bytes 393220
  67.6 43.2 %copy-start.1 = (bf16[8,16,512]{2,1,0:T(8,128)(2,1)S(1)}, bf16[8,16,512]{2,1,0:T(8,128)(2,1)}, u32[]{:S(2)}) copy-start(bf16[8,16,512]{2,1,0:T(8,128)(2,1)} %cot.3) | copy-start | bytes 393220
  67.6 43.2 %copy-start.2 = (f32[512]{0:T(512)S(1)}, f32[512]{0:T(512)}, u32[]{:S(2)}) copy-start(f32[512]{0:T(512)} %param.11) | copy-start | bytes 6148
  107.5 7.7 %all-to-all-start.3 = ((f32[4,32,128]{2,1,0:T(8,128)}), f32[4,32,128]{2,1,0:T(8,128)S(1)}, u32[]{:S(2)}, u32[]{:S(2)}) async-start(f32[4,32,128]{2,1,0:T(8,128)} %get-tuple-element.49), calls=%async_computation.3 | async-start | bytes 131072 | tf_op jit(solution)/shard_map/all_to_all | solution.py:484

commit v4 on v3

--- a/solution.py
+++ b/solution.py
@@ -98,7 +98,7 @@
         copy.wait()
     turned = jnp.concatenate([table[...], jnp.zeros((HEADS, 256 - NBIAS), F32)], axis=1)
     both = jnp.concatenate([bucket[...], bucket[...]], axis=1)
-    bucket2[...] = both
+    bucket2[...] = jnp.where(iota((32, 128), 1) < 64, both[0:32], both[32:64])
     for block in range(AREA // 8):
         index = both[block * 8 : block * 8 + 8]
         upper = index >= 128
@@ -221,7 +221,9 @@
         send[0:TOKENS, 2 * D + at : 2 * D + at + 128] = dot_tn(probs_low, outer_s).astype(BF16)
         for h in range(GROUP):
             one = grad_scores[h * 128 : h * 128 + 128]
-            pairs[g * GROUP + h] = one[0:64] + one[64:128]
+            pairs[g * GROUP + h] = (one[0:32] + one[96:128]) + pltpu.roll(
+                one[32:64] + one[64:96], 64, 1
+            )
 
     core = lax.axis_index("core")
     for k, matrix in ((0, normed), (1, attended[...])):
@@ -239,13 +241,22 @@
     gain_sum = jnp.sum(grad_normed * hat, axis=0, keepdims=True)
 
     bucket_of = iota((256, 128), 0)
-
-    def add_row(i, total):
-        high, low = split_high_low(pairs[:, i, :])
-        hot = (bucket_of == jnp.broadcast_to(bucket2[pl.ds(i, 1), :], (256, 128))).astype(BF16)
-        return total + dot_nt(jnp.concatenate([high, low], axis=0), hot)
-
-    sums = lax.fori_loop(0, AREA, add_row, jnp.zeros((2 * HEADS, 256), F32), unroll=8)
+    step = 2
+
+    def add_rows(k, total):
+        parts, hots = [], []
+        for t in range(step):
+            i = k * step + t
+            parts.append(pairs[:, i, :])
+            which = jnp.broadcast_to(bucket2[pl.ds(i, 1), :], (256, 128))
+            hots.append((bucket_of == which).astype(BF16))
+        high, low = split_high_low(jnp.concatenate(parts, axis=1))
+        both = jnp.concatenate([high, low], axis=0)
+        return total + dot_nt(both, jnp.concatenate(hots, axis=1))
+
+    sums = lax.fori_loop(
+        0, AREA // 2 // step, add_rows, jnp.zeros((2 * HEADS, 256), F32), unroll=True
+    )
     table = sums[0:HEADS] + sums[HEADS : 2 * HEADS]
     high, low = split_high_low(table)
     send[TOKENS : TOKENS + 16, 0:256] = high
@@ -413,7 +424,7 @@
         bias_kernel,
         [
             shape((HEADS, AREA, 128), F32),
-            shape((AREA, 128), jnp.int32),
+            shape((AREA // 2, 128), jnp.int32),
         ],
         (bias_table.T, bias_bucket),
         [
@@ -442,7 +453,7 @@
             pltpu.VMEM((TOKENS, 3 * D), BF16),
             pltpu.VMEM((TOKENS, D), BF16),
             pltpu.VMEM((TOKENS, D), BF16),
-            pltpu.VMEM((HEADS, AREA, 128), F32),
+            pltpu.VMEM((HEADS, AREA // 2, 128), F32),
             pltpu.VMEM((TOKENS, D), F32),
             pltpu.VMEM((8, 16, D), BF16),
             pltpu.VMEM((8, 16, D), BF16),
@@ -464,19 +475,18 @@
         flops=1 << 29,
         moved=1 << 21,
     )
-    products, down_grad, right_grad, diag_grad = lax.optimization_barrier(
-        (products, down_grad, right_grad, diag_grad)
-    )
+    products, down_grad = lax.optimization_barrier((products, down_grad))
     across = lax.all_to_all(products, "x", 0, 0)
     above_grad = neighbour(down_grad, 1, 0)
+    halves = call(across_sum_kernel, shape((8, 32, 640), BF16), (across,), moved=1 << 21)
+    halves, above_grad, right_grad, diag_grad = lax.optimization_barrier(
+        (halves, above_grad, right_grad, diag_grad)
+    )
+    planes = lax.all_to_all(halves, "y", 0, 0)
     left_grad = neighbour(right_grad, 0, 1)
     corner_grad = neighbour(diag_grad, 1, 1)
-    halves = call(across_sum_kernel, shape((8, 32, 640), BF16), (across,), moved=1 << 21)
-    halves, above_grad, left_grad, corner_grad = lax.optimization_barrier(
-        (halves, above_grad, left_grad, corner_grad)
-    )
-    planes = lax.all_to_all(halves, "y", 0, 0)
     chunks = call(plane_sum_kernel, shape((12, 16, 384), BF16), (planes,), moved=1 << 21)
+    chunks, left_grad, corner_grad = lax.optimization_barrier((chunks, left_grad, corner_grad))
     lines = lax.all_to_all(chunks, ("zh", "zl"), 0, 0)
     grad_qkv, finals = call(
         line_sum_kernel, [shape((16, 64), F32), shape((4, 32, 128), F32)], (lines,), moved=1 << 18

time: 118 us -> 117 us (level)
  the two profiles are of different devices: /device:TPU:1 before, /device:TPU:8 now
where the time goes in v4:
time: 117 us; the launch traced here: 116 us
  starting transfers between devices  48.1 us (41%)
  waiting for transfers between devices  32 us (27%)
  blocking collectives  22.1 us (19%)
  Pallas kernels  13.1 us (11%)
    ppermute x6, starting transfers between devices, neighbour(): return lax.ppermute(value, ROWS + COLS, pairs)  31.5 us
    all_to_all x1, blocking collectives, local(): lines = lax.all_to_all(chunks, ('zh', 'zl'), 0, 0)  22.1 us
    all_to_all x1, waiting for transfers between devices, local(): across = lax.all_to_all(products, 'x', 0, 0)  14.3 us
    pallas_call x9, Pallas kernels, call(): pl.pallas_call(kernel, in_specs=[pl.BlockSpec(memory_space=pltpu.HBM if k...  13.1 us
    all_to_all x1, starting transfers between devices, local(): planes = lax.all_to_all(halves, 'y', 0, 0)  7.8 us
    all_to_all x1, waiting for transfers between devices, local(): planes = lax.all_to_all(halves, 'y', 0, 0)  7.44 us
    all_to_all x1, waiting for transfers between devices, local(): finals = lax.all_to_all(finals, 'x', 0, 0)  4.6 us
    ppermute x6, waiting for transfers between devices, neighbour(): return lax.ppermute(value, ROWS + COLS, pairs)  3.63 us
  transfers between devices with their start and end apart: 10, of which 7 were waited for; matrix products, arithmetic and copies ran while one was open for 0% of the time, Pallas kernels for 3%

profile of v4, /device:TPU:8, one launch (start us, length us, event | category | flops | bytes accessed | tf_op | source)
XLA Modules:
  0.0 116.2 jit_solution(16640201212027781019)
XLA Ops:
  0.6 1.0 shard_map.120
  1.7 14.5 %collective-permute-start = (bf16[112,512]{1,0:T(8,128)(2,1)S(1)}, bf16[112,512]{1,0:T(8,128)(2,1)S(1)}, u32[]{:S(2)}, u32[]{:S(2)}) collective-permute-start(bf16[112,512]{1,0:T(8,128)(2,1)S(1)} %get-tuple-element.32), channel_id=1, source_target_pairs={{0,744},{1,745},{2,746},{3,747},{4,748},{5,749},{6,750},{7,751},{8... | collective-permute-start | bytes 344072 | tf_op jit(solution)/shard_map/ppermute | solution.py:402
  16.1 9.2 %collective-permute-start.1 = (bf16[9,4,512]{2,1,0:T(4,128)(2,1)S(1)}, bf16[9,4,512]{2,1,0:T(4,128)(2,1)S(1)}, u32[]{:S(2)}, u32[]{:S(2)}) collective-permute-start(bf16[9,4,512]{2,1,0:T(4,128)(2,1)S(1)} %get-tuple-element.33), channel_id=1, source_target_pairs={{0,23},{1,0},{2,1},{3,2},{4,3},{5,4},{6,5},{7,6},{8,7},{9,8},{10,9... | collective-permute-start | bytes 110600 | tf_op jit(solution)/shard_map/ppermute | solution.py:402
  25.4 1.9 %collective-permute-start.2 = (bf16[9,4,512]{2,1,0:T(4,128)(2,1)S(1)}, bf16[9,4,512]{2,1,0:T(4,128)(2,1)S(1)}, u32[]{:S(2)}, u32[]{:S(2)}) collective-permute-start(bf16[9,4,512]{2,1,0:T(4,128)(2,1)S(1)} %get-tuple-element.34), channel_id=1, source_target_pairs={{0,767},{1,744},{2,745},{3,746},{4,747},{5,748},{6,749},{7,750},{8... | collective-permute-start | bytes 110600 | tf_op jit(solution)/shard_map/ppermute | solution.py:402
  27.3 1.2 %shard_map.119 = (f32[16,64,128]{2,1,0:T(8,128)S(1)}, s32[32,128]{1,0:T(8,128)S(1)}) custom-call(f32[16,225]{1,0:T(8,128)} %bitcast.6, s32[64,64]{1,0:T(8,128)} %bucket_far.1), custom_call_target="tpu_custom_call" | custom-call | bytes 8388608 | tf_op jit(solution)/shard_map/pallas_call | solution.py:383
  28.5 0.0 collective-permute-done.1.left
  28.5 2.1 %collective-permute-done.2.diag = bf16[9,4,512]{2,1,0:T(4,128)(2,1)S(1)} collective-permute-done((bf16[9,4,512]{2,1,0:T(4,128)(2,1)S(1)}, bf16[9,4,512]{2,1,0:T(4,128)(2,1)S(1)}, u32[]{:S(2)}, u32[]{:S(2)}) %collective-permute-start.2) | collective-permute-done | bytes 36896 | tf_op jit(solution)/shard_map/ppermute | solution.py:402
  30.6 0.0 collective-permute-done.up
  30.6 6.2 %shard_map.121 = (bf16[144,2560]{1,0:T(8,128)(2,1)S(1)}, bf16[128,512]{1,0:T(8,128)(2,1)S(1)}, f32[4,12,512]{2,1,0:T(8,128)S(1)}, bf16[4,12,512]{2,1,0:T(8,128)(...) custom-call(bf16[8,16,512]{2,1,0:T(8,128)(2,1)} %tok.3, bf16[8,16,512]{2,1,0:T(8,128)(2,1)} %cot.3, ...), custom_call_target="tpu_custom_call" | custom-call | flops 1073741824 | bytes 8388608 | tf_op jit(solution)/shard_map/pallas_call | solution.py:383
  36.8 2.0 %collective-permute-start.3 = (bf16[144,2560]{1,0:T(8,128)(2,1)S(1)}, bf16[144,2560]{1,0:T(8,128)(2,1)S(1)}, u32[]{:S(2)}, u32[]{:S(2)}) collective-permute-start(bf16[144,2560]{1,0:T(8,128)(2,1)S(1)} %get-tuple-element.36.mine), channel_id=1, source_target_pairs={{0,24},{24,0},{1,25},{25,1},{2,26},{26,2},{3,27},{27,3},{4,28},{28... | collective-permute-start | bytes 2211848 | tf_op jit(solution)/shard_map/ppermute | solution.py:470
  38.9 2.1 %collective-permute-done.3.other = bf16[144,2560]{1,0:T(8,128)(2,1)S(1)} collective-permute-done((bf16[144,2560]{1,0:T(8,128)(2,1)S(1)}, bf16[144,2560]{1,0:T(8,128)(2,1)S(1)}, u32[]{:S(2)}, u32[]{:S(2)}) %collective-permute-start.3) | collective-permute-done | bytes 737312 | tf_op jit(solution)/shard_map/ppermute | solution.py:470
  40.9 1.5 %shard_map.122 = bf16[4,272,512]{2,1,0:T(8,128)(2,1)} custom-call(bf16[144,2560]{1,0:T(8,128)(2,1)S(1)} %get-tuple-element.36.mine, bf16[144,2560]{1,0:T(8,128)(2,1)S(1)} %collective-permute-done.3.other, bf16[128,512]{1,0:T(8,128)(2,1)S(1)} %get-tuple-element.37.keep), custom_call_target="tpu_custom_call" | custom-call | flops 536870912 | bytes 2097152 | tf_op jit(solution)/shard_map/pallas_call | solution.py:383
  42.4 3.5 %all-to-all-start = ((bf16[4,272,512]{2,1,0:T(8,128)(2,1)}), bf16[4,272,512]{2,1,0:T(8,128)(2,1)S(1)}, u32[]{:S(2)}, u32[]{:S(2)}) async-start(bf16[4,272,512]{2,1,0:T(8,128)(2,1)} %shard_map.122), calls=%async_computation | async-start | bytes 2228224 | tf_op jit(solution)/shard_map/all_to_all | solution.py:479
  45.9 2.0 %collective-permute-start.4 = (bf16[4,12,512]{2,1,0:T(8,128)(2,1)S(1)}, bf16[4,12,512]{2,1,0:T(8,128)(2,1)S(1)}, u32[]{:S(2)}, u32[]{:S(2)}) collective-permute-start(bf16[4,12,512]{2,1,0:T(8,128)(2,1)S(1)} %get-tuple-element.40), channel_id=1, source_target_pairs={{0,24},{1,25},{2,26},{3,27},{4,28},{5,29},{6,30},{7,31},{8,32},{9,... | collective-permute-start | bytes 147464 | tf_op jit(solution)/shard_map/ppermute | solution.py:402
  48.0 14.3 %all-to-all-done.parts = bf16[4,272,512]{2,1,0:T(8,128)(2,1)S(1)} async-done(((bf16[4,272,512]{2,1,0:T(8,128)(2,1)}), bf16[4,272,512]{2,1,0:T(8,128)(2,1)S(1)}, u32[]{:S(2)}, u32[]{:S(2)}) %all-to-all-start) | async-done | bytes 1114144 | tf_op jit(solution)/shard_map/all_to_all | solution.py:479
  62.3 0.9 shard_map.123
  63.1 0.0 copy-start
  63.1 0.0 copy-start.1
  63.1 0.0 copy-start.2
  63.1 0.0 collective-permute-done.4.above
  63.1 7.8 %all-to-all-start.1 = ((bf16[8,32,640]{2,1,0:T(8,128)(2,1)}), bf16[8,32,640]{2,1,0:T(8,128)(2,1)S(1)}, u32[]{:S(2)}, u32[]{:S(2)}) async-start(bf16[8,32,640]{2,1,0:T(8,128)(2,1)} %shard_map.123), calls=%async_computation.1 | async-start | bytes 655360 | tf_op jit(solution)/shard_map/all_to_all | solution.py:485
  70.9 1.9 %collective-permute-start.5 = (bf16[4,4,512]{2,1,0:T(4,128)(2,1)S(1)}, bf16[4,4,512]{2,1,0:T(4,128)(2,1)S(1)}, u32[]{:S(2)}, u32[]{:S(2)}) collective-permute-start(bf16[4,4,512]{2,1,0:T(4,128)(2,1)S(1)} %get-tuple-element.45), channel_id=1, source_target_pairs={{0,1},{1,2},{2,3},{3,4},{4,5},{5,6},{6,7},{7,8},{8,9},{9,10},{10,1... | collective-permute-start | bytes 49160 | tf_op jit(solution)/shard_map/ppermute | solution.py:402
  72.9 1.9 %collective-permute-start.6 = (bf16[4,4,512]{2,1,0:T(4,128)(2,1)S(1)}, bf16[4,4,512]{2,1,0:T(4,128)(2,1)S(1)}, u32[]{:S(2)}, u32[]{:S(2)}) collective-permute-start(bf16[4,4,512]{2,1,0:T(4,128)(2,1)S(1)} %get-tuple-element.46), channel_id=1, source_target_pairs={{0,25},{1,26},{2,27},{3,28},{4,29},{5,30},{6,31},{7,32},{8,33},{9,... | collective-permute-start | bytes 49160 | tf_op jit(solution)/shard_map/ppermute | solution.py:402
  74.8 7.4 %all-to-all-done.1.parts = bf16[8,32,640]{2,1,0:T(8,128)(2,1)S(1)} async-done(((bf16[8,32,640]{2,1,0:T(8,128)(2,1)}), bf16[8,32,640]{2,1,0:T(8,128)(2,1)S(1)}, u32[]{:S(2)}, u32[]{:S(2)}) %all-to-all-start.1) | async-done | bytes 327712 | tf_op jit(solution)/shard_map/all_to_all | solution.py:485
  82.2 0.1 shard_map.124
  82.3 1.2 collective-permute-done.5.left
  83.5 0.4 collective-permute-done.6.diag
  83.9 22.1 %all_to_all.20.parts = bf16[12,16,384]{2,1,0:T(8,128)(2,1)S(1)} all-to-all(bf16[12,16,384]{2,1,0:T(8,128)(2,1)S(1)} %shard_map.124), channel_id=1, replica_groups=mesh['y'=8,'zh'=2,'core'=2,'x'=4,'zl'=6] {'zh','zl'}, dimensions={0} | all-to-all | bytes 294912 | tf_op jit(solution)/shard_map/all_to_all | solution.py:490
  106.0 0.6 shard_map.126
  106.7 3.3 %all-to-all-start.3 = ((f32[4,32,128]{2,1,0:T(8,128)}), f32[4,32,128]{2,1,0:T(8,128)S(1)}, u32[]{:S(2)}, u32[]{:S(2)}) async-start(f32[4,32,128]{2,1,0:T(8,128)} %get-tuple-element.51), calls=%async_computation.3 | async-start | bytes 131072 | tf_op jit(solution)/shard_map/all_to_all | solution.py:494
  109.9 0.0 copy-done
  110.0 0.0 copy-done.1
  110.0 0.0 copy-done.2
  110.0 1.0 shard_map.125
  110.9 4.6 %all-to-all-done.3.parts = f32[4,32,128]{2,1,0:T(8,128)S(1)} async-done(((f32[4,32,128]{2,1,0:T(8,128)}), f32[4,32,128]{2,1,0:T(8,128)S(1)}, u32[]{:S(2)}, u32[]{:S(2)}) %all-to-all-start.3) | async-done | bytes 65568 | tf_op jit(solution)/shard_map/all_to_all | solution.py:494
  115.5 0.6 shard_map.127
Async XLA Ops:
  1.7 29.0 %collective-permute-start = (bf16[112,512]{1,0:T(8,128)(2,1)S(1)}, bf16[112,512]{1,0:T(8,128)(2,1)S(1)}, u32[]{:S(2)}, u32[]{:S(2)}) collective-permute-start(bf16[112,512]{1,0:T(8,128)(2,1)S(1)} %get-tuple-element.32), channel_id=1, source_target_pairs={{0,744},{1,745},{2,746},{3,747},{4,748},{5,749},{6,750},{7,751},{8... | collective-permute-start | bytes 344072 | tf_op jit(solution)/shard_map/ppermute | solution.py:402
  16.1 12.4 %collective-permute-start.1 = (bf16[9,4,512]{2,1,0:T(4,128)(2,1)S(1)}, bf16[9,4,512]{2,1,0:T(4,128)(2,1)S(1)}, u32[]{:S(2)}, u32[]{:S(2)}) collective-permute-start(bf16[9,4,512]{2,1,0:T(4,128)(2,1)S(1)} %get-tuple-element.33), channel_id=1, source_target_pairs={{0,23},{1,0},{2,1},{3,2},{4,3},{5,4},{6,5},{7,6},{8,7},{9,8},{10,9... | collective-permute-start | bytes 110600 | tf_op jit(solution)/shard_map/ppermute | solution.py:402
  25.4 5.3 %collective-permute-start.2 = (bf16[9,4,512]{2,1,0:T(4,128)(2,1)S(1)}, bf16[9,4,512]{2,1,0:T(4,128)(2,1)S(1)}, u32[]{:S(2)}, u32[]{:S(2)}) collective-permute-start(bf16[9,4,512]{2,1,0:T(4,128)(2,1)S(1)} %get-tuple-element.34), channel_id=1, source_target_pairs={{0,767},{1,744},{2,745},{3,746},{4,747},{5,748},{6,749},{7,750},{8... | collective-permute-start | bytes 110600 | tf_op jit(solution)/shard_map/ppermute | solution.py:402
  36.8 4.1 %collective-permute-start.3 = (bf16[144,2560]{1,0:T(8,128)(2,1)S(1)}, bf16[144,2560]{1,0:T(8,128)(2,1)S(1)}, u32[]{:S(2)}, u32[]{:S(2)}) collective-permute-start(bf16[144,2560]{1,0:T(8,128)(2,1)S(1)} %get-tuple-element.36.mine), channel_id=1, source_target_pairs={{0,24},{24,0},{1,25},{25,1},{2,26},{26,2},{3,27},{27,3},{4,28},{28... | collective-permute-start | bytes 2211848 | tf_op jit(solution)/shard_map/ppermute | solution.py:470
  42.4 19.9 %all-to-all-start = ((bf16[4,272,512]{2,1,0:T(8,128)(2,1)}), bf16[4,272,512]{2,1,0:T(8,128)(2,1)S(1)}, u32[]{:S(2)}, u32[]{:S(2)}) async-start(bf16[4,272,512]{2,1,0:T(8,128)(2,1)} %shard_map.122), calls=%async_computation | async-start | bytes 2228224 | tf_op jit(solution)/shard_map/all_to_all | solution.py:479
  45.9 17.2 %collective-permute-start.4 = (bf16[4,12,512]{2,1,0:T(8,128)(2,1)S(1)}, bf16[4,12,512]{2,1,0:T(8,128)(2,1)S(1)}, u32[]{:S(2)}, u32[]{:S(2)}) collective-permute-start(bf16[4,12,512]{2,1,0:T(8,128)(2,1)S(1)} %get-tuple-element.40), channel_id=1, source_target_pairs={{0,24},{1,25},{2,26},{3,27},{4,28},{5,29},{6,30},{7,31},{8,32},{9,... | collective-permute-start | bytes 147464 | tf_op jit(solution)/shard_map/ppermute | solution.py:402
  63.1 46.8 %copy-start = (bf16[8,16,512]{2,1,0:T(8,128)(2,1)S(1)}, bf16[8,16,512]{2,1,0:T(8,128)(2,1)}, u32[]{:S(2)}) copy-start(bf16[8,16,512]{2,1,0:T(8,128)(2,1)} %tok.3) | copy-start | bytes 393220
  63.1 46.8 %copy-start.1 = (bf16[8,16,512]{2,1,0:T(8,128)(2,1)S(1)}, bf16[8,16,512]{2,1,0:T(8,128)(2,1)}, u32[]{:S(2)}) copy-start(bf16[8,16,512]{2,1,0:T(8,128)(2,1)} %cot.3) | copy-start | bytes 393220
  63.1 46.8 %copy-start.2 = (f32[512]{0:T(512)S(1)}, f32[512]{0:T(512)}, u32[]{:S(2)}) copy-start(f32[512]{0:T(512)} %param.11) | copy-start | bytes 6148
  63.1 19.1 %all-to-all-start.1 = ((bf16[8,32,640]{2,1,0:T(8,128)(2,1)}), bf16[8,32,640]{2,1,0:T(8,128)(2,1)S(1)}, u32[]{:S(2)}, u32[]{:S(2)}) async-start(bf16[8,32,640]{2,1,0:T(8,128)(2,1)} %shard_map.123), calls=%async_computation.1 | async-start | bytes 655360 | tf_op jit(solution)/shard_map/all_to_all | solution.py:485
  70.9 12.5 %collective-permute-start.5 = (bf16[4,4,512]{2,1,0:T(4,128)(2,1)S(1)}, bf16[4,4,512]{2,1,0:T(4,128)(2,1)S(1)}, u32[]{:S(2)}, u32[]{:S(2)}) collective-permute-start(bf16[4,4,512]{2,1,0:T(4,128)(2,1)S(1)} %get-tuple-element.45), channel_id=1, source_target_pairs={{0,1},{1,2},{2,3},{3,4},{4,5},{5,6},{6,7},{7,8},{8,9},{9,10},{10,1... | collective-permute-start | bytes 49160 | tf_op jit(solution)/shard_map/ppermute | solution.py:402
  72.9 11.0 %collective-permute-start.6 = (bf16[4,4,512]{2,1,0:T(4,128)(2,1)S(1)}, bf16[4,4,512]{2,1,0:T(4,128)(2,1)S(1)}, u32[]{:S(2)}, u32[]{:S(2)}) collective-permute-start(bf16[4,4,512]{2,1,0:T(4,128)(2,1)S(1)} %get-tuple-element.46), channel_id=1, source_target_pairs={{0,25},{1,26},{2,27},{3,28},{4,29},{5,30},{6,31},{7,32},{8,33},{9,... | collective-permute-start | bytes 49160 | tf_op jit(solution)/shard_map/ppermute | solution.py:402
  106.7 8.9 %all-to-all-start.3 = ((f32[4,32,128]{2,1,0:T(8,128)}), f32[4,32,128]{2,1,0:T(8,128)S(1)}, u32[]{:S(2)}, u32[]{:S(2)}) async-start(f32[4,32,128]{2,1,0:T(8,128)} %get-tuple-element.51), calls=%async_computation.3 | async-start | bytes 131072 | tf_op jit(solution)/shard_map/all_to_all | solution.py:494

commit v5 on v4

--- a/solution.py
+++ b/solution.py
@@ -286,71 +286,73 @@
 
     right = jnp.concatenate([mine[0:TOKENS, 0 : 4 * D], other[0:TOKENS, 0 : 4 * D]], axis=0)
     for half in range(2):
-        at = half * 128
         qkv = dot(rows(half), right[:, 0 : 3 * D]).astype(BF16)
         proj = dot(rows(2 + half), right[:, 3 * D : 4 * D]).astype(BF16)
-        for x in range(4):
-            out[x, at : at + 128, 0:384] = qkv[:, x * 384 : x * 384 + 384]
-            out[x, at : at + 128, 384:512] = proj[:, x * 128 : x * 128 + 128]
+        for k in range(4):
+            for x in range(4):
+                to = (half * 4 + k) * 4 + x
+                at = k * 32
+                for block in range(3):
+                    lane = x * 384 + block * 128
+                    out[to, block * 32 : block * 32 + 32, :] = qkv[at : at + 32, lane : lane + 128]
+                out[to, 96:128, :] = proj[at : at + 32, x * 128 : x * 128 + 128]
+    first = lax.axis_index("core") == 0
     small = mine[TOKENS : TOKENS + 16, 0:1536].astype(F32) + other[TOKENS : TOKENS + 16, 0:1536].astype(F32)
     table = small[:, 0:256] + small[:, 256:512]
+    table = jnp.where(first, table[0:8], table[8:16])
     gain = small[0:8, 512:1024] + small[0:8, 1024:1536]
+    gain = jnp.where(first, gain[:, 0:256], gain[:, 256:512])
     for x in range(4):
+        lane = (x // 2) * 128
+        piece = gain[:, lane : lane + 128]
+        if x % 2 == 1:
+            piece = pltpu.roll(piece, 64, 1)
         part = jnp.concatenate(
-            [
-                table[4 * x : 4 * x + 4, 0:128],
-                table[4 * x : 4 * x + 4, 128:256],
-                gain[:, x * 128 : x * 128 + 128],
-            ],
-            axis=0,
-        )
-        high, low = split_high_low(part)
-        out[x, 256:272, 0:128] = high
-        out[x, 256:272, 128:256] = low
-        out[x, 256:272, 256:512] = jnp.zeros((16, 256), BF16)
-
-
-def across_sum_kernel(parts, out):
-    small = jnp.sum(parts[:, 256:272, 0:256].astype(F32), axis=0)
-    high, low = split_high_low(small[:, 0:128] + small[:, 128:256])
-    both = jnp.concatenate([high, low], axis=0)
-    for y in range(8):
-        total = jnp.sum(parts[:, y * 32 : y * 32 + 32, :].astype(F32), axis=0)
-        out[y, :, 0:512] = total.astype(BF16)
-        out[y, :, 512:640] = both
+            [table[2 * x : 2 * x + 2, 0:128], table[2 * x : 2 * x + 2, 128:256], piece[0:4]], axis=0
+        ).astype(BF16)
+        for y in range(8):
+            out[y * 4 + x, 128:136, :] = part
 
 
 def plane_sum_kernel(parts, out):
     total = jnp.sum(parts[...].astype(F32), axis=0)
-    small = (total[0:16, 512:640] + total[16:32, 512:640]).astype(BF16)
+    left_half = iota((8, 128), 1) < 64
+    small = total[128:136]
     for zh in range(2):
-        rows = total[zh * 16 : zh * 16 + 16]
-        proj = rows[:, 384:512].astype(BF16)
+        proj = total[96 + zh * 16 : 112 + zh * 16].astype(BF16)
         for zl in range(6):
-            lane = (zl // 2) * 128
-            qkv = rows[:, lane : lane + 128]
-            if zl % 2 == 1:
-                qkv = pltpu.roll(qkv, 64, 1)
-            out[zh * 6 + zl, :, 0:128] = proj
-            out[zh * 6 + zl, :, 128:256] = qkv.astype(BF16)
-            out[zh * 6 + zl, :, 256:384] = small
+            at = (zl // 2) * 32 + zh * 16
+            upper, lower = total[at : at + 8], total[at + 8 : at + 16]
+            if zl % 2 == 0:
+                lower = pltpu.roll(lower, 64, 1)
+            else:
+                upper = pltpu.roll(upper, 64, 1)
+            qkv = jnp.where(left_half, upper, lower)
+            out[zh * 6 + zl, 0:16, :] = proj
+            out[zh * 6 + zl, 16:32, :] = jnp.concatenate([qkv, small], axis=0).astype(BF16)
 
 
 def line_sum_kernel(parts, qkv, out):
     total = jnp.sum(parts[...].astype(F32), axis=0)
-    qkv[...] = total[:, 128:192]
+    qkv[0:8, :] = total[16:24, 0:64]
+    qkv[8:16, :] = pltpu.roll(total[16:24], 64, 1)[:, 0:64]
+    for to in range(8):
+        out[to, 0:16, :] = total[0:16]
+        out[to, 16:24, :] = total[24:32]
+
+
+def finish_kernel(parts, proj, gain, table):
+    core = lax.axis_index("core")
     for x in range(4):
-        out[x, 0:16, :] = total[:, 0:128]
-        out[x, 16:32, :] = total[:, 256:384]
-
-
-def finish_kernel(parts, proj, gain, table):
+        proj[:, x * 128 : x * 128 + 128] = parts[core * 4 + x, 0:16, :]
+    left_half = iota((1, 128), 1) < 64
     low, high = [], []
-    for x in range(4):
-        proj[:, x * 128 : x * 128 + 128] = parts[x, 0:16, :]
-        gain[:, x * 128 : x * 128 + 128] = parts[x, 24:25, :]
-        low.append(parts[x, 16:20, :])
-        high.append(parts[x, 20:24, :])
+    for k in range(8):
+        low.append(parts[k, 16:18, :])
+        high.append(parts[k, 18:20, :])
+    for k in range(4):
+        second = pltpu.roll(parts[2 * k + 1, 16:24, :], 64, 1)[4:5]
+        gain[:, k * 128 : k * 128 + 128] = jnp.where(left_half, parts[2 * k, 20:21, :], second)
     table[:, 0:128] = jnp.concatenate(low, axis=0)
     table[:, 128:NBIAS] = jnp.concatenate(high, axis=0)[:, 0 : NBIAS - 128]
 
@@ -470,28 +472,27 @@
     other = lax.ppermute(send, "core", [(0, 1), (1, 0)])
     products = call(
         product_kernel,
-        shape((4, 272, D), BF16),
+        shape((32, 136, 128), BF16),
         (send, other, keep),
         flops=1 << 29,
         moved=1 << 21,
     )
-    products, down_grad = lax.optimization_barrier((products, down_grad))
-    across = lax.all_to_all(products, "x", 0, 0)
+    products, down_grad, right_grad, diag_grad = lax.optimization_barrier(
+        (products, down_grad, right_grad, diag_grad)
+    )
+    planes = lax.all_to_all(products, ("y", "x"), 0, 0)
     above_grad = neighbour(down_grad, 1, 0)
-    halves = call(across_sum_kernel, shape((8, 32, 640), BF16), (across,), moved=1 << 21)
-    halves, above_grad, right_grad, diag_grad = lax.optimization_barrier(
-        (halves, above_grad, right_grad, diag_grad)
-    )
-    planes = lax.all_to_all(halves, "y", 0, 0)
     left_grad = neighbour(right_grad, 0, 1)
     corner_grad = neighbour(diag_grad, 1, 1)
-    chunks = call(plane_sum_kernel, shape((12, 16, 384), BF16), (planes,), moved=1 << 21)
-    chunks, left_grad, corner_grad = lax.optimization_barrier((chunks, left_grad, corner_grad))
+    chunks = call(plane_sum_kernel, shape((12, 32, 128), BF16), (planes,), moved=1 << 21)
+    chunks, above_grad, left_grad, corner_grad = lax.optimization_barrier(
+        (chunks, above_grad, left_grad, corner_grad)
+    )
     lines = lax.all_to_all(chunks, ("zh", "zl"), 0, 0)
     grad_qkv, finals = call(
-        line_sum_kernel, [shape((16, 64), F32), shape((4, 32, 128), F32)], (lines,), moved=1 << 18
-    )
-    finals = lax.all_to_all(finals, "x", 0, 0)
+        line_sum_kernel, [shape((16, 64), F32), shape((8, 24, 128), F32)], (lines,), moved=1 << 18
+    )
+    finals = lax.all_to_all(finals, ("core", "x"), 0, 0)
     grad_tokens = call(
         token_kernel,
         shape((8, 16, D), BF16),

time: 117 us -> 114 us (0.974)
  the two profiles are of different devices: /device:TPU:8 before, /device:TPU:1 now
where the time goes in v5:
time: 114 us
  starting transfers between devices  59.9 us (53%)
  waiting for transfers between devices  23.3 us (20%)
  blocking collectives  17.3 us (15%)
  Pallas kernels  12.4 us (11%)
    ppermute x6, starting transfers between devices, neighbour(): return lax.ppermute(value, ROWS + COLS, pairs)  42.8 us
    all_to_all x1, waiting for transfers between devices, local(): planes = lax.all_to_all(products, ('y', 'x'), 0, 0)  17.4 us
    all_to_all x1, blocking collectives, local(): lines = lax.all_to_all(chunks, ('zh', 'zl'), 0, 0)  17.3 us
    pallas_call x8, Pallas kernels, call(): pl.pallas_call(kernel, in_specs=[pl.BlockSpec(memory_space=pltpu.HBM if k...  12.4 us
    all_to_all x1, starting transfers between devices, local(): finals = lax.all_to_all(finals, ('core', 'x'), 0, 0)  8.36 us
    all_to_all x1, starting transfers between devices, local(): planes = lax.all_to_all(products, ('y', 'x'), 0, 0)  5.52 us
    all_to_all x1, waiting for transfers between devices, local(): finals = lax.all_to_all(finals, ('core', 'x'), 0, 0)  4.03 us
    ppermute x1, starting transfers between devices, local(): other = lax.ppermute(send, 'core', [(0, 1), (1, 0)])  3.23 us
  transfers between devices with their start and end apart: 9, of which 3 were waited for; matrix products, arithmetic and copies ran while one was open for 0% of the time, Pallas kernels for 2%

profile of v5, /device:TPU:1, one launch (start us, length us, event | category | flops | bytes accessed | tf_op | source)
XLA Modules:
  0.0 113.8 jit_solution(14783912293369832496)
XLA Ops:
  0.6 1.0 shard_map.120
  1.7 12.4 %collective-permute-start = (bf16[112,512]{1,0:T(8,128)(2,1)S(1)}, bf16[112,512]{1,0:T(8,128)(2,1)S(1)}, u32[]{:S(2)}, u32[]{:S(2)}) collective-permute-start(bf16[112,512]{1,0:T(8,128)(2,1)S(1)} %get-tuple-element.31), channel_id=1, source_target_pairs={{0,744},{1,745},{2,746},{3,747},{4,748},{5,749},{6,750},{7,751},{8... | collective-permute-start | bytes 344072 | tf_op jit(solution)/shard_map/ppermute | solution.py:404
  14.1 5.6 %collective-permute-start.1 = (bf16[9,4,512]{2,1,0:T(4,128)(2,1)S(1)}, bf16[9,4,512]{2,1,0:T(4,128)(2,1)S(1)}, u32[]{:S(2)}, u32[]{:S(2)}) collective-permute-start(bf16[9,4,512]{2,1,0:T(4,128)(2,1)S(1)} %get-tuple-element.32), channel_id=1, source_target_pairs={{0,23},{1,0},{2,1},{3,2},{4,3},{5,4},{6,5},{7,6},{8,7},{9,8},{10,9... | collective-permute-start | bytes 110600 | tf_op jit(solution)/shard_map/ppermute | solution.py:404
  19.7 12.8 %collective-permute-start.2 = (bf16[9,4,512]{2,1,0:T(4,128)(2,1)S(1)}, bf16[9,4,512]{2,1,0:T(4,128)(2,1)S(1)}, u32[]{:S(2)}, u32[]{:S(2)}) collective-permute-start(bf16[9,4,512]{2,1,0:T(4,128)(2,1)S(1)} %get-tuple-element.33), channel_id=1, source_target_pairs={{0,767},{1,744},{2,745},{3,746},{4,747},{5,748},{6,749},{7,750},{8... | collective-permute-start | bytes 110600 | tf_op jit(solution)/shard_map/ppermute | solution.py:404
  32.6 1.2 %shard_map.119 = (f32[16,64,128]{2,1,0:T(8,128)S(1)}, s32[32,128]{1,0:T(8,128)S(1)}) custom-call(f32[16,225]{1,0:T(8,128)} %bitcast.6, s32[64,64]{1,0:T(8,128)} %bucket_far.1), custom_call_target="tpu_custom_call" | custom-call | bytes 8388608 | tf_op jit(solution)/shard_map/pallas_call | solution.py:385
  33.8 0.0 collective-permute-done.1.left
  33.8 0.0 collective-permute-done.2.diag
  33.8 0.0 collective-permute-done.up
  33.8 6.2 %shard_map.121 = (bf16[144,2560]{1,0:T(8,128)(2,1)S(1)}, bf16[128,512]{1,0:T(8,128)(2,1)S(1)}, f32[4,12,512]{2,1,0:T(8,128)S(1)}, bf16[4,12,512]{2,1,0:T(8,128)(...) custom-call(bf16[8,16,512]{2,1,0:T(8,128)(2,1)} %tok.3, bf16[8,16,512]{2,1,0:T(8,128)(2,1)} %cot.3, ...), custom_call_target="tpu_custom_call" | custom-call | flops 1073741824 | bytes 8388608 | tf_op jit(solution)/shard_map/pallas_call | solution.py:385
  40.0 3.2 %collective-permute-start.3 = (bf16[144,2560]{1,0:T(8,128)(2,1)S(1)}, bf16[144,2560]{1,0:T(8,128)(2,1)S(1)}, u32[]{:S(2)}, u32[]{:S(2)}) collective-permute-start(bf16[144,2560]{1,0:T(8,128)(2,1)S(1)} %get-tuple-element.35.mine), channel_id=1, source_target_pairs={{0,24},{24,0},{1,25},{25,1},{2,26},{26,2},{3,27},{27,3},{4,28},{28... | collective-permute-start | bytes 2211848 | tf_op jit(solution)/shard_map/ppermute | solution.py:472
  43.3 1.8 %collective-permute-done.3.other = bf16[144,2560]{1,0:T(8,128)(2,1)S(1)} collective-permute-done((bf16[144,2560]{1,0:T(8,128)(2,1)S(1)}, bf16[144,2560]{1,0:T(8,128)(2,1)S(1)}, u32[]{:S(2)}, u32[]{:S(2)}) %collective-permute-start.3) | collective-permute-done | bytes 737312 | tf_op jit(solution)/shard_map/ppermute | solution.py:472
  45.1 1.5 %shard_map.122 = bf16[32,136,128]{2,1,0:T(8,128)(2,1)} custom-call(bf16[144,2560]{1,0:T(8,128)(2,1)S(1)} %get-tuple-element.35.mine, bf16[144,2560]{1,0:T(8,128)(2,1)S(1)} %collective-permute-done.3.other, bf16[128,512]{1,0:T(8,128)(2,1)S(1)} %get-tuple-element.36.keep), custom_call_target="tpu_custom_call" | custom-call | flops 536870912 | bytes 2097152 | tf_op jit(solution)/shard_map/pallas_call | solution.py:385
  46.6 5.5 %all-to-all-start = ((bf16[32,136,128]{2,1,0:T(8,128)(2,1)}), bf16[32,136,128]{2,1,0:T(8,128)(2,1)S(1)}, u32[]{:S(2)}, u32[]{:S(2)}) async-start(bf16[32,136,128]{2,1,0:T(8,128)(2,1)} %shard_map.122), calls=%async_computation | async-start | bytes 2228224 | tf_op jit(solution)/shard_map/all_to_all | solution.py:483
  52.1 0.0 copy-start
  52.1 0.0 copy-start.1
  52.1 0.0 copy-start.2
  52.1 8.1 %collective-permute-start.4 = (bf16[4,12,512]{2,1,0:T(8,128)(2,1)S(1)}, bf16[4,12,512]{2,1,0:T(8,128)(2,1)S(1)}, u32[]{:S(2)}, u32[]{:S(2)}) collective-permute-start(bf16[4,12,512]{2,1,0:T(8,128)(2,1)S(1)} %get-tuple-element.41), channel_id=1, source_target_pairs={{0,24},{1,25},{2,26},{3,27},{4,28},{5,29},{6,30},{7,31},{8,32},{9,... | collective-permute-start | bytes 147464 | tf_op jit(solution)/shard_map/ppermute | solution.py:404
  60.2 1.9 %collective-permute-start.5 = (bf16[4,4,512]{2,1,0:T(4,128)(2,1)S(1)}, bf16[4,4,512]{2,1,0:T(4,128)(2,1)S(1)}, u32[]{:S(2)}, u32[]{:S(2)}) collective-permute-start(bf16[4,4,512]{2,1,0:T(4,128)(2,1)S(1)} %get-tuple-element.42), channel_id=1, source_target_pairs={{0,1},{1,2},{2,3},{3,4},{4,5},{5,6},{6,7},{7,8},{8,9},{9,10},{10,1... | collective-permute-start | bytes 49160 | tf_op jit(solution)/shard_map/ppermute | solution.py:404
  62.2 1.9 %collective-permute-start.6 = (bf16[4,4,512]{2,1,0:T(4,128)(2,1)S(1)}, bf16[4,4,512]{2,1,0:T(4,128)(2,1)S(1)}, u32[]{:S(2)}, u32[]{:S(2)}) collective-permute-start(bf16[4,4,512]{2,1,0:T(4,128)(2,1)S(1)} %get-tuple-element.43), channel_id=1, source_target_pairs={{0,25},{1,26},{2,27},{3,28},{4,29},{5,30},{6,31},{7,32},{8,33},{9,... | collective-permute-start | bytes 49160 | tf_op jit(solution)/shard_map/ppermute | solution.py:404
  64.1 17.4 %all-to-all-done.parts = bf16[32,136,128]{2,1,0:T(8,128)(2,1)S(1)} async-done(((bf16[32,136,128]{2,1,0:T(8,128)(2,1)}), bf16[32,136,128]{2,1,0:T(8,128)(2,1)S(1)}, u32[]{:S(2)}, u32[]{:S(2)}) %all-to-all-start) | async-done | bytes 1114144 | tf_op jit(solution)/shard_map/all_to_all | solution.py:483
  81.5 0.2 shard_map.123
  81.7 0.0 collective-permute-done.5.left
  81.7 0.0 collective-permute-done.6.diag
  81.7 0.0 collective-permute-done.4.above
  81.7 17.3 %all_to_all.15.parts = bf16[12,32,128]{2,1,0:T(8,128)(2,1)S(1)} all-to-all(bf16[12,32,128]{2,1,0:T(8,128)(2,1)S(1)} %shard_map.123), channel_id=1, replica_groups=mesh['y'=8,'zh'=2,'core'=2,'x'=4,'zl'=6] {'zh','zl'}, dimensions={0} | all-to-all | bytes 196608 | tf_op jit(solution)/shard_map/all_to_all | solution.py:491
  99.0 0.7 shard_map.125
  99.7 8.4 %all-to-all-start.2 = ((f32[8,24,128]{2,1,0:T(8,128)}), f32[8,24,128]{2,1,0:T(8,128)S(1)}, u32[]{:S(2)}, u32[]{:S(2)}) async-start(f32[8,24,128]{2,1,0:T(8,128)} %get-tuple-element.49), calls=%async_computation.2 | async-start | bytes 196608 | tf_op jit(solution)/shard_map/all_to_all | solution.py:495
  108.1 0.0 copy-done
  108.1 0.0 copy-done.1
  108.1 0.0 copy-done.2
  108.1 1.0 shard_map.124
  109.0 4.0 %all-to-all-done.2.parts = f32[8,24,128]{2,1,0:T(8,128)S(1)} async-done(((f32[8,24,128]{2,1,0:T(8,128)}), f32[8,24,128]{2,1,0:T(8,128)S(1)}, u32[]{:S(2)}, u32[]{:S(2)}) %all-to-all-start.2) | async-done | bytes 98336 | tf_op jit(solution)/shard_map/all_to_all | solution.py:495
  113.1 0.7 shard_map.126
Async XLA Ops:
  1.7 32.2 %collective-permute-start = (bf16[112,512]{1,0:T(8,128)(2,1)S(1)}, bf16[112,512]{1,0:T(8,128)(2,1)S(1)}, u32[]{:S(2)}, u32[]{:S(2)}) collective-permute-start(bf16[112,512]{1,0:T(8,128)(2,1)S(1)} %get-tuple-element.31), channel_id=1, source_target_pairs={{0,744},{1,745},{2,746},{3,747},{4,748},{5,749},{6,750},{7,751},{8... | collective-permute-start | bytes 344072 | tf_op jit(solution)/shard_map/ppermute | solution.py:404
  14.1 19.7 %collective-permute-start.1 = (bf16[9,4,512]{2,1,0:T(4,128)(2,1)S(1)}, bf16[9,4,512]{2,1,0:T(4,128)(2,1)S(1)}, u32[]{:S(2)}, u32[]{:S(2)}) collective-permute-start(bf16[9,4,512]{2,1,0:T(4,128)(2,1)S(1)} %get-tuple-element.32), channel_id=1, source_target_pairs={{0,23},{1,0},{2,1},{3,2},{4,3},{5,4},{6,5},{7,6},{8,7},{9,8},{10,9... | collective-permute-start | bytes 110600 | tf_op jit(solution)/shard_map/ppermute | solution.py:404
  19.7 14.1 %collective-permute-start.2 = (bf16[9,4,512]{2,1,0:T(4,128)(2,1)S(1)}, bf16[9,4,512]{2,1,0:T(4,128)(2,1)S(1)}, u32[]{:S(2)}, u32[]{:S(2)}) collective-permute-start(bf16[9,4,512]{2,1,0:T(4,128)(2,1)S(1)} %get-tuple-element.33), channel_id=1, source_target_pairs={{0,767},{1,744},{2,745},{3,746},{4,747},{5,748},{6,749},{7,750},{8... | collective-permute-start | bytes 110600 | tf_op jit(solution)/shard_map/ppermute | solution.py:404
  40.0 5.1 %collective-permute-start.3 = (bf16[144,2560]{1,0:T(8,128)(2,1)S(1)}, bf16[144,2560]{1,0:T(8,128)(2,1)S(1)}, u32[]{:S(2)}, u32[]{:S(2)}) collective-permute-start(bf16[144,2560]{1,0:T(8,128)(2,1)S(1)} %get-tuple-element.35.mine), channel_id=1, source_target_pairs={{0,24},{24,0},{1,25},{25,1},{2,26},{26,2},{3,27},{27,3},{4,28},{28... | collective-permute-start | bytes 2211848 | tf_op jit(solution)/shard_map/ppermute | solution.py:472
  46.6 34.9 %all-to-all-start = ((bf16[32,136,128]{2,1,0:T(8,128)(2,1)}), bf16[32,136,128]{2,1,0:T(8,128)(2,1)S(1)}, u32[]{:S(2)}, u32[]{:S(2)}) async-start(bf16[32,136,128]{2,1,0:T(8,128)(2,1)} %shard_map.122), calls=%async_computation | async-start | bytes 2228224 | tf_op jit(solution)/shard_map/all_to_all | solution.py:483
  52.1 56.0 %copy-start = (bf16[8,16,512]{2,1,0:T(8,128)(2,1)S(1)}, bf16[8,16,512]{2,1,0:T(8,128)(2,1)}, u32[]{:S(2)}) copy-start(bf16[8,16,512]{2,1,0:T(8,128)(2,1)} %tok.3) | copy-start | bytes 393220
  52.1 56.0 %copy-start.1 = (bf16[8,16,512]{2,1,0:T(8,128)(2,1)S(1)}, bf16[8,16,512]{2,1,0:T(8,128)(2,1)}, u32[]{:S(2)}) copy-start(bf16[8,16,512]{2,1,0:T(8,128)(2,1)} %cot.3) | copy-start | bytes 393220
  52.1 56.0 %copy-start.2 = (f32[512]{0:T(512)S(1)}, f32[512]{0:T(512)}, u32[]{:S(2)}) copy-start(f32[512]{0:T(512)} %param.11) | copy-start | bytes 6148
  52.1 29.6 %collective-permute-start.4 = (bf16[4,12,512]{2,1,0:T(8,128)(2,1)S(1)}, bf16[4,12,512]{2,1,0:T(8,128)(2,1)S(1)}, u32[]{:S(2)}, u32[]{:S(2)}) collective-permute-start(bf16[4,12,512]{2,1,0:T(8,128)(2,1)S(1)} %get-tuple-element.41), channel_id=1, source_target_pairs={{0,24},{1,25},{2,26},{3,27},{4,28},{5,29},{6,30},{7,31},{8,32},{9,... | collective-permute-start | bytes 147464 | tf_op jit(solution)/shard_map/ppermute | solution.py:404
  60.2 21.4 %collective-permute-start.5 = (bf16[4,4,512]{2,1,0:T(4,128)(2,1)S(1)}, bf16[4,4,512]{2,1,0:T(4,128)(2,1)S(1)}, u32[]{:S(2)}, u32[]{:S(2)}) collective-permute-start(bf16[4,4,512]{2,1,0:T(4,128)(2,1)S(1)} %get-tuple-element.42), channel_id=1, source_target_pairs={{0,1},{1,2},{2,3},{3,4},{4,5},{5,6},{6,7},{7,8},{8,9},{9,10},{10,1... | collective-permute-start | bytes 49160 | tf_op jit(solution)/shard_map/ppermute | solution.py:404
  62.2 19.5 %collective-permute-start.6 = (bf16[4,4,512]{2,1,0:T(4,128)(2,1)S(1)}, bf16[4,4,512]{2,1,0:T(4,128)(2,1)S(1)}, u32[]{:S(2)}, u32[]{:S(2)}) collective-permute-start(bf16[4,4,512]{2,1,0:T(4,128)(2,1)S(1)} %get-tuple-element.43), channel_id=1, source_target_pairs={{0,25},{1,26},{2,27},{3,28},{4,29},{5,30},{6,31},{7,32},{8,33},{9,... | collective-permute-start | bytes 49160 | tf_op jit(solution)/shard_map/ppermute | solution.py:404
  99.7 13.4 %all-to-all-start.2 = ((f32[8,24,128]{2,1,0:T(8,128)}), f32[8,24,128]{2,1,0:T(8,128)S(1)}, u32[]{:S(2)}, u32[]{:S(2)}) async-start(f32[8,24,128]{2,1,0:T(8,128)} %get-tuple-element.49), calls=%async_computation.2 | async-start | bytes 196608 | tf_op jit(solution)/shard_map/all_to_all | solution.py:495

commit v6 on v5

--- a/solution.py
+++ b/solution.py
@@ -290,7 +290,7 @@
         proj = dot(rows(2 + half), right[:, 3 * D : 4 * D]).astype(BF16)
         for k in range(4):
             for x in range(4):
-                to = (half * 4 + k) * 4 + x
+                to = x * 8 + half * 4 + k
                 at = k * 32
                 for block in range(3):
                     lane = x * 384 + block * 128
@@ -311,7 +311,7 @@
             [table[2 * x : 2 * x + 2, 0:128], table[2 * x : 2 * x + 2, 128:256], piece[0:4]], axis=0
         ).astype(BF16)
         for y in range(8):
-            out[y * 4 + x, 128:136, :] = part
+            out[x * 8 + y, 128:136, :] = part
 
 
 def plane_sum_kernel(parts, out):
@@ -420,8 +420,8 @@
         remain=(0, 1, 2),
     )
     up = neighbour(to_up, -1, 0)
+    left = neighbour(to_left, 0, -1)
     diag = neighbour(to_diag, -1, -1)
-    left = neighbour(to_left, 0, -1)
     bias, bucket2 = call(
         bias_kernel,
         [
@@ -480,7 +480,7 @@
     products, down_grad, right_grad, diag_grad = lax.optimization_barrier(
         (products, down_grad, right_grad, diag_grad)
     )
-    planes = lax.all_to_all(products, ("y", "x"), 0, 0)
+    planes = lax.all_to_all(products, ("x", "y"), 0, 0)
     above_grad = neighbour(down_grad, 1, 0)
     left_grad = neighbour(right_grad, 0, 1)
     corner_grad = neighbour(diag_grad, 1, 1)

time: 114 us -> 114 us (level)
  waiting for transfers between devices: 23.3 us -> 21 us
    all_to_all x1, waiting for transfers between devices: 17.4 us -> 15.1 us  [local(): planes = lax.all_to_all(products, ('x', 'y'), 0, 0)]
where the time goes in v6:
time: 114 us; the launch traced here: 113 us
  starting transfers between devices  60.8 us (53%)
  waiting for transfers between devices  21 us (18%)
  blocking collectives  17.8 us (16%)
  Pallas kernels  12.4 us (11%)
    ppermute x6, starting transfers between devices, neighbour(): return lax.ppermute(value, ROWS + COLS, pairs)  42.8 us
    all_to_all x1, blocking collectives, local(): lines = lax.all_to_all(chunks, ('zh', 'zl'), 0, 0)  17.8 us
    all_to_all x1, waiting for transfers between devices, local(): planes = lax.all_to_all(products, ('x', 'y'), 0, 0)  15.1 us
    pallas_call x8, Pallas kernels, call(): pl.pallas_call(kernel, in_specs=[pl.BlockSpec(memory_space=pltpu.HBM if k...  12.4 us
    all_to_all x1, starting transfers between devices, local(): finals = lax.all_to_all(finals, ('core', 'x'), 0, 0)  9.28 us
    all_to_all x1, starting transfers between devices, local(): planes = lax.all_to_all(products, ('x', 'y'), 0, 0)  5.52 us
    all_to_all x1, waiting for transfers between devices, local(): finals = lax.all_to_all(finals, ('core', 'x'), 0, 0)  4.02 us
    ppermute x1, starting transfers between devices, local(): other = lax.ppermute(send, 'core', [(0, 1), (1, 0)])  3.23 us
  transfers between devices with their start and end apart: 9, of which 3 were waited for; matrix products, arithmetic and copies ran while one was open for 0% of the time, Pallas kernels for 2%

profile of v6, /device:TPU:1, one launch (start us, length us, event | category | flops | bytes accessed | tf_op | source)
XLA Modules:
  0.0 112.9 jit_solution(7690830381720753796)
XLA Ops:
  0.6 1.0 shard_map.120
  1.7 12.4 %collective-permute-start = (bf16[112,512]{1,0:T(8,128)(2,1)S(1)}, bf16[112,512]{1,0:T(8,128)(2,1)S(1)}, u32[]{:S(2)}, u32[]{:S(2)}) collective-permute-start(bf16[112,512]{1,0:T(8,128)(2,1)S(1)} %get-tuple-element.31), channel_id=1, source_target_pairs={{0,744},{1,745},{2,746},{3,747},{4,748},{5,749},{6,750},{7,751},{8... | collective-permute-start | bytes 344072 | tf_op jit(solution)/shard_map/ppermute | solution.py:404
  14.1 5.6 %collective-permute-start.1 = (bf16[9,4,512]{2,1,0:T(4,128)(2,1)S(1)}, bf16[9,4,512]{2,1,0:T(4,128)(2,1)S(1)}, u32[]{:S(2)}, u32[]{:S(2)}) collective-permute-start(bf16[9,4,512]{2,1,0:T(4,128)(2,1)S(1)} %get-tuple-element.32), channel_id=1, source_target_pairs={{0,23},{1,0},{2,1},{3,2},{4,3},{5,4},{6,5},{7,6},{8,7},{9,8},{10,9... | collective-permute-start | bytes 110600 | tf_op jit(solution)/shard_map/ppermute | solution.py:404
  19.7 12.8 %collective-permute-start.2 = (bf16[9,4,512]{2,1,0:T(4,128)(2,1)S(1)}, bf16[9,4,512]{2,1,0:T(4,128)(2,1)S(1)}, u32[]{:S(2)}, u32[]{:S(2)}) collective-permute-start(bf16[9,4,512]{2,1,0:T(4,128)(2,1)S(1)} %get-tuple-element.33), channel_id=1, source_target_pairs={{0,767},{1,744},{2,745},{3,746},{4,747},{5,748},{6,749},{7,750},{8... | collective-permute-start | bytes 110600 | tf_op jit(solution)/shard_map/ppermute | solution.py:404
  32.6 1.2 %shard_map.119 = (f32[16,64,128]{2,1,0:T(8,128)S(1)}, s32[32,128]{1,0:T(8,128)S(1)}) custom-call(f32[16,225]{1,0:T(8,128)} %bitcast.6, s32[64,64]{1,0:T(8,128)} %bucket_far.1), custom_call_target="tpu_custom_call" | custom-call | bytes 8388608 | tf_op jit(solution)/shard_map/pallas_call | solution.py:385
  33.8 0.0 collective-permute-done.1.left
  33.8 0.0 collective-permute-done.2.diag
  33.8 0.0 collective-permute-done.up
  33.8 6.2 %shard_map.121 = (bf16[144,2560]{1,0:T(8,128)(2,1)S(1)}, bf16[128,512]{1,0:T(8,128)(2,1)S(1)}, f32[4,12,512]{2,1,0:T(8,128)S(1)}, bf16[4,12,512]{2,1,0:T(8,128)(...) custom-call(bf16[8,16,512]{2,1,0:T(8,128)(2,1)} %tok.3, bf16[8,16,512]{2,1,0:T(8,128)(2,1)} %cot.3, ...), custom_call_target="tpu_custom_call" | custom-call | flops 1073741824 | bytes 8388608 | tf_op jit(solution)/shard_map/pallas_call | solution.py:385
  40.0 3.2 %collective-permute-start.3 = (bf16[144,2560]{1,0:T(8,128)(2,1)S(1)}, bf16[144,2560]{1,0:T(8,128)(2,1)S(1)}, u32[]{:S(2)}, u32[]{:S(2)}) collective-permute-start(bf16[144,2560]{1,0:T(8,128)(2,1)S(1)} %get-tuple-element.35.mine), channel_id=1, source_target_pairs={{0,24},{24,0},{1,25},{25,1},{2,26},{26,2},{3,27},{27,3},{4,28},{28... | collective-permute-start | bytes 2211848 | tf_op jit(solution)/shard_map/ppermute | solution.py:472
  43.3 1.8 %collective-permute-done.3.other = bf16[144,2560]{1,0:T(8,128)(2,1)S(1)} collective-permute-done((bf16[144,2560]{1,0:T(8,128)(2,1)S(1)}, bf16[144,2560]{1,0:T(8,128)(2,1)S(1)}, u32[]{:S(2)}, u32[]{:S(2)}) %collective-permute-start.3) | collective-permute-done | bytes 737312 | tf_op jit(solution)/shard_map/ppermute | solution.py:472
  45.1 1.5 %shard_map.122 = bf16[32,136,128]{2,1,0:T(8,128)(2,1)} custom-call(bf16[144,2560]{1,0:T(8,128)(2,1)S(1)} %get-tuple-element.35.mine, bf16[144,2560]{1,0:T(8,128)(2,1)S(1)} %collective-permute-done.3.other, bf16[128,512]{1,0:T(8,128)(2,1)S(1)} %get-tuple-element.36.keep), custom_call_target="tpu_custom_call" | custom-call | flops 536870912 | bytes 2097152 | tf_op jit(solution)/shard_map/pallas_call | solution.py:385
  46.6 5.5 %all-to-all-start = ((bf16[32,136,128]{2,1,0:T(8,128)(2,1)}), bf16[32,136,128]{2,1,0:T(8,128)(2,1)S(1)}, u32[]{:S(2)}, u32[]{:S(2)}) async-start(bf16[32,136,128]{2,1,0:T(8,128)(2,1)} %shard_map.122), calls=%async_computation | async-start | bytes 2228224 | tf_op jit(solution)/shard_map/all_to_all | solution.py:483
  52.1 0.0 copy-start
  52.1 0.0 copy-start.1
  52.1 0.0 copy-start.2
  52.1 8.1 %collective-permute-start.4 = (bf16[4,12,512]{2,1,0:T(8,128)(2,1)S(1)}, bf16[4,12,512]{2,1,0:T(8,128)(2,1)S(1)}, u32[]{:S(2)}, u32[]{:S(2)}) collective-permute-start(bf16[4,12,512]{2,1,0:T(8,128)(2,1)S(1)} %get-tuple-element.41), channel_id=1, source_target_pairs={{0,24},{1,25},{2,26},{3,27},{4,28},{5,29},{6,30},{7,31},{8,32},{9,... | collective-permute-start | bytes 147464 | tf_op jit(solution)/shard_map/ppermute | solution.py:404
  60.2 1.9 %collective-permute-start.5 = (bf16[4,4,512]{2,1,0:T(4,128)(2,1)S(1)}, bf16[4,4,512]{2,1,0:T(4,128)(2,1)S(1)}, u32[]{:S(2)}, u32[]{:S(2)}) collective-permute-start(bf16[4,4,512]{2,1,0:T(4,128)(2,1)S(1)} %get-tuple-element.42), channel_id=1, source_target_pairs={{0,1},{1,2},{2,3},{3,4},{4,5},{5,6},{6,7},{7,8},{8,9},{9,10},{10,1... | collective-permute-start | bytes 49160 | tf_op jit(solution)/shard_map/ppermute | solution.py:404
  62.2 1.9 %collective-permute-start.6 = (bf16[4,4,512]{2,1,0:T(4,128)(2,1)S(1)}, bf16[4,4,512]{2,1,0:T(4,128)(2,1)S(1)}, u32[]{:S(2)}, u32[]{:S(2)}) collective-permute-start(bf16[4,4,512]{2,1,0:T(4,128)(2,1)S(1)} %get-tuple-element.43), channel_id=1, source_target_pairs={{0,25},{1,26},{2,27},{3,28},{4,29},{5,30},{6,31},{7,32},{8,33},{9,... | collective-permute-start | bytes 49160 | tf_op jit(solution)/shard_map/ppermute | solution.py:404
  64.1 15.1 %all-to-all-done.parts = bf16[32,136,128]{2,1,0:T(8,128)(2,1)S(1)} async-done(((bf16[32,136,128]{2,1,0:T(8,128)(2,1)}), bf16[32,136,128]{2,1,0:T(8,128)(2,1)S(1)}, u32[]{:S(2)}, u32[]{:S(2)}) %all-to-all-start) | async-done | bytes 1114144 | tf_op jit(solution)/shard_map/all_to_all | solution.py:483
  79.2 0.2 shard_map.123
  79.4 0.0 collective-permute-done.5.left
  79.4 0.0 collective-permute-done.6.diag
  79.4 0.0 collective-permute-done.4.above
  79.4 17.8 %all_to_all.15.parts = bf16[12,32,128]{2,1,0:T(8,128)(2,1)S(1)} all-to-all(bf16[12,32,128]{2,1,0:T(8,128)(2,1)S(1)} %shard_map.123), channel_id=1, replica_groups=mesh['y'=8,'zh'=2,'core'=2,'x'=4,'zl'=6] {'zh','zl'}, dimensions={0} | all-to-all | bytes 196608 | tf_op jit(solution)/shard_map/all_to_all | solution.py:491
  97.3 0.7 shard_map.125
  98.0 9.3 %all-to-all-start.2 = ((f32[8,24,128]{2,1,0:T(8,128)}), f32[8,24,128]{2,1,0:T(8,128)S(1)}, u32[]{:S(2)}, u32[]{:S(2)}) async-start(f32[8,24,128]{2,1,0:T(8,128)} %get-tuple-element.49), calls=%async_computation.2 | async-start | bytes 196608 | tf_op jit(solution)/shard_map/all_to_all | solution.py:495
  107.2 0.0 copy-done
  107.2 0.0 copy-done.1
  107.2 0.0 copy-done.2
  107.3 1.0 shard_map.124
  108.2 4.0 %all-to-all-done.2.parts = f32[8,24,128]{2,1,0:T(8,128)S(1)} async-done(((f32[8,24,128]{2,1,0:T(8,128)}), f32[8,24,128]{2,1,0:T(8,128)S(1)}, u32[]{:S(2)}, u32[]{:S(2)}) %all-to-all-start.2) | async-done | bytes 98336 | tf_op jit(solution)/shard_map/all_to_all | solution.py:495
  112.2 0.7 shard_map.126
Async XLA Ops:
  1.7 32.2 %collective-permute-start = (bf16[112,512]{1,0:T(8,128)(2,1)S(1)}, bf16[112,512]{1,0:T(8,128)(2,1)S(1)}, u32[]{:S(2)}, u32[]{:S(2)}) collective-permute-start(bf16[112,512]{1,0:T(8,128)(2,1)S(1)} %get-tuple-element.31), channel_id=1, source_target_pairs={{0,744},{1,745},{2,746},{3,747},{4,748},{5,749},{6,750},{7,751},{8... | collective-permute-start | bytes 344072 | tf_op jit(solution)/shard_map/ppermute | solution.py:404
  14.1 19.7 %collective-permute-start.1 = (bf16[9,4,512]{2,1,0:T(4,128)(2,1)S(1)}, bf16[9,4,512]{2,1,0:T(4,128)(2,1)S(1)}, u32[]{:S(2)}, u32[]{:S(2)}) collective-permute-start(bf16[9,4,512]{2,1,0:T(4,128)(2,1)S(1)} %get-tuple-element.32), channel_id=1, source_target_pairs={{0,23},{1,0},{2,1},{3,2},{4,3},{5,4},{6,5},{7,6},{8,7},{9,8},{10,9... | collective-permute-start | bytes 110600 | tf_op jit(solution)/shard_map/ppermute | solution.py:404
  19.7 14.1 %collective-permute-start.2 = (bf16[9,4,512]{2,1,0:T(4,128)(2,1)S(1)}, bf16[9,4,512]{2,1,0:T(4,128)(2,1)S(1)}, u32[]{:S(2)}, u32[]{:S(2)}) collective-permute-start(bf16[9,4,512]{2,1,0:T(4,128)(2,1)S(1)} %get-tuple-element.33), channel_id=1, source_target_pairs={{0,767},{1,744},{2,745},{3,746},{4,747},{5,748},{6,749},{7,750},{8... | collective-permute-start | bytes 110600 | tf_op jit(solution)/shard_map/ppermute | solution.py:404
  40.0 5.1 %collective-permute-start.3 = (bf16[144,2560]{1,0:T(8,128)(2,1)S(1)}, bf16[144,2560]{1,0:T(8,128)(2,1)S(1)}, u32[]{:S(2)}, u32[]{:S(2)}) collective-permute-start(bf16[144,2560]{1,0:T(8,128)(2,1)S(1)} %get-tuple-element.35.mine), channel_id=1, source_target_pairs={{0,24},{24,0},{1,25},{25,1},{2,26},{26,2},{3,27},{27,3},{4,28},{28... | collective-permute-start | bytes 2211848 | tf_op jit(solution)/shard_map/ppermute | solution.py:472
  46.6 32.7 %all-to-all-start = ((bf16[32,136,128]{2,1,0:T(8,128)(2,1)}), bf16[32,136,128]{2,1,0:T(8,128)(2,1)S(1)}, u32[]{:S(2)}, u32[]{:S(2)}) async-start(bf16[32,136,128]{2,1,0:T(8,128)(2,1)} %shard_map.122), calls=%async_computation | async-start | bytes 2228224 | tf_op jit(solution)/shard_map/all_to_all | solution.py:483
  52.1 55.2 %copy-start = (bf16[8,16,512]{2,1,0:T(8,128)(2,1)S(1)}, bf16[8,16,512]{2,1,0:T(8,128)(2,1)}, u32[]{:S(2)}) copy-start(bf16[8,16,512]{2,1,0:T(8,128)(2,1)} %tok.3) | copy-start | bytes 393220
  52.1 55.2 %copy-start.1 = (bf16[8,16,512]{2,1,0:T(8,128)(2,1)S(1)}, bf16[8,16,512]{2,1,0:T(8,128)(2,1)}, u32[]{:S(2)}) copy-start(bf16[8,16,512]{2,1,0:T(8,128)(2,1)} %cot.3) | copy-start | bytes 393220
  52.1 55.1 %copy-start.2 = (f32[512]{0:T(512)S(1)}, f32[512]{0:T(512)}, u32[]{:S(2)}) copy-start(f32[512]{0:T(512)} %param.11) | copy-start | bytes 6148
  52.1 27.3 %collective-permute-start.4 = (bf16[4,12,512]{2,1,0:T(8,128)(2,1)S(1)}, bf16[4,12,512]{2,1,0:T(8,128)(2,1)S(1)}, u32[]{:S(2)}, u32[]{:S(2)}) collective-permute-start(bf16[4,12,512]{2,1,0:T(8,128)(2,1)S(1)} %get-tuple-element.41), channel_id=1, source_target_pairs={{0,24},{1,25},{2,26},{3,27},{4,28},{5,29},{6,30},{7,31},{8,32},{9,... | collective-permute-start | bytes 147464 | tf_op jit(solution)/shard_map/ppermute | solution.py:404
  60.2 19.2 %collective-permute-start.5 = (bf16[4,4,512]{2,1,0:T(4,128)(2,1)S(1)}, bf16[4,4,512]{2,1,0:T(4,128)(2,1)S(1)}, u32[]{:S(2)}, u32[]{:S(2)}) collective-permute-start(bf16[4,4,512]{2,1,0:T(4,128)(2,1)S(1)} %get-tuple-element.42), channel_id=1, source_target_pairs={{0,1},{1,2},{2,3},{3,4},{4,5},{5,6},{6,7},{7,8},{8,9},{9,10},{10,1... | collective-permute-start | bytes 49160 | tf_op jit(solution)/shard_map/ppermute | solution.py:404
  62.2 17.3 %collective-permute-start.6 = (bf16[4,4,512]{2,1,0:T(4,128)(2,1)S(1)}, bf16[4,4,512]{2,1,0:T(4,128)(2,1)S(1)}, u32[]{:S(2)}, u32[]{:S(2)}) collective-permute-start(bf16[4,4,512]{2,1,0:T(4,128)(2,1)S(1)} %get-tuple-element.43), channel_id=1, source_target_pairs={{0,25},{1,26},{2,27},{3,28},{4,29},{5,30},{6,31},{7,32},{8,33},{9,... | collective-permute-start | bytes 49160 | tf_op jit(solution)/shard_map/ppermute | solution.py:404
  98.0 14.3 %all-to-all-start.2 = ((f32[8,24,128]{2,1,0:T(8,128)}), f32[8,24,128]{2,1,0:T(8,128)S(1)}, u32[]{:S(2)}, u32[]{:S(2)}) async-start(f32[8,24,128]{2,1,0:T(8,128)} %get-tuple-element.49), calls=%async_computation.2 | async-start | bytes 196608 | tf_op jit(solution)/shard_map/all_to_all | solution.py:495

commit v7 on v6

--- a/solution.py
+++ b/solution.py
@@ -112,7 +112,7 @@
 
 
 def window_kernel(
-    tok_far, cot_far, reg_far, wqkv_far, wout_far, gain_far, bias, bucket2, up, left, diag,
+    tok_far, cot_far, reg_far, wqkv_far, wout_far, gain_far, bias, bucket2, up, diag, left,
     send, keep, own_grad, down_grad, right_grad, diag_grad,
     frame_t, frame_c, labels, packed, attended, grad_att, pairs, grad_in,
     tok, cot, reg, wqkv, wout, gain, sem,
@@ -447,7 +447,7 @@
             shape((4, 4, D), BF16),
             shape((4, 4, D), BF16),
         ],
-        (tokens, cotangent, region, qkv_weight, out_weight, gain, bias, bucket2, up, left, diag),
+        (tokens, cotangent, region, qkv_weight, out_weight, gain, bias, bucket2, up, diag, left),
         [
             pltpu.VMEM((TOKENS, D), F32),
             pltpu.VMEM((TOKENS, D), F32),

time: 114 us -> 113 us (level)
  starting transfers between devices: 60.8 us -> 57.9 us
  blocking collectives: 17.8 us -> 19.3 us
    all_to_all x1, blocking collectives: 17.8 us -> 19.3 us  [local(): lines = lax.all_to_all(chunks, ('zh', 'zl'), 0, 0)]
    ppermute x1, starting transfers between devices: 3.23 us -> 1.92 us  [local(): other = lax.ppermute(send, 'core', [(0, 1), (1, 0)])]
  transfers between devices with their start and end apart: 9 -> 9, of which waited for: 3 -> 4; matrix products, arithmetic and copies ran while one was open for 0% -> 0% of each run, Pallas kernels for 2% -> 2%
where the time goes in v7:
time: 113 us; the launch traced here: 112 us
  starting transfers between devices  57.9 us (51%)
  waiting for transfers between devices  22 us (19%)
  blocking collectives  19.3 us (17%)
  Pallas kernels  12.4 us (11%)
    ppermute x6, starting transfers between devices, neighbour(): return lax.ppermute(value, ROWS + COLS, pairs)  42.2 us
    all_to_all x1, blocking collectives, local(): lines = lax.all_to_all(chunks, ('zh', 'zl'), 0, 0)  19.3 us
    all_to_all x1, waiting for transfers between devices, local(): planes = lax.all_to_all(products, ('x', 'y'), 0, 0)  15.1 us
    pallas_call x8, Pallas kernels, call(): pl.pallas_call(kernel, in_specs=[pl.BlockSpec(memory_space=pltpu.HBM if k...  12.4 us
    all_to_all x1, starting transfers between devices, local(): finals = lax.all_to_all(finals, ('core', 'x'), 0, 0)  9.28 us
    all_to_all x1, starting transfers between devices, local(): planes = lax.all_to_all(products, ('x', 'y'), 0, 0)  4.57 us
    all_to_all x1, waiting for transfers between devices, local(): finals = lax.all_to_all(finals, ('core', 'x'), 0, 0)  4.02 us
  transfers between devices with their start and end apart: 9, of which 4 were waited for; matrix products, arithmetic and copies ran while one was open for 0% of the time, Pallas kernels for 2%

profile of v7, /device:TPU:1, one launch (start us, length us, event | category | flops | bytes accessed | tf_op | source)
XLA Modules:
  0.0 112.4 jit_solution(16725747515216943866)
XLA Ops:
  0.6 1.0 shard_map.120
  1.7 12.4 %collective-permute-start = (bf16[112,512]{1,0:T(8,128)(2,1)S(1)}, bf16[112,512]{1,0:T(8,128)(2,1)S(1)}, u32[]{:S(2)}, u32[]{:S(2)}) collective-permute-start(bf16[112,512]{1,0:T(8,128)(2,1)S(1)} %get-tuple-element.31), channel_id=1, source_target_pairs={{0,744},{1,745},{2,746},{3,747},{4,748},{5,749},{6,750},{7,751},{8... | collective-permute-start | bytes 344072 | tf_op jit(solution)/shard_map/ppermute | solution.py:404
  14.1 15.4 %collective-permute-start.1 = (bf16[9,4,512]{2,1,0:T(4,128)(2,1)S(1)}, bf16[9,4,512]{2,1,0:T(4,128)(2,1)S(1)}, u32[]{:S(2)}, u32[]{:S(2)}) collective-permute-start(bf16[9,4,512]{2,1,0:T(4,128)(2,1)S(1)} %get-tuple-element.32), channel_id=1, source_target_pairs={{0,767},{1,744},{2,745},{3,746},{4,747},{5,748},{6,749},{7,750},{8... | collective-permute-start | bytes 110600 | tf_op jit(solution)/shard_map/ppermute | solution.py:404
  29.5 2.8 %collective-permute-start.2 = (bf16[9,4,512]{2,1,0:T(4,128)(2,1)S(1)}, bf16[9,4,512]{2,1,0:T(4,128)(2,1)S(1)}, u32[]{:S(2)}, u32[]{:S(2)}) collective-permute-start(bf16[9,4,512]{2,1,0:T(4,128)(2,1)S(1)} %get-tuple-element.33), channel_id=1, source_target_pairs={{0,23},{1,0},{2,1},{3,2},{4,3},{5,4},{6,5},{7,6},{8,7},{9,8},{10,9... | collective-permute-start | bytes 110600 | tf_op jit(solution)/shard_map/ppermute | solution.py:404
  32.3 1.2 %shard_map.119 = (f32[16,64,128]{2,1,0:T(8,128)S(1)}, s32[32,128]{1,0:T(8,128)S(1)}) custom-call(f32[16,225]{1,0:T(8,128)} %bitcast.6, s32[64,64]{1,0:T(8,128)} %bucket_far.1), custom_call_target="tpu_custom_call" | custom-call | bytes 8388608 | tf_op jit(solution)/shard_map/pallas_call | solution.py:385
  33.5 0.0 collective-permute-done.1.diag
  33.5 0.7 collective-permute-done.2.left
  34.2 0.0 collective-permute-done.up
  34.2 6.2 %shard_map.121 = (bf16[144,2560]{1,0:T(8,128)(2,1)S(1)}, bf16[128,512]{1,0:T(8,128)(2,1)S(1)}, f32[4,12,512]{2,1,0:T(8,128)S(1)}, bf16[4,12,512]{2,1,0:T(8,128)(...) custom-call(bf16[8,16,512]{2,1,0:T(8,128)(2,1)} %tok.3, bf16[8,16,512]{2,1,0:T(8,128)(2,1)} %cot.3, ...), custom_call_target="tpu_custom_call" | custom-call | flops 1073741824 | bytes 8388608 | tf_op jit(solution)/shard_map/pallas_call | solution.py:385
  40.4 1.9 %collective-permute-start.3 = (bf16[144,2560]{1,0:T(8,128)(2,1)S(1)}, bf16[144,2560]{1,0:T(8,128)(2,1)S(1)}, u32[]{:S(2)}, u32[]{:S(2)}) collective-permute-start(bf16[144,2560]{1,0:T(8,128)(2,1)S(1)} %get-tuple-element.35.mine), channel_id=1, source_target_pairs={{0,24},{24,0},{1,25},{25,1},{2,26},{26,2},{3,27},{27,3},{4,28},{28... | collective-permute-start | bytes 2211848 | tf_op jit(solution)/shard_map/ppermute | solution.py:472
  42.3 2.2 %collective-permute-done.3.other = bf16[144,2560]{1,0:T(8,128)(2,1)S(1)} collective-permute-done((bf16[144,2560]{1,0:T(8,128)(2,1)S(1)}, bf16[144,2560]{1,0:T(8,128)(2,1)S(1)}, u32[]{:S(2)}, u32[]{:S(2)}) %collective-permute-start.3) | collective-permute-done | bytes 737312 | tf_op jit(solution)/shard_map/ppermute | solution.py:472
  44.5 1.5 %shard_map.122 = bf16[32,136,128]{2,1,0:T(8,128)(2,1)} custom-call(bf16[144,2560]{1,0:T(8,128)(2,1)S(1)} %get-tuple-element.35.mine, bf16[144,2560]{1,0:T(8,128)(2,1)S(1)} %collective-permute-done.3.other, bf16[128,512]{1,0:T(8,128)(2,1)S(1)} %get-tuple-element.36.keep), custom_call_target="tpu_custom_call" | custom-call | flops 536870912 | bytes 2097152 | tf_op jit(solution)/shard_map/pallas_call | solution.py:385
  46.0 4.6 %all-to-all-start = ((bf16[32,136,128]{2,1,0:T(8,128)(2,1)}), bf16[32,136,128]{2,1,0:T(8,128)(2,1)S(1)}, u32[]{:S(2)}, u32[]{:S(2)}) async-start(bf16[32,136,128]{2,1,0:T(8,128)(2,1)} %shard_map.122), calls=%async_computation | async-start | bytes 2228224 | tf_op jit(solution)/shard_map/all_to_all | solution.py:483
  50.5 0.0 copy-start
  50.6 0.0 copy-start.1
  50.6 0.0 copy-start.2
  50.6 5.7 %collective-permute-start.4 = (bf16[4,12,512]{2,1,0:T(8,128)(2,1)S(1)}, bf16[4,12,512]{2,1,0:T(8,128)(2,1)S(1)}, u32[]{:S(2)}, u32[]{:S(2)}) collective-permute-start(bf16[4,12,512]{2,1,0:T(8,128)(2,1)S(1)} %get-tuple-element.41), channel_id=1, source_target_pairs={{0,24},{1,25},{2,26},{3,27},{4,28},{5,29},{6,30},{7,31},{8,32},{9,... | collective-permute-start | bytes 147464 | tf_op jit(solution)/shard_map/ppermute | solution.py:404
  56.3 1.9 %collective-permute-start.5 = (bf16[4,4,512]{2,1,0:T(4,128)(2,1)S(1)}, bf16[4,4,512]{2,1,0:T(4,128)(2,1)S(1)}, u32[]{:S(2)}, u32[]{:S(2)}) collective-permute-start(bf16[4,4,512]{2,1,0:T(4,128)(2,1)S(1)} %get-tuple-element.42), channel_id=1, source_target_pairs={{0,1},{1,2},{2,3},{3,4},{4,5},{5,6},{6,7},{7,8},{8,9},{9,10},{10,1... | collective-permute-start | bytes 49160 | tf_op jit(solution)/shard_map/ppermute | solution.py:404
  58.2 4.0 %collective-permute-start.6 = (bf16[4,4,512]{2,1,0:T(4,128)(2,1)S(1)}, bf16[4,4,512]{2,1,0:T(4,128)(2,1)S(1)}, u32[]{:S(2)}, u32[]{:S(2)}) collective-permute-start(bf16[4,4,512]{2,1,0:T(4,128)(2,1)S(1)} %get-tuple-element.43), channel_id=1, source_target_pairs={{0,25},{1,26},{2,27},{3,28},{4,29},{5,30},{6,31},{7,32},{8,33},{9,... | collective-permute-start | bytes 49160 | tf_op jit(solution)/shard_map/ppermute | solution.py:404
  62.2 15.1 %all-to-all-done.parts = bf16[32,136,128]{2,1,0:T(8,128)(2,1)S(1)} async-done(((bf16[32,136,128]{2,1,0:T(8,128)(2,1)}), bf16[32,136,128]{2,1,0:T(8,128)(2,1)S(1)}, u32[]{:S(2)}, u32[]{:S(2)}) %all-to-all-start) | async-done | bytes 1114144 | tf_op jit(solution)/shard_map/all_to_all | solution.py:483
  77.3 0.2 shard_map.123
  77.5 0.0 collective-permute-done.5.left
  77.5 0.0 collective-permute-done.6.diag
  77.5 0.0 collective-permute-done.4.above
  77.5 19.3 %all_to_all.15.parts = bf16[12,32,128]{2,1,0:T(8,128)(2,1)S(1)} all-to-all(bf16[12,32,128]{2,1,0:T(8,128)(2,1)S(1)} %shard_map.123), channel_id=1, replica_groups=mesh['y'=8,'zh'=2,'core'=2,'x'=4,'zl'=6] {'zh','zl'}, dimensions={0} | all-to-all | bytes 196608 | tf_op jit(solution)/shard_map/all_to_all | solution.py:491
  96.8 0.7 shard_map.125
  97.5 9.3 %all-to-all-start.2 = ((f32[8,24,128]{2,1,0:T(8,128)}), f32[8,24,128]{2,1,0:T(8,128)S(1)}, u32[]{:S(2)}, u32[]{:S(2)}) async-start(f32[8,24,128]{2,1,0:T(8,128)} %get-tuple-element.49), calls=%async_computation.2 | async-start | bytes 196608 | tf_op jit(solution)/shard_map/all_to_all | solution.py:495
  106.8 0.0 copy-done
  106.8 0.0 copy-done.1
  106.8 0.0 copy-done.2
  106.8 1.0 shard_map.124
  107.7 4.0 %all-to-all-done.2.parts = f32[8,24,128]{2,1,0:T(8,128)S(1)} async-done(((f32[8,24,128]{2,1,0:T(8,128)}), f32[8,24,128]{2,1,0:T(8,128)S(1)}, u32[]{:S(2)}, u32[]{:S(2)}) %all-to-all-start.2) | async-done | bytes 98336 | tf_op jit(solution)/shard_map/all_to_all | solution.py:495
  111.8 0.7 shard_map.126
Async XLA Ops:
  1.7 32.5 %collective-permute-start = (bf16[112,512]{1,0:T(8,128)(2,1)S(1)}, bf16[112,512]{1,0:T(8,128)(2,1)S(1)}, u32[]{:S(2)}, u32[]{:S(2)}) collective-permute-start(bf16[112,512]{1,0:T(8,128)(2,1)S(1)} %get-tuple-element.31), channel_id=1, source_target_pairs={{0,744},{1,745},{2,746},{3,747},{4,748},{5,749},{6,750},{7,751},{8... | collective-permute-start | bytes 344072 | tf_op jit(solution)/shard_map/ppermute | solution.py:404
  14.1 19.4 %collective-permute-start.1 = (bf16[9,4,512]{2,1,0:T(4,128)(2,1)S(1)}, bf16[9,4,512]{2,1,0:T(4,128)(2,1)S(1)}, u32[]{:S(2)}, u32[]{:S(2)}) collective-permute-start(bf16[9,4,512]{2,1,0:T(4,128)(2,1)S(1)} %get-tuple-element.32), channel_id=1, source_target_pairs={{0,767},{1,744},{2,745},{3,746},{4,747},{5,748},{6,749},{7,750},{8... | collective-permute-start | bytes 110600 | tf_op jit(solution)/shard_map/ppermute | solution.py:404
  29.5 4.7 %collective-permute-start.2 = (bf16[9,4,512]{2,1,0:T(4,128)(2,1)S(1)}, bf16[9,4,512]{2,1,0:T(4,128)(2,1)S(1)}, u32[]{:S(2)}, u32[]{:S(2)}) collective-permute-start(bf16[9,4,512]{2,1,0:T(4,128)(2,1)S(1)} %get-tuple-element.33), channel_id=1, source_target_pairs={{0,23},{1,0},{2,1},{3,2},{4,3},{5,4},{6,5},{7,6},{8,7},{9,8},{10,9... | collective-permute-start | bytes 110600 | tf_op jit(solution)/shard_map/ppermute | solution.py:404
  40.4 4.1 %collective-permute-start.3 = (bf16[144,2560]{1,0:T(8,128)(2,1)S(1)}, bf16[144,2560]{1,0:T(8,128)(2,1)S(1)}, u32[]{:S(2)}, u32[]{:S(2)}) collective-permute-start(bf16[144,2560]{1,0:T(8,128)(2,1)S(1)} %get-tuple-element.35.mine), channel_id=1, source_target_pairs={{0,24},{24,0},{1,25},{25,1},{2,26},{26,2},{3,27},{27,3},{4,28},{28... | collective-permute-start | bytes 2211848 | tf_op jit(solution)/shard_map/ppermute | solution.py:472
  46.0 31.4 %all-to-all-start = ((bf16[32,136,128]{2,1,0:T(8,128)(2,1)}), bf16[32,136,128]{2,1,0:T(8,128)(2,1)S(1)}, u32[]{:S(2)}, u32[]{:S(2)}) async-start(bf16[32,136,128]{2,1,0:T(8,128)(2,1)} %shard_map.122), calls=%async_computation | async-start | bytes 2228224 | tf_op jit(solution)/shard_map/all_to_all | solution.py:483
  50.5 56.2 %copy-start = (bf16[8,16,512]{2,1,0:T(8,128)(2,1)S(1)}, bf16[8,16,512]{2,1,0:T(8,128)(2,1)}, u32[]{:S(2)}) copy-start(bf16[8,16,512]{2,1,0:T(8,128)(2,1)} %tok.3) | copy-start | bytes 393220
  50.6 56.2 %copy-start.1 = (bf16[8,16,512]{2,1,0:T(8,128)(2,1)S(1)}, bf16[8,16,512]{2,1,0:T(8,128)(2,1)}, u32[]{:S(2)}) copy-start(bf16[8,16,512]{2,1,0:T(8,128)(2,1)} %cot.3) | copy-start | bytes 393220
  50.6 56.2 %copy-start.2 = (f32[512]{0:T(512)S(1)}, f32[512]{0:T(512)}, u32[]{:S(2)}) copy-start(f32[512]{0:T(512)} %param.11) | copy-start | bytes 6148
  50.6 26.9 %collective-permute-start.4 = (bf16[4,12,512]{2,1,0:T(8,128)(2,1)S(1)}, bf16[4,12,512]{2,1,0:T(8,128)(2,1)S(1)}, u32[]{:S(2)}, u32[]{:S(2)}) collective-permute-start(bf16[4,12,512]{2,1,0:T(8,128)(2,1)S(1)} %get-tuple-element.41), channel_id=1, source_target_pairs={{0,24},{1,25},{2,26},{3,27},{4,28},{5,29},{6,30},{7,31},{8,32},{9,... | collective-permute-start | bytes 147464 | tf_op jit(solution)/shard_map/ppermute | solution.py:404
  56.3 21.2 %collective-permute-start.5 = (bf16[4,4,512]{2,1,0:T(4,128)(2,1)S(1)}, bf16[4,4,512]{2,1,0:T(4,128)(2,1)S(1)}, u32[]{:S(2)}, u32[]{:S(2)}) collective-permute-start(bf16[4,4,512]{2,1,0:T(4,128)(2,1)S(1)} %get-tuple-element.42), channel_id=1, source_target_pairs={{0,1},{1,2},{2,3},{3,4},{4,5},{5,6},{6,7},{7,8},{8,9},{9,10},{10,1... | collective-permute-start | bytes 49160 | tf_op jit(solution)/shard_map/ppermute | solution.py:404
  58.2 19.3 %collective-permute-start.6 = (bf16[4,4,512]{2,1,0:T(4,128)(2,1)S(1)}, bf16[4,4,512]{2,1,0:T(4,128)(2,1)S(1)}, u32[]{:S(2)}, u32[]{:S(2)}) collective-permute-start(bf16[4,4,512]{2,1,0:T(4,128)(2,1)S(1)} %get-tuple-element.43), channel_id=1, source_target_pairs={{0,25},{1,26},{2,27},{3,28},{4,29},{5,30},{6,31},{7,32},{8,33},{9,... | collective-permute-start | bytes 49160 | tf_op jit(solution)/shard_map/ppermute | solution.py:404
  97.5 14.3 %all-to-all-start.2 = ((f32[8,24,128]{2,1,0:T(8,128)}), f32[8,24,128]{2,1,0:T(8,128)S(1)}, u32[]{:S(2)}, u32[]{:S(2)}) async-start(f32[8,24,128]{2,1,0:T(8,128)} %get-tuple-element.49), calls=%async_computation.2 | async-start | bytes 196608 | tf_op jit(solution)/shard_map/all_to_all | solution.py:495

commit v8 on v7

--- a/solution.py
+++ b/solution.py
@@ -87,14 +87,18 @@
     to_left[8, 0:4, 0:16] = classes[4:8].astype(BF16)
 
 
-def bias_kernel(table_far, bucket_far, bias, bucket2, table, bucket, sem):
+def bias_kernel(
+    table_far, bucket_far, wqkv_far, wout_far, bias, bucket2, wqkv, wout, table, bucket, sem
+):
     copies = [
         pltpu.make_async_copy(table_far, table, sem.at[0]),
         pltpu.make_async_copy(bucket_far, bucket, sem.at[1]),
+        pltpu.make_async_copy(wqkv_far, wqkv, sem.at[2]),
+        pltpu.make_async_copy(wout_far, wout, sem.at[3]),
     ]
     for copy in copies:
         copy.start()
-    for copy in copies:
+    for copy in copies[0:2]:
         copy.wait()
     turned = jnp.concatenate([table[...], jnp.zeros((HEADS, 256 - NBIAS), F32)], axis=1)
     both = jnp.concatenate([bucket[...], bucket[...]], axis=1)
@@ -109,18 +113,17 @@
             got_first = jnp.take_along_axis(first, within, axis=1, mode="promise_in_bounds")
             got_second = jnp.take_along_axis(second, within, axis=1, mode="promise_in_bounds")
             bias[h, block * 8 : block * 8 + 8, :] = jnp.where(upper, got_second, got_first)
+    for copy in copies[2:]:
+        copy.wait()
 
 
 def window_kernel(
-    tok_far, cot_far, reg_far, wqkv_far, wout_far, gain_far, bias, bucket2, up, diag, left,
+    tok_far, cot_far, reg_far, gain_far, wqkv, wout, bias, bucket2, up, diag, left,
     send, keep, own_grad, down_grad, right_grad, diag_grad,
     frame_t, frame_c, labels, packed, attended, grad_att, pairs, grad_in,
-    tok, cot, reg, wqkv, wout, gain, sem,
+    tok, cot, reg, gain, sem,
 ):
-    moves = (
-        (tok_far, tok), (cot_far, cot), (reg_far, reg), (wqkv_far, wqkv),
-        (wout_far, wout), (gain_far, gain),
-    )
+    moves = ((tok_far, tok), (cot_far, cot), (reg_far, reg), (gain_far, gain))
     copies = [pltpu.make_async_copy(src, dst, sem.at[k]) for k, (src, dst) in enumerate(moves)]
     for copy in copies:
         copy.start()
@@ -174,11 +177,9 @@
     allowed4 = jnp.concatenate([allowed.astype(F32)] * GROUP, axis=0) > 0.5
 
     hat, _ = layer_stats(frame_t[...])
-    copies[5].wait()
+    copies[3].wait()
     normed = (hat * gain[...]).astype(BF16)
     cots = frame_c[...].astype(BF16)
-    for copy in copies[3:5]:
-        copy.wait()
     packed[...] = dot(normed, wqkv[...]).astype(BF16)
     grad_att[...] = dot_nt(cots, wout[...]).astype(BF16)
     send[0:TOKENS, 3 * D : 4 * D] = cots
@@ -422,20 +423,22 @@
     up = neighbour(to_up, -1, 0)
     left = neighbour(to_left, 0, -1)
     diag = neighbour(to_diag, -1, -1)
-    bias, bucket2 = call(
+    bias, bucket2, wqkv, wout = call(
         bias_kernel,
         [
             shape((HEADS, AREA, 128), F32),
             shape((AREA // 2, 128), jnp.int32),
+            shape((D, 3 * D), BF16),
+            shape((D, D), BF16),
         ],
-        (bias_table.T, bias_bucket),
+        (bias_table.T, bias_bucket, qkv_weight, out_weight),
         [
             pltpu.VMEM((HEADS, NBIAS), F32),
             pltpu.VMEM((AREA, AREA), jnp.int32),
-            pltpu.SemaphoreType.DMA((2,)),
+            pltpu.SemaphoreType.DMA((4,)),
         ],
         moved=1 << 23,
-        remain=(0, 1),
+        remain=(0, 1, 2, 3),
     )
     send, keep, own_grad, down_grad, right_grad, diag_grad = call(
         window_kernel,
@@ -447,7 +450,7 @@
             shape((4, 4, D), BF16),
             shape((4, 4, D), BF16),
         ],
-        (tokens, cotangent, region, qkv_weight, out_weight, gain, bias, bucket2, up, diag, left),
+        (tokens, cotangent, region, gain, wqkv, wout, bias, bucket2, up, diag, left),
         [
             pltpu.VMEM((TOKENS, D), F32),
             pltpu.VMEM((TOKENS, D), F32),
@@ -460,14 +463,12 @@
             pltpu.VMEM((8, 16, D), BF16),
             pltpu.VMEM((8, 16, D), BF16),
             pltpu.VMEM((8, 16), jnp.int32),
-            pltpu.VMEM((D, 3 * D), BF16),
-            pltpu.VMEM((D, D), BF16),
             pltpu.VMEM((1, D), F32),
-            pltpu.SemaphoreType.DMA((6,)),
+            pltpu.SemaphoreType.DMA((4,)),
         ],
         flops=1 << 30,
         moved=1 << 23,
-        remain=tuple(range(6)),
+        remain=tuple(range(4)),
     )
     other = lax.ppermute(send, "core", [(0, 1), (1, 0)])
     products = call(

time: 113 us -> 113 us (level)
  no operation moved by 1% of the time
where the time goes in v8:
time: 113 us
  starting transfers between devices  58.3 us (52%)
  waiting for transfers between devices  21.8 us (19%)
  blocking collectives  19.3 us (17%)
  Pallas kernels  12.3 us (11%)
    ppermute x6, starting transfers between devices, neighbour(): return lax.ppermute(value, ROWS + COLS, pairs)  42 us
    all_to_all x1, blocking collectives, local(): lines = lax.all_to_all(chunks, ('zh', 'zl'), 0, 0)  19.3 us
    all_to_all x1, waiting for transfers between devices, local(): planes = lax.all_to_all(products, ('x', 'y'), 0, 0)  15.3 us
    pallas_call x8, Pallas kernels, call(): pl.pallas_call(kernel, in_specs=[pl.BlockSpec(memory_space=pltpu.HBM if k...  12.3 us
    all_to_all x1, starting transfers between devices, local(): finals = lax.all_to_all(finals, ('core', 'x'), 0, 0)  9.66 us
    all_to_all x1, starting transfers between devices, local(): planes = lax.all_to_all(products, ('x', 'y'), 0, 0)  4.72 us
    all_to_all x1, waiting for transfers between devices, local(): finals = lax.all_to_all(finals, ('core', 'x'), 0, 0)  4.02 us
  transfers between devices with their start and end apart: 9, of which 4 were waited for; matrix products, arithmetic and copies ran while one was open for 0% of the time, Pallas kernels for 2%

profile of v8, /device:TPU:1, one launch (start us, length us, event | category | flops | bytes accessed | tf_op | source)
XLA Modules:
  0.0 112.6 jit_solution(2185363940250888550)
XLA Ops:
  0.6 1.0 shard_map.120
  1.7 12.4 %collective-permute-start = (bf16[112,512]{1,0:T(8,128)(2,1)S(1)}, bf16[112,512]{1,0:T(8,128)(2,1)S(1)}, u32[]{:S(2)}, u32[]{:S(2)}) collective-permute-start(bf16[112,512]{1,0:T(8,128)(2,1)S(1)} %get-tuple-element.35), channel_id=1, source_target_pairs={{0,744},{1,745},{2,746},{3,747},{4,748},{5,749},{6,750},{7,751},{8... | collective-permute-start | bytes 344072 | tf_op jit(solution)/shard_map/ppermute | solution.py:405
  14.1 15.4 %collective-permute-start.1 = (bf16[9,4,512]{2,1,0:T(4,128)(2,1)S(1)}, bf16[9,4,512]{2,1,0:T(4,128)(2,1)S(1)}, u32[]{:S(2)}, u32[]{:S(2)}) collective-permute-start(bf16[9,4,512]{2,1,0:T(4,128)(2,1)S(1)} %get-tuple-element.36), channel_id=1, source_target_pairs={{0,767},{1,744},{2,745},{3,746},{4,747},{5,748},{6,749},{7,750},{8... | collective-permute-start | bytes 110600 | tf_op jit(solution)/shard_map/ppermute | solution.py:405
  29.5 2.8 %collective-permute-start.2 = (bf16[9,4,512]{2,1,0:T(4,128)(2,1)S(1)}, bf16[9,4,512]{2,1,0:T(4,128)(2,1)S(1)}, u32[]{:S(2)}, u32[]{:S(2)}) collective-permute-start(bf16[9,4,512]{2,1,0:T(4,128)(2,1)S(1)} %get-tuple-element.37), channel_id=1, source_target_pairs={{0,23},{1,0},{2,1},{3,2},{4,3},{5,4},{6,5},{7,6},{8,7},{9,8},{10,9... | collective-permute-start | bytes 110600 | tf_op jit(solution)/shard_map/ppermute | solution.py:405
  32.3 1.6 %shard_map.119 = (f32[16,64,128]{2,1,0:T(8,128)S(1)}, s32[32,128]{1,0:T(8,128)S(1)}, bf16[512,1536]{1,0:T(8,128)(2,1)S(1)}, bf16[512,512]{1,0:T(8,128)(2,1)S(1)}) custom-call(f32[16,225]{1,0:T(8,128)} %bitcast.6, s32[64,64]{1,0:T(8,128)} %bucket_far.1, bf16[512,1536]{1,0:T(8,128)(2,1)} %wqkv_far.1, bf16[512,512]{1,0:T(8,128)(2,1)} %wout_far.1), custom_call_target="tpu_custom_call" | custom-call | bytes 8388608 | tf_op jit(solution)/shard_map/pallas_call | solution.py:386
  33.9 0.0 collective-permute-done.1.diag
  33.9 0.3 collective-permute-done.2.left
  34.2 0.0 collective-permute-done.up
  34.2 5.8 %shard_map.121 = (bf16[144,2560]{1,0:T(8,128)(2,1)S(1)}, bf16[128,512]{1,0:T(8,128)(2,1)S(1)}, f32[4,12,512]{2,1,0:T(8,128)S(1)}, bf16[4,12,512]{2,1,0:T(8,128)(...) custom-call(bf16[8,16,512]{2,1,0:T(8,128)(2,1)} %tok.3, bf16[8,16,512]{2,1,0:T(8,128)(2,1)} %cot.3, ...), custom_call_target="tpu_custom_call" | custom-call | flops 1073741824 | bytes 8388608 | tf_op jit(solution)/shard_map/pallas_call | solution.py:386
  40.0 1.9 %collective-permute-start.3 = (bf16[144,2560]{1,0:T(8,128)(2,1)S(1)}, bf16[144,2560]{1,0:T(8,128)(2,1)S(1)}, u32[]{:S(2)}, u32[]{:S(2)}) collective-permute-start(bf16[144,2560]{1,0:T(8,128)(2,1)S(1)} %get-tuple-element.39.mine), channel_id=1, source_target_pairs={{0,24},{24,0},{1,25},{25,1},{2,26},{26,2},{3,27},{27,3},{4,28},{28... | collective-permute-start | bytes 2211848 | tf_op jit(solution)/shard_map/ppermute | solution.py:473
  41.9 2.2 %collective-permute-done.3.other = bf16[144,2560]{1,0:T(8,128)(2,1)S(1)} collective-permute-done((bf16[144,2560]{1,0:T(8,128)(2,1)S(1)}, bf16[144,2560]{1,0:T(8,128)(2,1)S(1)}, u32[]{:S(2)}, u32[]{:S(2)}) %collective-permute-start.3) | collective-permute-done | bytes 737312 | tf_op jit(solution)/shard_map/ppermute | solution.py:473
  44.1 1.5 %shard_map.122 = bf16[32,136,128]{2,1,0:T(8,128)(2,1)} custom-call(bf16[144,2560]{1,0:T(8,128)(2,1)S(1)} %get-tuple-element.39.mine, bf16[144,2560]{1,0:T(8,128)(2,1)S(1)} %collective-permute-done.3.other, bf16[128,512]{1,0:T(8,128)(2,1)S(1)} %get-tuple-element.40.keep), custom_call_target="tpu_custom_call" | custom-call | flops 536870912 | bytes 2097152 | tf_op jit(solution)/shard_map/pallas_call | solution.py:386
  45.5 0.0 copy-start
  45.5 0.0 copy-start.1
  45.5 0.0 copy-start.2
  45.5 4.7 %all-to-all-start = ((bf16[32,136,128]{2,1,0:T(8,128)(2,1)}), bf16[32,136,128]{2,1,0:T(8,128)(2,1)S(1)}, u32[]{:S(2)}, u32[]{:S(2)}) async-start(bf16[32,136,128]{2,1,0:T(8,128)(2,1)} %shard_map.122), calls=%async_computation | async-start | bytes 2228224 | tf_op jit(solution)/shard_map/all_to_all | solution.py:484
  50.3 5.5 %collective-permute-start.4 = (bf16[4,12,512]{2,1,0:T(8,128)(2,1)S(1)}, bf16[4,12,512]{2,1,0:T(8,128)(2,1)S(1)}, u32[]{:S(2)}, u32[]{:S(2)}) collective-permute-start(bf16[4,12,512]{2,1,0:T(8,128)(2,1)S(1)} %get-tuple-element.45), channel_id=1, source_target_pairs={{0,24},{1,25},{2,26},{3,27},{4,28},{5,29},{6,30},{7,31},{8,32},{9,... | collective-permute-start | bytes 147464 | tf_op jit(solution)/shard_map/ppermute | solution.py:405
  55.8 1.9 %collective-permute-start.5 = (bf16[4,4,512]{2,1,0:T(4,128)(2,1)S(1)}, bf16[4,4,512]{2,1,0:T(4,128)(2,1)S(1)}, u32[]{:S(2)}, u32[]{:S(2)}) collective-permute-start(bf16[4,4,512]{2,1,0:T(4,128)(2,1)S(1)} %get-tuple-element.46), channel_id=1, source_target_pairs={{0,1},{1,2},{2,3},{3,4},{4,5},{5,6},{6,7},{7,8},{8,9},{9,10},{10,1... | collective-permute-start | bytes 49160 | tf_op jit(solution)/shard_map/ppermute | solution.py:405
  57.7 4.0 %collective-permute-start.6 = (bf16[4,4,512]{2,1,0:T(4,128)(2,1)S(1)}, bf16[4,4,512]{2,1,0:T(4,128)(2,1)S(1)}, u32[]{:S(2)}, u32[]{:S(2)}) collective-permute-start(bf16[4,4,512]{2,1,0:T(4,128)(2,1)S(1)} %get-tuple-element.47), channel_id=1, source_target_pairs={{0,25},{1,26},{2,27},{3,28},{4,29},{5,30},{6,31},{7,32},{8,33},{9,... | collective-permute-start | bytes 49160 | tf_op jit(solution)/shard_map/ppermute | solution.py:405
  61.7 15.3 %all-to-all-done.parts = bf16[32,136,128]{2,1,0:T(8,128)(2,1)S(1)} async-done(((bf16[32,136,128]{2,1,0:T(8,128)(2,1)}), bf16[32,136,128]{2,1,0:T(8,128)(2,1)S(1)}, u32[]{:S(2)}, u32[]{:S(2)}) %all-to-all-start) | async-done | bytes 1114144 | tf_op jit(solution)/shard_map/all_to_all | solution.py:484
  77.0 0.2 shard_map.123
  77.2 0.0 collective-permute-done.5.left
  77.2 0.0 collective-permute-done.6.diag
  77.2 0.0 collective-permute-done.4.above
  77.2 19.3 %all_to_all.15.parts = bf16[12,32,128]{2,1,0:T(8,128)(2,1)S(1)} all-to-all(bf16[12,32,128]{2,1,0:T(8,128)(2,1)S(1)} %shard_map.123), channel_id=1, replica_groups=mesh['y'=8,'zh'=2,'core'=2,'x'=4,'zl'=6] {'zh','zl'}, dimensions={0} | all-to-all | bytes 196608 | tf_op jit(solution)/shard_map/all_to_all | solution.py:492
  96.6 0.7 shard_map.125
  97.2 9.7 %all-to-all-start.2 = ((f32[8,24,128]{2,1,0:T(8,128)}), f32[8,24,128]{2,1,0:T(8,128)S(1)}, u32[]{:S(2)}, u32[]{:S(2)}) async-start(f32[8,24,128]{2,1,0:T(8,128)} %get-tuple-element.53), calls=%async_computation.2 | async-start | bytes 196608 | tf_op jit(solution)/shard_map/all_to_all | solution.py:496
  106.9 0.0 copy-done
  106.9 0.0 copy-done.1
  106.9 0.0 copy-done.2
  106.9 1.0 shard_map.124
  107.9 4.0 %all-to-all-done.2.parts = f32[8,24,128]{2,1,0:T(8,128)S(1)} async-done(((f32[8,24,128]{2,1,0:T(8,128)}), f32[8,24,128]{2,1,0:T(8,128)S(1)}, u32[]{:S(2)}, u32[]{:S(2)}) %all-to-all-start.2) | async-done | bytes 98336 | tf_op jit(solution)/shard_map/all_to_all | solution.py:496
  111.9 0.7 shard_map.126
Async XLA Ops:
  1.7 32.5 %collective-permute-start = (bf16[112,512]{1,0:T(8,128)(2,1)S(1)}, bf16[112,512]{1,0:T(8,128)(2,1)S(1)}, u32[]{:S(2)}, u32[]{:S(2)}) collective-permute-start(bf16[112,512]{1,0:T(8,128)(2,1)S(1)} %get-tuple-element.35), channel_id=1, source_target_pairs={{0,744},{1,745},{2,746},{3,747},{4,748},{5,749},{6,750},{7,751},{8... | collective-permute-start | bytes 344072 | tf_op jit(solution)/shard_map/ppermute | solution.py:405
  14.1 19.8 %collective-permute-start.1 = (bf16[9,4,512]{2,1,0:T(4,128)(2,1)S(1)}, bf16[9,4,512]{2,1,0:T(4,128)(2,1)S(1)}, u32[]{:S(2)}, u32[]{:S(2)}) collective-permute-start(bf16[9,4,512]{2,1,0:T(4,128)(2,1)S(1)} %get-tuple-element.36), channel_id=1, source_target_pairs={{0,767},{1,744},{2,745},{3,746},{4,747},{5,748},{6,749},{7,750},{8... | collective-permute-start | bytes 110600 | tf_op jit(solution)/shard_map/ppermute | solution.py:405
  29.5 4.7 %collective-permute-start.2 = (bf16[9,4,512]{2,1,0:T(4,128)(2,1)S(1)}, bf16[9,4,512]{2,1,0:T(4,128)(2,1)S(1)}, u32[]{:S(2)}, u32[]{:S(2)}) collective-permute-start(bf16[9,4,512]{2,1,0:T(4,128)(2,1)S(1)} %get-tuple-element.37), channel_id=1, source_target_pairs={{0,23},{1,0},{2,1},{3,2},{4,3},{5,4},{6,5},{7,6},{8,7},{9,8},{10,9... | collective-permute-start | bytes 110600 | tf_op jit(solution)/shard_map/ppermute | solution.py:405
  40.0 4.1 %collective-permute-start.3 = (bf16[144,2560]{1,0:T(8,128)(2,1)S(1)}, bf16[144,2560]{1,0:T(8,128)(2,1)S(1)}, u32[]{:S(2)}, u32[]{:S(2)}) collective-permute-start(bf16[144,2560]{1,0:T(8,128)(2,1)S(1)} %get-tuple-element.39.mine), channel_id=1, source_target_pairs={{0,24},{24,0},{1,25},{25,1},{2,26},{26,2},{3,27},{27,3},{4,28},{28... | collective-permute-start | bytes 2211848 | tf_op jit(solution)/shard_map/ppermute | solution.py:473
  45.5 61.4 %copy-start = (bf16[8,16,512]{2,1,0:T(8,128)(2,1)S(1)}, bf16[8,16,512]{2,1,0:T(8,128)(2,1)}, u32[]{:S(2)}) copy-start(bf16[8,16,512]{2,1,0:T(8,128)(2,1)} %tok.3) | copy-start | bytes 393220
  45.5 61.4 %copy-start.1 = (bf16[8,16,512]{2,1,0:T(8,128)(2,1)S(1)}, bf16[8,16,512]{2,1,0:T(8,128)(2,1)}, u32[]{:S(2)}) copy-start(bf16[8,16,512]{2,1,0:T(8,128)(2,1)} %cot.3) | copy-start | bytes 393220
  45.5 61.4 %copy-start.2 = (f32[512]{0:T(512)S(1)}, f32[512]{0:T(512)}, u32[]{:S(2)}) copy-start(f32[512]{0:T(512)} %param.11) | copy-start | bytes 6148
  45.5 31.5 %all-to-all-start = ((bf16[32,136,128]{2,1,0:T(8,128)(2,1)}), bf16[32,136,128]{2,1,0:T(8,128)(2,1)S(1)}, u32[]{:S(2)}, u32[]{:S(2)}) async-start(bf16[32,136,128]{2,1,0:T(8,128)(2,1)} %shard_map.122), calls=%async_computation | async-start | bytes 2228224 | tf_op jit(solution)/shard_map/all_to_all | solution.py:484
  50.3 27.0 %collective-permute-start.4 = (bf16[4,12,512]{2,1,0:T(8,128)(2,1)S(1)}, bf16[4,12,512]{2,1,0:T(8,128)(2,1)S(1)}, u32[]{:S(2)}, u32[]{:S(2)}) collective-permute-start(bf16[4,12,512]{2,1,0:T(8,128)(2,1)S(1)} %get-tuple-element.45), channel_id=1, source_target_pairs={{0,24},{1,25},{2,26},{3,27},{4,28},{5,29},{6,30},{7,31},{8,32},{9,... | collective-permute-start | bytes 147464 | tf_op jit(solution)/shard_map/ppermute | solution.py:405
  55.8 21.4 %collective-permute-start.5 = (bf16[4,4,512]{2,1,0:T(4,128)(2,1)S(1)}, bf16[4,4,512]{2,1,0:T(4,128)(2,1)S(1)}, u32[]{:S(2)}, u32[]{:S(2)}) collective-permute-start(bf16[4,4,512]{2,1,0:T(4,128)(2,1)S(1)} %get-tuple-element.46), channel_id=1, source_target_pairs={{0,1},{1,2},{2,3},{3,4},{4,5},{5,6},{6,7},{7,8},{8,9},{9,10},{10,1... | collective-permute-start | bytes 49160 | tf_op jit(solution)/shard_map/ppermute | solution.py:405
  57.7 19.5 %collective-permute-start.6 = (bf16[4,4,512]{2,1,0:T(4,128)(2,1)S(1)}, bf16[4,4,512]{2,1,0:T(4,128)(2,1)S(1)}, u32[]{:S(2)}, u32[]{:S(2)}) collective-permute-start(bf16[4,4,512]{2,1,0:T(4,128)(2,1)S(1)} %get-tuple-element.47), channel_id=1, source_target_pairs={{0,25},{1,26},{2,27},{3,28},{4,29},{5,30},{6,31},{7,32},{8,33},{9,... | collective-permute-start | bytes 49160 | tf_op jit(solution)/shard_map/ppermute | solution.py:405
  97.2 14.7 %all-to-all-start.2 = ((f32[8,24,128]{2,1,0:T(8,128)}), f32[8,24,128]{2,1,0:T(8,128)S(1)}, u32[]{:S(2)}, u32[]{:S(2)}) async-start(f32[8,24,128]{2,1,0:T(8,128)} %get-tuple-element.53), calls=%async_computation.2 | async-start | bytes 196608 | tf_op jit(solution)/shard_map/all_to_all | solution.py:496
